TPU v7x, 256 devices: a whole 4x4x8 slice. The times are simulated.
256 devices in a mesh: blk: 128 (over x_lo, z, y, core), stretch: 2 (over x_hi).
Axes of the slice: x: 4 (x_hi: 2, x_lo: 2; x = x_hi * 2 + x_lo), y: 4, z: 8, core: 2. Of those that a mesh axis runs over, the one named last changes fastest.
Arguments:
- activations: bfloat16 [32768, 2048], P('blk', 'stretch'), may hold values from -6 to 6
- document_ids: int32 [32768], replicated, may hold values from 0 to 511, never falling along the last dimension, each value on 1 to 128 neighbouring positions
- joint_input_weights: bfloat16 [128, 2048, 1536], P('blk', 'stretch'), may hold values from -0.125 to 0.125
- output_weights: bfloat16 [128, 1024, 2048], P('blk', None, 'stretch'), may hold values from -0.1875 to 0.1875
- norm_gains: bfloat16 [128, 2048], P('blk', 'stretch'), may hold values from 0.5 to 1.5
Outputs:
- input_weight_grad: bfloat16 [128, 2048, 1536], P('blk', 'stretch')
- output_weight_grad: bfloat16 [128, 1024, 2048], P('blk', None, 'stretch')
Inputs may be any that keep to these rules, and one draw needn't show every extreme that they name: `document_ids`: document numbers never fall along the tokens; a document spans at most half of 256 positions.
All inputs are finite; a program needn't handle non-finite values.
Results may differ from a plain program's by a relative error of at most 0.015.
Values may be sent and summed in bfloat16 or wider, within the bound.
No kernel may reach another device: no remote copies, remote signals or barrier semaphores. Data moves between devices by JAX's collectives and lax.ppermute only.
A program may use at most 128 MiB of HBM per device.

v0:
```python
from functools import partial

import jax
import jax.numpy as jnp
from jax import lax
from jax.sharding import PartitionSpec as P

MODEL_WIDTH = 2048
HEAD_WIDTH = 64
QUERY_HEADS = 16
KEY_VALUE_HEADS = 4


EPS = 1e-05
THETA = 10000.0
PRECISE = lax.Precision.HIGHEST


def from_behind(value, axis, steps):
    count = lax.axis_size(axis)
    pairs = [(source, (source + steps) % count) for source in range(count)]
    return lax.ppermute(value, axis, pairs)


def rotate(matrix, cosine, sine_part):
    half_size = matrix.shape[-1] // 2
    first_half = matrix[..., :half_size]
    second = matrix[..., half_size:]
    return jnp.concatenate(
        [first_half * cosine - second * sine_part, first_half * sine_part + second * cosine],
        axis=-1,
    )


def attend(projected_input, doc_ids):
    count_of_rows = projected_input.shape[0]
    half_size = HEAD_WIDTH // 2
    queries_per_group = QUERY_HEADS // KEY_VALUE_HEADS
    position = jnp.arange(count_of_rows, dtype=jnp.float32)[:, None]
    frequency = THETA ** (-2.0 * jnp.arange(half_size, dtype=jnp.float32) / HEAD_WIDTH)
    angles = position * frequency[None, :]
    cosine = jnp.cos(angles)
    sine_part = jnp.sin(angles)
    query_rows = projected_input[:, : QUERY_HEADS * HEAD_WIDTH].reshape(
        count_of_rows, KEY_VALUE_HEADS, queries_per_group, HEAD_WIDTH
    )
    query_rows = rotate(query_rows, cosine[:, None, None, :], sine_part[:, None, None, :])
    key_rows_rotated = projected_input[
        :, QUERY_HEADS * HEAD_WIDTH : (QUERY_HEADS + KEY_VALUE_HEADS) * HEAD_WIDTH
    ].reshape(count_of_rows, KEY_VALUE_HEADS, HEAD_WIDTH)
    key_rows_rotated = rotate(key_rows_rotated, cosine[:, None, :], sine_part[:, None, :])
    value_rows = projected_input[:, (QUERY_HEADS + KEY_VALUE_HEADS) * HEAD_WIDTH :].reshape(
        count_of_rows, KEY_VALUE_HEADS, HEAD_WIDTH
    )
    row_index = jnp.arange(count_of_rows)[:, None]
    col_index = jnp.arange(count_of_rows)[None, :]
    allowed = (col_index <= row_index) & (doc_ids[:, None] == doc_ids[None, :])

    def one_group(operands):
        group_queries, group_keys, group_values = operands
        scores = jnp.einsum(
            "tgd,sd->gts", group_queries, group_keys, precision=PRECISE
        ) * HEAD_WIDTH ** (-0.5)
        scores = jnp.where(allowed[None], scores, -1e30)
        row_max = jnp.max(scores, axis=2, keepdims=True)
        weights = jnp.exp(scores - row_max)
        weights = weights / jnp.sum(weights, axis=2, keepdims=True)
        return jnp.einsum("gts,sd->tgd", weights, group_values, precision=PRECISE)

    results = lax.map(
        one_group,
        (
            jnp.moveaxis(query_rows, 1, 0),
            jnp.moveaxis(key_rows_rotated, 1, 0),
            jnp.moveaxis(value_rows, 1, 0),
        ),
    )
    return jnp.moveaxis(results, 0, 1).reshape(count_of_rows, QUERY_HEADS * HEAD_WIDTH)


def norm_scale(value_rows):
    summed = lax.psum(jnp.sum(value_rows * value_rows, axis=1, keepdims=True), "stretch")
    return lax.rsqrt(summed / MODEL_WIDTH + EPS)


def norm_total(scaled, value_rows):
    return lax.psum(jnp.sum(scaled * value_rows, axis=1, keepdims=True), "stretch")


def project(left_side, right_side):
    return lax.psum(jnp.dot(left_side, right_side, preferred_element_type=jnp.float32), "stretch")


def project_back(left_side, right_side):
    return lax.psum(
        jnp.dot(left_side, right_side.T, preferred_element_type=jnp.float32).astype(jnp.bfloat16),
        "stretch",
    ).astype(jnp.float32)


def forward_pass(inputs, layer, doc_ids):
    joint_input_weights, output_weights, norm_gains = layer
    inputs_float = inputs.astype(jnp.float32)
    scale_one = norm_scale(inputs_float)
    normed_one = (inputs_float * scale_one * norm_gains.astype(jnp.float32)).astype(jnp.bfloat16)
    projected_input = project(normed_one, joint_input_weights)
    attended = attend(projected_input, doc_ids).astype(jnp.bfloat16)
    result = (
        inputs_float + jnp.dot(attended, output_weights, preferred_element_type=jnp.float32)
    ).astype(jnp.bfloat16)
    stored = (inputs_float, scale_one, normed_one, projected_input, attended)
    return (result, stored)


def backward_pass(upstream, layer, stored, doc_ids):
    joint_input_weights, output_weights, norm_gains = layer
    inputs_float, scale_one, normed_one, projected_input, attended = stored
    upstream_bf = upstream.astype(jnp.bfloat16)
    attended_grad = project_back(upstream_bf, output_weights)
    out_grad = jnp.dot(attended.T, upstream_bf, preferred_element_type=jnp.float32)
    projected_grad = jax.vjp(partial(attend, doc_ids=doc_ids), projected_input)[1](attended_grad)[
        0
    ].astype(jnp.bfloat16)
    attn_grad = jnp.dot(normed_one.T, projected_grad, preferred_element_type=jnp.float32)
    normed_one_grad = jnp.dot(
        projected_grad, joint_input_weights.T, preferred_element_type=jnp.float32
    )
    scaled_one = norm_gains.astype(jnp.float32) * normed_one_grad
    input_sum = norm_total(scaled_one, inputs_float)
    input_grad = (
        upstream + scale_one * scaled_one - inputs_float * scale_one**3 * input_sum / MODEL_WIDTH
    )
    return (input_grad, (attn_grad, out_grad))


def shards(activations, document_ids, joint_input_weights, output_weights, norm_gains):
    count_of_rows = activations.shape[0]
    cycle_index = lax.axis_index("blk")
    own_docs = lax.dynamic_slice_in_dim(document_ids, cycle_index * count_of_rows, count_of_rows)
    own_layer = (joint_input_weights[0], output_weights[0], norm_gains[0])
    first_out, first_stored = forward_pass(activations, own_layer, own_docs)
    other_layer = from_behind((own_layer[0], own_layer[1], own_layer[2]), "blk", 1)
    second_out, second_stored = forward_pass(first_out, other_layer, own_docs)
    upstream, other_grads = backward_pass(
        second_out.astype(jnp.float32), other_layer, second_stored, own_docs
    )
    returned = (
        from_behind(other_grads[0].astype(jnp.bfloat16), "blk", -1).astype(jnp.float32),
        from_behind(other_grads[1].astype(jnp.bfloat16), "blk", -1).astype(jnp.float32),
    )
    unused_grad, own_grads = backward_pass(upstream, own_layer, first_stored, own_docs)
    total_in = (own_grads[0] + returned[0]).astype(jnp.bfloat16)[None]
    total_out = (own_grads[1] + returned[1]).astype(jnp.bfloat16)[None]
    return (total_in, total_out)


def solution(mesh):
    placed = (
        P("blk", "stretch"),
        P(),
        P("blk", "stretch", None),
        P("blk", None, "stretch"),
        P("blk", "stretch"),
    )
    return jax.shard_map(
        shards,
        mesh=mesh,
        in_specs=placed,
        out_specs=(P("blk", "stretch", None), P("blk", None, "stretch")),
        check_vma=False,
    )
```

profile of v0, /device:TPU:2, one launch (start us, length us, event | category | flops | bytes accessed | tf_op | source)
XLA Modules:
  0.0 532.8 jit_solution(16170285538769937764)
XLA Ops:
  9.2 6.4 %psum.49 = f32[256,1]{0,1:T(1,128)S(1)} all-reduce(f32[256,1]{0,1:T(1,128)S(1)} %bitcast.456), channel_id=1, replica_groups=mesh['blk'=128,'stretch'=2] {'stretch'}, use_global_device_ids=true, to_apply=%region_1.0 | all-reduce | flops 256 | bytes 2048 | tf_op jit(solution)/shard_map/psum | solution.py:82
  15.6 4.3 fusion.147
  23.0 4.9 collective-permute-done
  27.9 100.7 %all-reduce.19.cloned.1.call-done = f32[256,1536]{1,0:T(8,128)} async-done(((f32[256,1536]{1,0:T(8,128)}), f32[256,1536]{1,0:T(8,128)}) %all-reduce.19.cloned.1.call-update) | async-done | bytes 1572880 | tf_op jit(solution)/shard_map/psum | solution.py:91
  129.8 2.3 slice.74
  136.3 9.2 %while.104 = (s32[]{:T(128)}, bf16[4,256,4,64]{1,3,2,0:T(8,128)(2,1)S(1)}, f32[4,256,64]{1,2,0:T(8,128)S(1)}, f32[4,256,64]{1,2,0:T(8,128)S(1)}, f32[4,256,4,64]...) while((s32[]{:T(128)}, bf16[4,256,4,64]{1,3,2,0:T(8,128)(2,1)S(1)}, ...), condition=%wide.region_6.7_spmd.clone, body=%wide.region_3.6_spmd.clone.sunk | while | flops 404682752 | bytes 3955789 | solution.py:70
  145.5 2.7 fusion.133
  148.2 6.4 %psum.51 = f32[256,1]{0,1:T(1,128)S(1)} all-reduce(f32[256,1]{0,1:T(1,128)S(1)} %bitcast.457), channel_id=1, replica_groups=mesh['blk'=128,'stretch'=2] {'stretch'}, use_global_device_ids=true, to_apply=%region_8.9 | all-reduce | flops 256 | bytes 2048 | tf_op jit(solution)/shard_map/psum | solution.py:82
  155.2 4.1 fusion.144
  159.6 2.4 broadcast.218.clone.3
  162.0 2.4 broadcast.218.clone.4
  164.4 2.4 broadcast.218.clone.5
  166.8 13.5 %while.108 = (s32[]{:T(128)}, f32[4,4,256,256]{2,3,1,0:T(8,128)}, f32[4,4,256]{2,1,0:T(4,128)S(1)}, f32[4,4,256,256]{2,3,1,0:T(8,128)}, f32[4,4,256,1]{2,1,3,0:T...) while((s32[]{:T(128)}, f32[4,4,256,256]{2,3,1,0:T(8,128)}, ...), condition=%wide.region_31.32_spmd.clone, body=%wide.region_27.31_spmd.clone.sunk | while | flops 204209152 | bytes 7255669 | solution.py:70
  180.3 43.4 %all-reduce.21.cloned.1.call-done = f32[256,1536]{1,0:T(8,128)} async-done(((f32[256,1536]{1,0:T(8,128)}), f32[256,1536]{1,0:T(8,128)}) %all-reduce.21.cloned.1.call-update) | async-done | bytes 1572880 | tf_op jit(solution)/shard_map/psum | solution.py:91
  223.7 2.3 slice.81
  234.4 18.4 %while.105 = (s32[]{:T(128)}, bf16[4,256,4,64]{1,3,2,0:T(8,128)(2,1)}, f32[4,256,64]{1,2,0:T(8,128)}, f32[4,256,64]{1,2,0:T(8,128)}, f32[4,256,4,64]{1,3,2,0:T(8,128)S(1)}, /*index=5*/s32[256]{0:T(256)S(1)}, s32[]{:T(128)}) while((s32[]{:T(128)}, bf16[4,256,4,64]{1,3,2,0:T(8,128)(2,1)}, f32[4,256,64]{1,2,0:T(8,128)}, ...), condition=%wide.region_13.14_spmd.clone, body=%wide.region_10.13_spmd.clone.sunk | while | flops 404682752 | bytes 3955789 | solution.py:70
  236.7 2.4 fusion.223
  239.1 2.0 fusion.221
  241.3 2.4 fusion.223
  243.8 2.0 fusion.221
  245.9 2.4 fusion.223
  250.5 2.4 fusion.223
  252.9 2.5 fusion.129
  256.2 3.1 convolution_convert_fusion.3
  259.3 2.0 copy.31
  261.6 2.4 broadcast.218.clone
  264.0 2.4 broadcast.218.clone.1
  266.4 2.4 broadcast.218.clone.2
  270.6 21.5 %while.106 = (s32[]{:T(128)}, f32[4,4,256,256]{2,3,1,0:T(8,128)}, f32[4,4,256]{2,1,0:T(4,128)}, f32[4,4,256,256]{2,3,1,0:T(8,128)}, f32[4,4,256,1]{2,1,3,0:T(4,1...) while((s32[]{:T(128)}, f32[4,4,256,256]{2,3,1,0:T(8,128)}, ...), condition=%wide.region_19.20_spmd.clone, body=%wide.region_15.19_spmd.clone.sunk | while | flops 204209152 | bytes 7256685 | solution.py:70
  281.4 2.0 fusion.224
  292.1 10.7 %all-reduce.23.cloned.1.call-done = bf16[4,256,4,64]{1,3,2,0:T(8,128)(2,1)} async-done(((bf16[4,256,4,64]{1,3,2,0:T(8,128)(2,1)}), bf16[4,256,4,64]{1,3,2,0:T(8,128)(2,1)}) %all-reduce.23.cloned.1.call-update) | async-done | bytes 524304 | tf_op jit(solution)/shard_map/psum | solution.py:95
  302.8 2.1 transpose.178
  307.5 51.4 %while.107 = (s32[]{:T(128)}, f32[4,256,4,64]{1,3,2,0:T(8,128)}, f32[4,256,64]{1,2,0:T(8,128)}, f32[4,256,64]{1,2,0:T(8,128)}, f32[4,256,4,64]{1,3,2,0:T(8,128)}...) while((s32[]{:T(128)}, f32[4,256,4,64]{1,3,2,0:T(8,128)}, ...), condition=%wide.region_23.24_spmd.clone, body=%wide.region_20.23_spmd.clone.sunk | while | flops 809239552 | bytes 28776656 | solution.py:70
  308.3 2.6 fusion.231
  314.9 2.5 fusion.233
  317.4 3.0 fusion.235
  321.2 2.6 fusion.231
  327.7 2.5 fusion.233
  330.2 3.0 fusion.235
  334.0 2.6 fusion.231
  340.6 2.5 fusion.233
  343.1 3.0 fusion.235
  346.9 2.6 fusion.231
  353.4 2.5 fusion.233
  355.9 3.0 fusion.235
  362.4 4.6 fusion.140
  366.9 7.1 %psum.54 = f32[256]{0:T(256)} all-reduce(f32[256]{0:T(256)} %get-tuple-element.1250), channel_id=1, replica_groups=mesh['blk'=128,'stretch'=2] {'stretch'}, use_global_device_ids=true, to_apply=%region_25.26 | all-reduce | flops 256 | bytes 2048 | tf_op jit(solution)/shard_map/psum | solution.py:87
  376.4 3.1 convolution_convert_fusion.2
  379.6 2.1 copy.33
  381.7 2.0 convolution_convert_fusion.1
  383.8 4.7 collective-permute-start.4
  388.4 4.2 convolution_convert_fusion
  394.4 75.8 %all-reduce.25.cloned.1.call-done = bf16[4,256,4,64]{1,3,2,0:T(8,128)(2,1)} async-done(((bf16[4,256,4,64]{1,3,2,0:T(8,128)(2,1)}), bf16[4,256,4,64]{1,3,2,0:T(8,128)(2,1)}) %all-reduce.25.cloned.1.call-update) | async-done | bytes 524304 | tf_op jit(solution)/shard_map/psum | solution.py:95
  472.5 42.8 %while.109 = (s32[]{:T(128)}, f32[4,256,4,64]{1,3,2,0:T(8,128)}, f32[4,256,64]{1,2,0:T(8,128)S(1)}, f32[4,256,64]{1,2,0:T(8,128)S(1)}, f32[4,256,4,64]{1,3,2,0:T...) while((s32[]{:T(128)}, f32[4,256,4,64]{1,3,2,0:T(8,128)}, ...), condition=%wide.region_35.36_spmd.clone, body=%wide.region_32.35_spmd.clone.sunk | while | flops 809239552 | bytes 28776656 | solution.py:70
  473.4 2.5 fusion.243
  480.9 2.3 fusion.247
  484.1 2.5 fusion.243
  491.6 2.3 fusion.247
  494.8 2.5 fusion.243
  502.3 2.3 fusion.247
  505.5 2.5 fusion.243
  513.0 2.3 fusion.247
  518.1 3.7 fusion.127
  521.7 4.6 fusion.126
  (228 shorter events, 127.0 us)
Async XLA Ops:
  7.2 121.4 %all-reduce.19.cloned.1.call-start = ((), (), s32[]{:S(2)}) async-start(), calls=%async_computation | async-start | bytes 3145728 | tf_op jit(solution)/shard_map/psum | solution.py:91
  15.6 7.0 %copy-start.17 = (f32[256,1]{0,1:T(1,128)}, f32[256,1]{0,1:T(1,128)S(1)}, u32[]{:S(2)}) copy-start(f32[256,1]{0,1:T(1,128)S(1)} %add_rsqrt_fusion.1) | copy-start | bytes 3076
  19.9 203.8 %all-reduce.21.cloned.1.call-start = ((), (), s32[]{:S(2)}) async-start(), calls=%async_computation.1 | async-start | bytes 3145728 | tf_op jit(solution)/shard_map/psum | solution.py:91
  19.9 7.9 %collective-permute-start = (bf16[1024]{0:T(1024)(128)(2,1)S(1)}, bf16[1024]{0:T(1024)(128)(2,1)S(1)}, u32[]{:S(2)}, u32[]{:S(2)}) collective-permute-start(bf16[1024]{0:T(1024)(128)(2,1)S(1)} %reduce), channel_id=1, source_target_pairs={{0,2},{2,4},{4,6},{6,8},{8,10},{10,12},{12,14},{14,16},{16,18},{18... | collective-permute-start | bytes 6152 | tf_op jit(solution)/shard_map/ppermute | solution.py:22
  20.0 135.2 %collective-permute-start.1 = (bf16[1024,1536]{1,0:T(8,128)(2,1)}, bf16[1024,1536]{1,0:T(8,128)(2,1)}, u32[]{:S(2)}, u32[]{:S(2)}) collective-permute-start(bf16[1024,1536]{1,0:T(8,128)(2,1)} %bitcast.2), channel_id=1, source_target_pairs={{0,2},{2,4},{4,6},{6,8},{8,10},{10,12},{12,14},{14,16},{16,18},{18... | collective-permute-start | bytes 9437192 | tf_op jit(solution)/shard_map/ppermute | solution.py:22
  21.7 231.2 %collective-permute-start.2 = (bf16[1024,1024]{1,0:T(8,128)(2,1)}, bf16[1024,1024]{1,0:T(8,128)(2,1)}, u32[]{:S(2)}, u32[]{:S(2)}) collective-permute-start(bf16[1024,1024]{1,0:T(8,128)(2,1)} %bitcast.11), channel_id=1, source_target_pairs={{0,2},{2,4},{4,6},{6,8},{8,10},{10,12},{12,14},{14,16},{16,18},{18... | collective-permute-start | bytes 6291464 | tf_op jit(solution)/shard_map/ppermute | solution.py:22
  22.9 111.9 %copy-start.3 = (bf16[4,256,4,64]{1,3,2,0:T(8,128)(2,1)}, bf16[4,256,4,64]{1,3,2,0:T(8,128)(2,1)S(1)}, u32[]{:S(2)}) copy-start(bf16[4,256,4,64]{1,3,2,0:T(8,128)(2,1)S(1)} %fusion.163) | copy-start | bytes 1572868
  136.3 9.2 %copy-start.2 = (bf16[256,1024]{1,0:T(8,128)(2,1)S(1)}, bf16[256,1024]{1,0:T(8,128)(2,1)}, u32[]{:S(2)}) copy-start(bf16[256,1024]{1,0:T(8,128)(2,1)} %param.17) | copy-start | bytes 1572868
  145.4 13.9 %copy-start.5 = (bf16[4,256,4,64]{1,3,2,0:T(8,128)(2,1)}, bf16[4,256,4,64]{1,3,2,0:T(8,128)(2,1)S(1)}, u32[]{:S(2)}) copy-start(bf16[4,256,4,64]{1,3,2,0:T(8,128)(2,1)S(1)} %get-tuple-element.840) | copy-start | bytes 1572868
  145.5 13.9 %copy-start.12 = (f32[4,256,64]{1,2,0:T(8,128)}, f32[4,256,64]{1,2,0:T(8,128)S(1)}, u32[]{:S(2)}) copy-start(f32[4,256,64]{1,2,0:T(8,128)S(1)} %get-tuple-element.1937) | copy-start | bytes 786436
  159.4 143.4 %all-reduce.23.cloned.1.call-start = ((), (), s32[]{:S(2)}) async-start(), calls=%async_computation.2 | async-start | bytes 1048576 | tf_op jit(solution)/shard_map/psum | solution.py:95
  180.2 43.4 %copy-start.14 = (f32[4,4,256]{2,1,0:T(4,128)}, f32[4,4,256]{2,1,0:T(4,128)S(1)}, u32[]{:S(2)}) copy-start(f32[4,4,256]{2,1,0:T(4,128)S(1)} %get-tuple-element.1870) | copy-start | bytes 49156
  180.3 43.4 %copy-start.15 = (f32[4,4,256,1]{2,1,3,0:T(4,128)}, f32[4,4,256,1]{2,1,3,0:T(4,128)S(1)}, u32[]{:S(2)}) copy-start(f32[4,4,256,1]{2,1,3,0:T(4,128)S(1)} %get-tuple-element.1867) | copy-start | bytes 49156
  180.3 43.4 %copy-start.16 = (f32[4,4,256,1]{2,1,3,0:T(4,128)}, f32[4,4,256,1]{2,1,3,0:T(4,128)S(1)}, u32[]{:S(2)}) copy-start(f32[4,4,256,1]{2,1,3,0:T(4,128)S(1)} %get-tuple-element.1868) | copy-start | bytes 49156
  255.4 0.8 copy-start.7
  261.4 208.8 %all-reduce.25.cloned.1.call-start = ((), (), s32[]{:S(2)}) async-start(), calls=%async_computation.3 | async-start | bytes 1048576 | tf_op jit(solution)/shard_map/psum | solution.py:95
  307.5 5.6 %copy-start.1 = (f32[4,4,256,256]{2,3,1,0:T(8,128)S(1)}, f32[4,4,256,256]{2,3,1,0:T(8,128)}, u32[]{:S(2)}) copy-start(f32[4,4,256,256]{2,3,1,0:T(8,128)} %get-tuple-element.1821) | copy-start | bytes 12582916 | tf_op jit(solution)/shard_map/transpose(jvp())/while
  320.3 5.6 %copy-start.1 = (f32[4,4,256,256]{2,3,1,0:T(8,128)S(1)}, f32[4,4,256,256]{2,3,1,0:T(8,128)}, u32[]{:S(2)}) copy-start(f32[4,4,256,256]{2,3,1,0:T(8,128)} %get-tuple-element.1821) | copy-start | bytes 12582916 | tf_op jit(solution)/shard_map/transpose(jvp())/while
  333.2 5.6 %copy-start.1 = (f32[4,4,256,256]{2,3,1,0:T(8,128)S(1)}, f32[4,4,256,256]{2,3,1,0:T(8,128)}, u32[]{:S(2)}) copy-start(f32[4,4,256,256]{2,3,1,0:T(8,128)} %get-tuple-element.1821) | copy-start | bytes 12582916 | tf_op jit(solution)/shard_map/transpose(jvp())/while
  346.0 5.6 %copy-start.1 = (f32[4,4,256,256]{2,3,1,0:T(8,128)S(1)}, f32[4,4,256,256]{2,3,1,0:T(8,128)}, u32[]{:S(2)}) copy-start(f32[4,4,256,256]{2,3,1,0:T(8,128)} %get-tuple-element.1821) | copy-start | bytes 12582916 | tf_op jit(solution)/shard_map/transpose(jvp())/while
  361.3 5.7 %copy-start.13 = (f32[256,4,64]{0,2,1:T(8,128)}, f32[256,4,64]{0,2,1:T(8,128)S(1)}, u32[]{:S(2)}) copy-start(f32[256,4,64]{0,2,1:T(8,128)S(1)} %pad_add_fusion.3) | copy-start | bytes 786436
  361.3 12.8 %copy-start.8 = (bf16[256,1024]{1,0:T(8,128)(2,1)S(1)}, bf16[256,1024]{1,0:T(8,128)(2,1)}, u32[]{:S(2)}) copy-start(bf16[256,1024]{1,0:T(8,128)(2,1)} %copy-done.7) | copy-start | bytes 1572868
  361.3 12.8 %copy-start.19 = (f32[256,1]{0,1:T(1,128)S(1)}, f32[256,1]{0,1:T(1,128)}, u32[]{:S(2)}) copy-start(f32[256,1]{0,1:T(1,128)} %get-tuple-element.1194) | copy-start | bytes 3076
  361.4 1.0 copy-start.9
  366.9 14.8 %copy-start.4 = (bf16[4,256,4,64]{1,3,2,0:T(8,128)(2,1)S(1)}, bf16[4,256,4,64]{1,3,2,0:T(8,128)(2,1)}, u32[]{:S(2)}) copy-start(bf16[4,256,4,64]{1,3,2,0:T(8,128)(2,1)} %get-tuple-element.841) | copy-start | bytes 1572868
  375.6 0.8 copy-start.10
  383.8 134.3 %collective-permute-start.4 = (bf16[1024,1024]{1,0:T(8,128)(2,1)}, bf16[1024,1024]{1,0:T(8,128)(2,1)}, u32[]{:S(2)}, u32[]{:S(2)}) collective-permute-start(bf16[1024,1024]{1,0:T(8,128)(2,1)} %convolution_convert_fusion.1), channel_id=1, source_target_pairs={{0,254},{2,0},{4,2},{6,4},{8,6},{10,8},{12,10},{14,12},{16,14},{18... | collective-permute-start | bytes 6291464 | tf_op jit(solution)/shard_map/ppermute | solution.py:22
  392.6 129.1 %collective-permute-start.3 = (bf16[1024,1536]{1,0:T(8,128)(2,1)}, bf16[1024,1536]{1,0:T(8,128)(2,1)}, u32[]{:S(2)}, u32[]{:S(2)}) collective-permute-start(bf16[1024,1536]{1,0:T(8,128)(2,1)} %convolution_convert_fusion), channel_id=1, source_target_pairs={{0,254},{2,0},{4,2},{6,4},{8,6},{10,8},{12,10},{14,12},{16,14},{18... | collective-permute-start | bytes 9437192 | tf_op jit(solution)/shard_map/ppermute | solution.py:22
  472.6 5.5 %copy-start = (f32[4,4,256,256]{2,3,1,0:T(8,128)S(1)}, f32[4,4,256,256]{2,3,1,0:T(8,128)}, u32[]{:S(2)}) copy-start(f32[4,4,256,256]{2,3,1,0:T(8,128)} %get-tuple-element.1905) | copy-start | bytes 12582916 | tf_op jit(solution)/shard_map/transpose(jvp())/while
  483.2 5.5 %copy-start = (f32[4,4,256,256]{2,3,1,0:T(8,128)S(1)}, f32[4,4,256,256]{2,3,1,0:T(8,128)}, u32[]{:S(2)}) copy-start(f32[4,4,256,256]{2,3,1,0:T(8,128)} %get-tuple-element.1905) | copy-start | bytes 12582916 | tf_op jit(solution)/shard_map/transpose(jvp())/while
  493.9 5.5 %copy-start = (f32[4,4,256,256]{2,3,1,0:T(8,128)S(1)}, f32[4,4,256,256]{2,3,1,0:T(8,128)}, u32[]{:S(2)}) copy-start(f32[4,4,256,256]{2,3,1,0:T(8,128)} %get-tuple-element.1905) | copy-start | bytes 12582916 | tf_op jit(solution)/shard_map/transpose(jvp())/while
  504.6 5.5 %copy-start = (f32[4,4,256,256]{2,3,1,0:T(8,128)S(1)}, f32[4,4,256,256]{2,3,1,0:T(8,128)}, u32[]{:S(2)}) copy-start(f32[4,4,256,256]{2,3,1,0:T(8,128)} %get-tuple-element.1905) | copy-start | bytes 12582916 | tf_op jit(solution)/shard_map/transpose(jvp())/while
  515.3 1.5 copy-start.18
  516.9 1.2 copy-start.6
  516.9 1.2 copy-start.11
Sparse Core Ops, SparseCore 0:
  20.0 108.5 all-reduce.18
  159.5 64.1 all-reduce.20
  261.5 41.2 all-reduce.22
  381.8 88.3 all-reduce.24
where the time goes:
time: 537 us; the launch traced here: 533 us
  waiting for transfers between devices  236 us (44%)
  matrix products  143 us (27%)
  other arithmetic  62.7 us (12%)
  local copies, waits for them, and re-layouts  47.7 us (9%)
  blocking collectives  20 us (4%)
  between operations  14.2 us (3%)
  starting transfers between devices  8.91 us (2%)
    psum x2, waiting for transfers between devices, project(): lax.psum(jnp.dot(left_side, right_side, preferred_element_type=jnp.float3...  144 us
    psum x2, waiting for transfers between devices, project_back(): lax.psum(jnp.dot(left_side, right_side.T, preferred_element_type=jnp.floa...  86.5 us
    dot_general x24, matrix products, one_group(): return jnp.einsum('gts,sd->tgd', weights, group_values, precision=PRECISE)  54.8 us
    dot_general x32, matrix products, one_group(): jnp.einsum('tgd,sd->gts', group_queries, group_keys, precision=PRECISE)  53.3 us
    another operation x18, local copies, waits for them, and re-layouts  19.9 us
    dynamic_update_slice x16, other arithmetic, attend(): lax.map(one_group, (jnp.moveaxis(query_rows, 1, 0), jnp.moveaxis(key_rows...  17.3 us
    psum x2, blocking collectives, norm_scale(): lax.psum(jnp.sum(value_rows * value_rows, axis=1, keepdims=True), 'stretch')  12.9 us
    reduce_sum x8, other arithmetic, one_group(): weights = jnp.exp(scores - row_max)  11.2 us
  transfers between devices with their start and end apart: 9, of which 5 were waited for; matrix products, arithmetic and copies ran while one was open for 31% of the time, Pallas kernels for 0%

commit v1 on v0

v1 whole, which is shorter than its diff:
```python
from functools import partial

import numpy as np
import jax
import jax.numpy as jnp
from jax import lax
from jax.experimental import pallas as pl
from jax.experimental.pallas import tpu as pltpu
from jax.sharding import PartitionSpec as P

MODEL_WIDTH = 2048
HEAD_WIDTH = 64
EPS = 1e-05
THETA = 10000.0
F32, BF16 = jnp.float32, jnp.bfloat16

T = 256
HALF = 1024
QW, KW = 512, 128
OWN = QW + 2 * KW
MSG = T + 16

NN = (((1,), (0,)), ((), ()))
NT = (((1,), (1,)), ((), ()))
TN = (((0,), (0,)), ((), ()))


def dot(left, right, dims=NN):
    return lax.dot_general(left, right, dims, preferred_element_type=F32)


def tables():
    lane = np.arange(128)
    angles = np.arange(T)[:, None] * THETA ** (-2.0 * (lane % 32) / HEAD_WIDTH)[None, :]
    sign = np.where(lane % 64 < 32, -1.0, 1.0)[None, :]
    return np.cos(angles).astype(np.float32), (np.sin(angles) * sign).astype(np.float32)


def lane_index(shape):
    return lax.broadcasted_iota(jnp.int32, shape, 1)


def exchange_halves(block):
    first = lane_index(block.shape) % 64 < 32
    return jnp.where(first, pltpu.roll(block, 96, 1), pltpu.roll(block, 32, 1))


def rotate(block, cosine, sine):
    return block * cosine + exchange_halves(block) * sine


def rotate_back(block, cosine, sine):
    return block * cosine - exchange_halves(block) * sine


def to_row(column):
    return jnp.transpose(jnp.broadcast_to(column, (T, 128)))[0:1, :]


def to_lanes(row):
    return jnp.transpose(jnp.broadcast_to(row, (128, T)))


def split_row(row):
    high = row.astype(BF16)
    low = (row - high.astype(F32)).astype(BF16)
    return high, low


def wide(tile, width):
    return jnp.concatenate([tile] * (width // 128), axis=1)


def put_sums(msg_ref, row):
    high, low = split_row(row)
    index = lax.broadcasted_iota(jnp.int32, (16, T), 0)
    rows = jnp.where(index == 0, high.astype(F32), jnp.where(index == 1, low.astype(F32), 0.0))
    msg_ref[T:, :T] = rows.astype(BF16)
    msg_ref[T:, T:] = jnp.zeros((16, OWN - T), BF16)


def get_sums(msg_ref):
    rows = msg_ref[T:, :T].astype(F32)
    return rows[0:1, :] + rows[1:2, :]


def gained(x_ref, gain_ref):
    return (x_ref[...].astype(F32) * gain_ref[...].astype(F32)).astype(BF16)


def send_projection_kernel(s_ref, x_ref, gain_ref, wq_ref, wk_ref, wv_ref, msg_ref, sums_ref):
    x = x_ref[...].astype(F32)
    normed = (x * gain_ref[...].astype(F32)).astype(BF16)
    msg_ref[:T, :QW] = dot(normed, wq_ref[...]).astype(BF16)
    both = jnp.concatenate([wk_ref[...], wv_ref[...]], axis=1)
    msg_ref[:T, QW:] = dot(normed, both).astype(BF16)
    row = to_row(jnp.sum(x * x, axis=1, keepdims=True))
    sums_ref[...] = jnp.broadcast_to(row, (8, T))
    put_sums(msg_ref, row)


def own_projection_kernel(s_ref, x_ref, gain_ref, wq_ref, wk_ref, wv_ref, out_ref):
    normed = gained(x_ref, gain_ref)
    out_ref[:, :QW] = dot(normed, wq_ref[...])
    both = jnp.concatenate([wk_ref[...], wv_ref[...]], axis=1)
    out_ref[:, QW:] = dot(normed, both)


def group_pair(block, group):
    low = lane_index(block.shape) < 64
    if group == 0:
        first = jnp.where(low, block, 0.0)
        return jnp.concatenate([first, pltpu.roll(first, 64, 1)], axis=0)
    second = jnp.where(low, 0.0, block)
    return jnp.concatenate([pltpu.roll(second, 64, 1), second], axis=0)


def attend_kernel(
    msg_ref, own_ref, sums_ref, drow_ref, dcol_ref, cos_ref, sin_ref,
    att_ref, q_ref, k_ref, v_ref, p_ref, scale_ref,
):
    sums = sums_ref[0:1, :] + get_sums(msg_ref)
    scale = to_lanes(lax.rsqrt(sums / MODEL_WIDTH + EPS))
    scale_ref[...] = scale
    cosine, sine = cos_ref[...], sin_ref[...]

    def column(start):
        cols = slice(start, start + 128)
        return (own_ref[:, cols] + msg_ref[:T, cols].astype(F32)) * scale

    k = rotate(column(QW), cosine, sine)
    v = column(QW + KW)
    k_ref[...] = k.astype(BF16)
    v_ref[...] = v.astype(BF16)
    key = lax.broadcasted_iota(jnp.int32, (T, T), 0)
    query = lax.broadcasted_iota(jnp.int32, (T, T), 1)
    bias = jnp.where((key <= query) & (dcol_ref[...] == drow_ref[...]), 0.0, -1e30)
    for group in range(2):
        keys = group_pair(k, group).astype(BF16)
        values = jnp.transpose(group_pair(v, group)).astype(BF16)
        outs = []
        for pair in (2 * group, 2 * group + 1):
            q = (rotate(column(128 * pair), cosine, sine) * 0.125).astype(BF16)
            q_ref[:, 128 * pair : 128 * pair + 128] = q
            scores = dot(keys, q, NT)
            for half in range(2):
                part = scores[T * half : T * half + T] + bias
                weights = jnp.exp(part - jnp.max(part, axis=0, keepdims=True))
                weights = weights * (1.0 / jnp.sum(weights, axis=0, keepdims=True))
                start = (2 * pair + half) * T
                p_ref[start : start + T, :] = weights.astype(BF16)
            outs.append(dot(values, p_ref[2 * pair * T : 2 * pair * T + 2 * T, :]))
        att_ref[:, T * group : T * group + T] = jnp.transpose(
            jnp.concatenate(outs, axis=0)
        ).astype(BF16)


def attend_back_kernel(
    with_sums, recv_ref, own_ref, q_ref, k_ref, v_ref, p_ref, cos_ref, sin_ref, pg_ref
):
    cosine, sine = cos_ref[...], sin_ref[...]
    k, v = k_ref[...].astype(F32), v_ref[...].astype(F32)
    low = lane_index((T, 128)) < 64
    total = jnp.zeros((T, 128), F32)
    dks, dvs = [], []
    for group in range(2):
        keys = jnp.transpose(group_pair(k, group)).astype(BF16)
        values = group_pair(v, group).astype(BF16)
        dk = jnp.zeros((T, 128), F32)
        dv = jnp.zeros((T, 128), F32)
        dqs = []
        for pair in (2 * group, 2 * group + 1):
            cols = slice(128 * pair, 128 * pair + 128)
            grad = own_ref[:, cols] + recv_ref[:, cols].astype(F32)
            q = q_ref[:, cols].astype(F32)
            dp = dot(values, grad.astype(BF16), NT)
            dss = []
            for half in range(2):
                start = (2 * pair + half) * T
                weights = p_ref[start : start + T, :]
                wide_weights = weights.astype(F32)
                part = dp[T * half : T * half + T]
                product = wide_weights * part
                ds = product - wide_weights * jnp.sum(product, axis=0, keepdims=True)
                ds = ds.astype(BF16)
                keep = low if half == 0 else jnp.logical_not(low)
                dv = dv + dot(weights, jnp.where(keep, grad, 0.0).astype(BF16))
                dk = dk + dot(ds, jnp.where(keep, q, 0.0).astype(BF16))
                dss.append(ds)
            dqs.append(dot(keys, jnp.concatenate(dss, axis=0)))
        dq = jnp.transpose(jnp.concatenate(dqs, axis=0))
        for i, pair in enumerate((2 * group, 2 * group + 1)):
            cols = slice(128 * pair, 128 * pair + 128)
            block = dq[:, 128 * i : 128 * i + 128]
            if with_sums:
                total = total + block * q_ref[:, cols].astype(F32)
            pg_ref[:T, cols] = rotate_back(block * 0.125, cosine, sine).astype(BF16)
        dks.append(dk + pltpu.roll(dk, 64, 1))
        dvs.append(dv + pltpu.roll(dv, 64, 1))
    dk = jnp.where(low, dks[0], dks[1])
    dv = jnp.where(low, dvs[0], dvs[1])
    pg_ref[:T, QW : QW + KW] = rotate_back(dk, cosine, sine).astype(BF16)
    pg_ref[:T, QW + KW :] = dv.astype(BF16)
    if with_sums:
        total = total + dk * k + dv * v
        put_sums(pg_ref, to_row(jnp.sum(total, axis=1, keepdims=True)))


def own_output_kernel(s_ref, x_ref, gain_ref, scale_ref, att_ref, w_ref, acc_ref, normed_ref):
    x = x_ref[...].astype(F32)
    acc_ref[...] = x + dot(att_ref[...], w_ref[...])
    scale = wide(scale_ref[...], HALF)
    normed_ref[...] = (x * scale * gain_ref[...].astype(F32)).astype(BF16)


def output_kernel(s_ref, acc_ref, att_ref, w_ref, out_ref):
    out_ref[...] = (acc_ref[...] + dot(att_ref[...], w_ref[...])).astype(BF16)


def output_turn_kernel(s_ref, acc_ref, att_ref, w_ref, out_ref, msg_ref):
    out = (acc_ref[...] + dot(att_ref[...], w_ref[...])).astype(BF16)
    out_ref[...] = out
    msg_ref[...] = dot(out, w_ref[...], NT).astype(BF16)


def output_back_kernel(s_ref, up_ref, w_ref, out_ref):
    out_ref[...] = dot(up_ref[...], w_ref[...], NT).astype(out_ref.dtype)


def own_back_kernel(s_ref, pg_ref, wq_ref, wk_ref, wv_ref, out_ref):
    both = jnp.concatenate([wk_ref[...], wv_ref[...]], axis=1)
    out_ref[...] = dot(pg_ref[:T, :QW], wq_ref[...], NT) + dot(pg_ref[:T, QW:], both, NT)


def input_back_kernel(
    s_ref, acc_ref, recv_ref, pg_ref, wq_ref, wk_ref, wv_ref, x_ref, gain_ref, scale_ref, up_ref,
    out_ref,
):
    both = jnp.concatenate([wk_ref[...], wv_ref[...]], axis=1)
    grad = acc_ref[...] + dot(recv_ref[:T, :QW], wq_ref[...], NT)
    grad = grad + dot(recv_ref[:T, QW:], both, NT)
    scale = scale_ref[...]
    sums = to_lanes((get_sums(recv_ref) + get_sums(pg_ref)) / MODEL_WIDTH)
    factor = wide(scale * scale * sums, HALF)
    out = up_ref[...].astype(F32) + wide(scale, HALF) * (gain_ref[...].astype(F32) * grad)
    out_ref[...] = (out - x_ref[...].astype(F32) * factor).astype(BF16)


def output_weight_kernel(s_ref, a1_ref, r1_ref, u1_ref, a2_ref, r2_ref, u2_ref, out_ref):
    s = s_ref[0]
    u1, u2 = u1_ref[...], u2_ref[...]
    out_ref[pl.ds(QW * s, QW), :] = (dot(a1_ref[...], u1, TN) + dot(a2_ref[...], u2, TN)).astype(BF16)
    out_ref[pl.ds(QW * (1 - s), QW), :] = (
        dot(r1_ref[...], u1, TN) + dot(r2_ref[...], u2, TN)
    ).astype(BF16)


def input_weight_kernel(own, s_ref, n1_ref, p1_ref, n2_ref, p2_ref, *rest):
    out_ref, held, sems = rest[-3:]
    owner = s_ref[0] if own else 1 - s_ref[0]
    n1, n2 = n1_ref[...], n2_ref[...]
    copies = []
    for i, (start, size, place) in enumerate(
        ((0, QW, QW * owner), (QW, KW, 1024 + KW * owner), (QW + KW, KW, 1280 + KW * owner))
    ):
        cols = slice(start, start + size)
        part = dot(n1, p1_ref[:T, cols], TN) + dot(n2, p2_ref[:T, cols], TN)
        held[:, cols] = part.astype(BF16)
        copy = pltpu.make_async_copy(
            held.at[:, cols], out_ref.at[:, pl.ds(pl.multiple_of(place, 128), size)], sems.at[i]
        )
        copy.start()
        copies.append(copy)
    for copy in copies:
        copy.wait()


PARAMS = pltpu.CompilerParams(vmem_limit_bytes=40 * 1024 * 1024)


def full(*shape):
    return pl.BlockSpec(shape, lambda i, s: (0,) * len(shape))


def weight_specs(own):
    def at(base):
        return lambda i, s: (0, base + (s[0] if own else 1 - s[0]))

    return [
        pl.BlockSpec((HALF, QW), at(0)),
        pl.BlockSpec((HALF, KW), at(8)),
        pl.BlockSpec((HALF, KW), at(10)),
    ]


def out_weight_spec(own):
    return pl.BlockSpec((QW, HALF), lambda i, s: (s[0] if own else 1 - s[0], 0))


def shape_of(dtype, *shape):
    return jax.ShapeDtypeStruct(shape, dtype)


def call(kernel, s, in_specs, outs, args, flops, name, out_specs=None, scratch=(), aliases=None):
    moved = sum(int(np.prod(a.shape)) * a.dtype.itemsize for a in list(args) + list(outs))
    return pl.pallas_call(
        kernel,
        grid_spec=pltpu.PrefetchScalarGridSpec(
            num_scalar_prefetch=1,
            grid=(1,),
            in_specs=in_specs,
            out_specs=out_specs or [full(*o.shape) for o in outs],
            scratch_shapes=list(scratch),
        ),
        out_shape=list(outs),
        compiler_params=PARAMS,
        cost_estimate=pl.CostEstimate(flops=flops, bytes_accessed=moved, transcendentals=0),
        input_output_aliases=aliases or {},
        name=name,
    )(s, *args)


def swap(value):
    return lax.ppermute(value, "stretch", [(0, 1), (1, 0)])


def hop(value, step):
    count = lax.axis_size("blk")
    return lax.ppermute(value, "blk", [(i, (i + step) % count) for i in range(count)])


def no_scalar(kernel):
    return lambda s_ref, *refs: kernel(*refs)


def forward_start(s, x, layer, docs, trig):
    w_in, w_out, gain = layer
    xw = [full(T, HALF), full(1, HALF)]
    msg, sums = call(
        send_projection_kernel, s, xw + weight_specs(False),
        [shape_of(BF16, MSG, OWN), shape_of(F32, 8, T)],
        [x, gain, w_in, w_in, w_in], 2 * T * HALF * OWN, "send_projection",
    )
    recv = swap(msg)
    (own,) = call(
        own_projection_kernel, s, xw + weight_specs(True), [shape_of(F32, T, OWN)],
        [x, gain, w_in, w_in, w_in], 2 * T * HALF * OWN, "own_projection",
    )
    att, q, k, v, p, scale = call(
        no_scalar(attend_kernel), s,
        [full(MSG, OWN), full(T, OWN), full(8, T), full(1, T), full(T, 1), full(T, 128), full(T, 128)],
        [
            shape_of(BF16, T, QW), shape_of(BF16, T, QW), shape_of(BF16, T, KW),
            shape_of(BF16, T, KW), shape_of(BF16, 8 * T, T), shape_of(F32, T, 128),
        ],
        [recv, own, sums, docs[None, :], docs[:, None], *trig], 2 * 8 * T * T * 512, "attend",
    )
    att_recv = swap(att)
    acc, normed = call(
        own_output_kernel, s,
        [full(T, HALF), full(1, HALF), full(T, 128), full(T, QW), out_weight_spec(True)],
        [shape_of(F32, T, HALF), shape_of(BF16, T, HALF)],
        [x, gain, scale, att, w_out], 2 * T * HALF * QW, "own_output",
    )
    return acc, normed, att, att_recv, (q, k, v, p), scale


def backward_start(s, recv, own, kept, trig, with_sums):
    q, k, v, p = kept
    (pg,) = call(
        no_scalar(partial(attend_back_kernel, with_sums)), s,
        [
            full(T, QW), full(T, QW), full(T, QW), full(T, KW), full(T, KW), full(8 * T, T),
            full(T, 128), full(T, 128),
        ],
        [shape_of(BF16, MSG if with_sums else T, OWN)],
        [recv, own, q, k, v, p, *trig], 2 * 8 * T * T * 1024, "attend_back",
    )
    return pg, swap(pg)


def output_back(s, up, w_out, own):
    (out,) = call(
        output_back_kernel, s, [full(T, HALF), out_weight_spec(own)],
        [shape_of(F32 if own else BF16, T, QW)], [up, w_out], 2 * T * HALF * QW, "output_back",
    )
    return out


def input_weights(s, own, n1, p1, n2, p2, held=None):
    specs = [full(*a.shape) for a in (n1, p1, n2, p2)]
    args = [n1, p1, n2, p2]
    if held is not None:
        specs.append(pl.BlockSpec(memory_space=pl.ANY))
        args.append(held)
    (out,) = call(
        partial(input_weight_kernel, own), s, specs, [shape_of(BF16, HALF, 1536)], args,
        2 * 2 * T * HALF * OWN, "input_weights",
        out_specs=[pl.BlockSpec(memory_space=pl.ANY)],
        scratch=[pltpu.VMEM((HALF, OWN), BF16), pltpu.SemaphoreType.DMA((3,))],
        aliases={5: 0} if held is not None else None,
    )
    return out


def shards(activations, document_ids, joint_input_weights, output_weights, norm_gains):
    blk = lax.axis_index("blk")
    s = lax.axis_index("stretch").astype(jnp.int32)[None]
    own_docs = lax.dynamic_slice_in_dim(document_ids, blk * T, T)
    next_blk = lax.rem(blk + 1, lax.axis_size("blk"))
    next_docs = lax.dynamic_slice_in_dim(document_ids, next_blk * T, T)
    w_in, w_out, gain = layer = (joint_input_weights[0], output_weights[0], norm_gains)
    trig = tuple(jnp.asarray(t) for t in tables())

    acc1, n1, a1, r1, kept1, _ = forward_start(s, activations, layer, own_docs, trig)
    (first_out,) = call(
        output_kernel, s, [full(T, HALF), full(T, QW), out_weight_spec(False)],
        [shape_of(BF16, T, HALF)], [acc1, r1, w_out], 2 * T * HALF * QW, "output",
    )

    x2 = hop(first_out, -1)
    acc2, n2, a2, r2, kept2, scale2 = forward_start(s, x2, layer, next_docs, trig)
    second_out, msg = call(
        output_turn_kernel, s, [full(T, HALF), full(T, QW), out_weight_spec(False)],
        [shape_of(BF16, T, HALF), shape_of(BF16, T, QW)], [acc2, r2, w_out],
        4 * T * HALF * QW, "output_turn",
    )
    recv = swap(msg)
    own = output_back(s, second_out, w_out, True)
    p2, p2_recv = backward_start(s, recv, own, kept2, trig, True)
    (acc,) = call(
        own_back_kernel, s, [full(MSG, OWN)] + weight_specs(True), [shape_of(F32, T, HALF)],
        [p2, w_in, w_in, w_in], 2 * T * HALF * OWN, "own_back",
    )
    (up2,) = call(
        input_back_kernel, s,
        [full(T, HALF), full(MSG, OWN), full(MSG, OWN)] + weight_specs(False)
        + [full(T, HALF), full(1, HALF), full(T, 128), full(T, HALF)],
        [shape_of(BF16, T, HALF)],
        [acc, p2_recv, p2, w_in, w_in, w_in, x2, gain, scale2, second_out],
        2 * T * HALF * OWN, "input_back",
    )

    up1 = hop(up2, 1)
    recv = swap(output_back(s, up1, w_out, False))
    own = output_back(s, up1, w_out, True)
    p1, p1_recv = backward_start(s, recv, own, kept1, trig, False)
    (total_out,) = call(
        output_weight_kernel, s,
        [full(T, QW), full(T, QW), full(T, HALF)] * 2, [shape_of(BF16, HALF, HALF)],
        [a1, r1, up1, a2, r2, second_out], 2 * 2 * T * HALF * HALF, "output_weights",
    )
    half_in = input_weights(s, True, n1, p1, n2, p2)
    total_in = input_weights(s, False, n1, p1_recv, n2, p2_recv, half_in)
    return (total_in[None], total_out[None])


def solution(mesh):
    placed = (
        P("blk", "stretch"),
        P(),
        P("blk", "stretch", None),
        P("blk", None, "stretch"),
        P("blk", "stretch"),
    )
    return jax.shard_map(
        shards,
        mesh=mesh,
        in_specs=placed,
        out_specs=(P("blk", "stretch", None), P("blk", None, "stretch")),
        check_vma=False,
    )
```

time: 537 us -> 130 us (0.24)
  waiting for transfers between devices: 236 us -> 65.3 us
  matrix products: 143 us -> 0 us
  other arithmetic: 62.7 us -> 0 us
  local copies, waits for them, and re-layouts: 47.7 us -> 8.97 us
  Pallas kernels: 0 us -> 26.2 us
  blocking collectives: 20 us -> 0 us
  starting transfers between devices: 8.91 us -> 26.6 us
  between operations: 14.2 us -> 1.11 us
    psum x4 -> x0, waiting for transfers between devices: 231 us -> none  [the longest x2 144 us: project(): lax.psum(jnp.dot(left_side, right_side, preferred_element_type=jnp.float3...]
    dot_general x67 -> x0, matrix products: 143 us -> none  [the longest x24 54.8 us: one_group(): return jnp.einsum('gts,sd->tgd', weights, group_values, precision=PRECISE)]
    ppermute x5 -> x10, waiting for transfers between devices: 4.86 us -> 65.3 us  [the longest x8 44.1 us: swap(): return lax.ppermute(value, 'stretch', [(0, 1), (1, 0)])]
    pallas_call x0 -> x20, Pallas kernels: none -> 26.2 us  [call(): pl.pallas_call(kernel, grid_spec=pltpu.PrefetchScalarGridSpec(num_scalar_...]
    psum x3 -> x0, blocking collectives: 20 us -> none  [the longest x2 12.9 us: norm_scale(): lax.psum(jnp.sum(value_rows * value_rows, axis=1, keepdims=True), 'stretch')]
    another operation x18 -> x0, local copies, waits for them, and re-layouts: 19.9 us -> none
    ppermute x5 -> x10, starting transfers between devices: 8.35 us -> 26.6 us  [the longest x8 20.5 us: swap(): return lax.ppermute(value, 'stretch', [(0, 1), (1, 0)])]
    dynamic_update_slice x16 -> x0, other arithmetic: 17.3 us -> none  [attend(): lax.map(one_group, (jnp.moveaxis(query_rows, 1, 0), jnp.moveaxis(key_rows...]
  transfers between devices with their start and end apart: 9 -> 10, of which waited for: 5 -> 10; matrix products, arithmetic and copies ran while one was open for 31% -> 1% of each run, Pallas kernels for 0% -> 7%
where the time goes in v1:
time: 130 us; the launch traced here: 128 us
  waiting for transfers between devices  65.3 us (50%)
  starting transfers between devices  26.6 us (20%)
  Pallas kernels  26.2 us (20%)
  local copies, waits for them, and re-layouts  8.97 us (7%)
    ppermute x8, waiting for transfers between devices, swap(): return lax.ppermute(value, 'stretch', [(0, 1), (1, 0)])  44.1 us
    pallas_call x20, Pallas kernels, call(): pl.pallas_call(kernel, grid_spec=pltpu.PrefetchScalarGridSpec(num_scalar_...  26.2 us
    ppermute x2, waiting for transfers between devices, hop(): lax.ppermute(value, 'blk', [(i, (i + step) % count) for i in range(count)])  21.2 us
    ppermute x8, starting transfers between devices, swap(): return lax.ppermute(value, 'stretch', [(0, 1), (1, 0)])  20.5 us
    unnamed x60, local copies, waits for them, and re-layouts  7.87 us
    ppermute x2, starting transfers between devices, hop(): lax.ppermute(value, 'blk', [(i, (i + step) % count) for i in range(count)])  6.09 us
  transfers between devices with their start and end apart: 10, of which 10 were waited for; matrix products, arithmetic and copies ran while one was open for 1% of the time, Pallas kernels for 7%

profile of v1, /device:TPU:2, one launch (start us, length us, event | category | flops | bytes accessed | tf_op | source)
XLA Modules:
  0.0 128.2 jit_solution(11287491204554149368)
XLA Ops:
  0.6 0.0 copy-start
  0.6 1.9 %copy-done = bf16[1,1024,1536]{2,1,0:T(8,128)(2,1)S(1)} copy-done((bf16[1,1024,1536]{2,1,0:T(8,128)(2,1)S(1)}, bf16[1,1024,1536]{2,1,0:T(8,128)(2,1)}, u32[]{:S(2)}) %copy-start) | copy-done | bytes 3145752
  2.5 1.0 copy-done.7
  3.6 0.7 copy-done.14
  4.3 1.4 %send_projection.2 = (bf16[272,768]{1,0:T(8,128)(2,1)}, f32[8,256]{1,0:T(8,128)S(1)}) custom-call(s32[1]{0:T(128)} %bitcast.s_ref, bf16[256,1024]{1,0:T(8,128)(2,1)S(1)} %copy-done.7, bf16[1,1024]{1,0:T(2,128)(2,1)S(1)} %copy-done.14, bf16[1024,1536]{1,0:T(8,128)(2,1)S(1)} %bitcast.9, bf16[1024,1536]{1,0:T(8,128)(2,1)S(1)} %bitcast.10, ...), custom_call_target="tpu_custom_call" | custom-call | flops 402653184 | bytes 10389504 | tf_op jit(solution)/shard_map/send_projection/pallas_call | solution.py:306
  5.6 2.1 %collective-permute-start = (bf16[272,768]{1,0:T(8,128)(2,1)}, bf16[272,768]{1,0:T(8,128)(2,1)}, u32[]{:S(2)}, u32[]{:S(2)}) collective-permute-start(bf16[272,768]{1,0:T(8,128)(2,1)} %get-tuple-element.24), channel_id=1, source_target_pairs={{0,1},{1,0},{2,3},{3,2},{4,5},{5,4},{6,7},{7,6},{8,9},{9,8},{10,11... | collective-permute-start | bytes 1253384 | tf_op jit(solution)/shard_map/ppermute | solution.py:324
  7.7 0.8 fusion
  8.6 0.1 copy.10.refs_4_
  8.7 0.0 copy-done.1
  8.7 0.0 copy-done.15
  8.7 0.0 copy-start.8
  8.8 1.0 copy-done.8
  9.8 0.6 own_projection.2.refs_1_
  10.4 8.4 %collective-permute-done.refs_0_ = bf16[272,768]{1,0:T(8,128)(2,1)} collective-permute-done((bf16[272,768]{1,0:T(8,128)(2,1)}, bf16[272,768]{1,0:T(8,128)(2,1)}, u32[]{:S(2)}, u32[]{:S(2)}) %collective-permute-start) | collective-permute-done | bytes 417824 | tf_op jit(solution)/shard_map/ppermute | solution.py:324
  18.8 0.7 copy-done.17
  19.5 3.3 %attend.2 = (bf16[256,512]{1,0:T(8,128)(2,1)S(1)}, bf16[256,512]{1,0:T(8,128)(2,1)S(1)}, bf16[256,128]{1,0:T(8,128)(2,1)S(1)}, bf16[256,128]{1,0:T(8,128)(2,1)S(...) custom-call(s32[1]{0:T(128)} %bitcast.s_ref, bf16[272,768]{1,0:T(8,128)(2,1)} %collective-permute-done.refs_0_, ...), custom_call_target="tpu_custom_call" | custom-call | flops 536870912 | bytes 3311616 | tf_op jit(solution)/shard_map/attend/pallas_call | solution.py:306
  22.8 0.6 copy-done.28
  23.5 2.1 %collective-permute-start.1 = (bf16[256,512]{1,0:T(8,128)(2,1)S(1)}, bf16[256,512]{1,0:T(8,128)(2,1)S(1)}, u32[]{:S(2)}, u32[]{:S(2)}) collective-permute-start(bf16[256,512]{1,0:T(8,128)(2,1)S(1)} %get-tuple-element.27.att_ref.a1_ref), channel_id=1, source_target_pairs={{0,1},{1,0},{2,3},{3,2},{4,5},{5,4},{6,7},{7,6},{8,9},{9,8},{10,11... | collective-permute-start | bytes 786440 | tf_op jit(solution)/shard_map/ppermute | solution.py:324
  25.6 0.0 copy-done.9
  25.6 0.4 own_output.2
  26.0 0.0 copy-start.10
  26.0 0.8 copy-done.10
  26.8 5.3 %collective-permute-done.1.att_ref.r1_ref = bf16[256,512]{1,0:T(8,128)(2,1)S(1)} collective-permute-done((bf16[256,512]{1,0:T(8,128)(2,1)S(1)}, bf16[256,512]{1,0:T(8,128)(2,1)S(1)}, u32[]{:S(2)}, u32[]{:S(2)}) %collective-permute-start.1) | collective-permute-done | bytes 262176 | tf_op jit(solution)/shard_map/ppermute | solution.py:324
  32.1 0.4 output.1
  32.6 0.0 copy-done.24
  32.6 0.0 copy-done.26
  32.6 6.0 %collective-permute-start.2 = (bf16[256,1024]{1,0:T(8,128)(2,1)S(1)}, bf16[256,1024]{1,0:T(8,128)(2,1)S(1)}, u32[]{:S(2)}, u32[]{:S(2)}) collective-permute-start(bf16[256,1024]{1,0:T(8,128)(2,1)S(1)} %output.1), channel_id=1, source_target_pairs={{0,254},{2,0},{4,2},{6,4},{8,6},{10,8},{12,10},{14,12},{16,14},{18... | collective-permute-start | bytes 1572872 | tf_op jit(solution)/shard_map/ppermute | solution.py:329
  38.6 6.7 %collective-permute-done.2.x_ref = bf16[256,1024]{1,0:T(8,128)(2,1)S(1)} collective-permute-done((bf16[256,1024]{1,0:T(8,128)(2,1)S(1)}, bf16[256,1024]{1,0:T(8,128)(2,1)S(1)}, u32[]{:S(2)}, u32[]{:S(2)}) %collective-permute-start.2) | collective-permute-done | bytes 524320 | tf_op jit(solution)/shard_map/ppermute | solution.py:329
  45.3 1.4 %send_projection.3 = (bf16[272,768]{1,0:T(8,128)(2,1)}, f32[8,256]{1,0:T(8,128)S(1)}) custom-call(s32[1]{0:T(128)} %bitcast.s_ref, bf16[256,1024]{1,0:T(8,128)(2,1)S(1)} %collective-permute-done.2.x_ref, bf16[1,1024]{1,0:T(2,128)(2,1)S(1)} %copy-done.15, bf16[1024,1536]{1,0:T(8,128)(2,1)S(1)} %bitcast.15, bf16[1024,1536]{1,0:T(8,128)(2,1)S(1)} %bitcast.16, ...), custom_call_target="tpu_custom_call" | custom-call | flops 402653184 | bytes 10389504 | tf_op jit(solution)/shard_map/send_projection/pallas_call | solution.py:306
  46.7 2.4 %collective-permute-start.3 = (bf16[272,768]{1,0:T(8,128)(2,1)}, bf16[272,768]{1,0:T(8,128)(2,1)}, u32[]{:S(2)}, u32[]{:S(2)}) collective-permute-start(bf16[272,768]{1,0:T(8,128)(2,1)} %get-tuple-element.30), channel_id=1, source_target_pairs={{0,1},{1,0},{2,3},{3,2},{4,5},{5,4},{6,7},{7,6},{8,9},{9,8},{10,11... | collective-permute-start | bytes 1253384 | tf_op jit(solution)/shard_map/ppermute | solution.py:324
  49.1 0.1 copy.11.refs_4_
  49.3 1.0 copy-done.5
  50.3 0.6 own_projection.3.refs_1_
  50.9 5.6 %collective-permute-done.3.refs_0_ = bf16[272,768]{1,0:T(8,128)(2,1)} collective-permute-done((bf16[272,768]{1,0:T(8,128)(2,1)}, bf16[272,768]{1,0:T(8,128)(2,1)}, u32[]{:S(2)}, u32[]{:S(2)}) %collective-permute-start.3) | collective-permute-done | bytes 417824 | tf_op jit(solution)/shard_map/ppermute | solution.py:324
  56.6 0.0 copy-done.19
  56.6 3.3 %attend.3 = (bf16[256,512]{1,0:T(8,128)(2,1)S(1)}, bf16[256,512]{1,0:T(8,128)(2,1)S(1)}, bf16[256,128]{1,0:T(8,128)(2,1)S(1)}, bf16[256,128]{1,0:T(8,128)(2,1)S(...) custom-call(s32[1]{0:T(128)} %bitcast.s_ref, bf16[272,768]{1,0:T(8,128)(2,1)} %collective-permute-done.3.refs_0_, ...), custom_call_target="tpu_custom_call" | custom-call | flops 536870912 | bytes 3311616 | tf_op jit(solution)/shard_map/attend/pallas_call | solution.py:306
  59.8 2.5 %collective-permute-start.4 = (bf16[256,512]{1,0:T(8,128)(2,1)S(1)}, bf16[256,512]{1,0:T(8,128)(2,1)S(1)}, u32[]{:S(2)}, u32[]{:S(2)}) collective-permute-start(bf16[256,512]{1,0:T(8,128)(2,1)S(1)} %get-tuple-element.33.att_ref.a2_ref), channel_id=1, source_target_pairs={{0,1},{1,0},{2,3},{3,2},{4,5},{5,4},{6,7},{7,6},{8,9},{9,8},{10,11... | collective-permute-start | bytes 786440 | tf_op jit(solution)/shard_map/ppermute | solution.py:324
  62.4 0.0 copy-done.6
  62.4 0.4 own_output.3
  62.8 6.2 %collective-permute-done.4.att_ref.r2_ref = bf16[256,512]{1,0:T(8,128)(2,1)S(1)} collective-permute-done((bf16[256,512]{1,0:T(8,128)(2,1)S(1)}, bf16[256,512]{1,0:T(8,128)(2,1)S(1)}, u32[]{:S(2)}, u32[]{:S(2)}) %collective-permute-start.4) | collective-permute-done | bytes 262176 | tf_op jit(solution)/shard_map/ppermute | solution.py:324
  69.0 0.7 output_turn.1
  69.7 3.0 %collective-permute-start.5 = (bf16[256,512]{1,0:T(8,128)(2,1)S(1)}, bf16[256,512]{1,0:T(8,128)(2,1)S(1)}, u32[]{:S(2)}, u32[]{:S(2)}) collective-permute-start(bf16[256,512]{1,0:T(8,128)(2,1)S(1)} %get-tuple-element.35), channel_id=1, source_target_pairs={{0,1},{1,0},{2,3},{3,2},{4,5},{5,4},{6,7},{7,6},{8,9},{9,8},{10,11... | collective-permute-start | bytes 786440 | tf_op jit(solution)/shard_map/ppermute | solution.py:324
  72.8 0.5 output_back.3.refs_1_
  73.3 5.7 %collective-permute-done.5.refs_0_ = bf16[256,512]{1,0:T(8,128)(2,1)S(1)} collective-permute-done((bf16[256,512]{1,0:T(8,128)(2,1)S(1)}, bf16[256,512]{1,0:T(8,128)(2,1)S(1)}, u32[]{:S(2)}, u32[]{:S(2)}) %collective-permute-start.5) | collective-permute-done | bytes 262176 | tf_op jit(solution)/shard_map/ppermute | solution.py:324
  78.9 2.1 %attend_back.2.pg_ref.p2_ref = bf16[272,768]{1,0:T(8,128)(2,1)S(1)} custom-call(s32[1]{0:T(128)} %bitcast.s_ref, bf16[256,512]{1,0:T(8,128)(2,1)S(1)} %collective-permute-done.5.refs_0_, f32[256,512]{1,0:T(8,128)S(1)} %output_back.3.refs_1_, bf16[256,512]{1,0:T(8,128)(2,1)S(1)} %get-tuple-element.37.refs_2_, bf16[256,128]{1,0:T(8,128)(2,1)S(1)} %get-tuple-element.38.refs_3_, ...), custom_call_target="tpu_custom_call" | custom-call | flops 1073741824 | bytes 2908160 | tf_op jit(solution)/shard_map/attend_back/pallas_call | solution.py:306
  81.1 3.2 %collective-permute-start.6 = (bf16[272,768]{1,0:T(8,128)(2,1)S(1)}, bf16[272,768]{1,0:T(8,128)(2,1)S(1)}, u32[]{:S(2)}, u32[]{:S(2)}) collective-permute-start(bf16[272,768]{1,0:T(8,128)(2,1)S(1)} %attend_back.2.pg_ref.p2_ref), channel_id=1, source_target_pairs={{0,1},{1,0},{2,3},{3,2},{4,5},{5,4},{6,7},{7,6},{8,9},{9,8},{10,11... | collective-permute-start | bytes 1253384 | tf_op jit(solution)/shard_map/ppermute | solution.py:324
  84.3 0.6 own_back.1.acc_ref
  84.9 5.8 %collective-permute-done.6.recv_ref.p2_ref = bf16[272,768]{1,0:T(8,128)(2,1)S(1)} collective-permute-done((bf16[272,768]{1,0:T(8,128)(2,1)S(1)}, bf16[272,768]{1,0:T(8,128)(2,1)S(1)}, u32[]{:S(2)}, u32[]{:S(2)}) %collective-permute-start.6) | collective-permute-done | bytes 417824 | tf_op jit(solution)/shard_map/ppermute | solution.py:324
  90.7 0.8 input_back.1
  91.5 0.0 copy-start.23
  91.6 0.1 collective-permute-start.7
  91.6 14.5 %collective-permute-done.7.up_ref.u1_ref = bf16[256,1024]{1,0:T(8,128)(2,1)S(1)} collective-permute-done((bf16[256,1024]{1,0:T(8,128)(2,1)S(1)}, bf16[256,1024]{1,0:T(8,128)(2,1)S(1)}, u32[]{:S(2)}, u32[]{:S(2)}) %collective-permute-start.7) | collective-permute-done | bytes 524320 | tf_op jit(solution)/shard_map/ppermute | solution.py:329
  106.2 0.5 output_back.4
  106.7 2.5 %collective-permute-start.8 = (bf16[256,512]{1,0:T(8,128)(2,1)S(1)}, bf16[256,512]{1,0:T(8,128)(2,1)S(1)}, u32[]{:S(2)}, u32[]{:S(2)}) collective-permute-start(bf16[256,512]{1,0:T(8,128)(2,1)S(1)} %output_back.4), channel_id=1, source_target_pairs={{0,1},{1,0},{2,3},{3,2},{4,5},{5,4},{6,7},{7,6},{8,9},{9,8},{10,11... | collective-permute-start | bytes 786440 | tf_op jit(solution)/shard_map/ppermute | solution.py:324
  109.2 0.5 output_back.5.refs_1_
  109.7 5.0 %collective-permute-done.8.refs_0_ = bf16[256,512]{1,0:T(8,128)(2,1)S(1)} collective-permute-done((bf16[256,512]{1,0:T(8,128)(2,1)S(1)}, bf16[256,512]{1,0:T(8,128)(2,1)S(1)}, u32[]{:S(2)}, u32[]{:S(2)}) %collective-permute-start.8) | collective-permute-done | bytes 262176 | tf_op jit(solution)/shard_map/ppermute | solution.py:324
  114.6 0.0 copy-done.25
  114.7 0.0 copy-start.11
  114.7 1.9 %attend_back.3.p1_ref = bf16[256,768]{1,0:T(8,128)(2,1)S(1)} custom-call(s32[1]{0:T(128)} %bitcast.s_ref, bf16[256,512]{1,0:T(8,128)(2,1)S(1)} %collective-permute-done.8.refs_0_, f32[256,512]{1,0:T(8,128)S(1)} %output_back.5.refs_1_, bf16[256,512]{1,0:T(8,128)(2,1)S(1)} %copy-done.25, bf16[256,128]{1,0:T(8,128)(2,1)S(1)} %copy-done.27, ...), custom_call_target="tpu_custom_call" | custom-call | flops 1073741824 | bytes 2883584 | tf_op jit(solution)/shard_map/attend_back/pallas_call | solution.py:306
  116.5 2.5 %collective-permute-start.9 = (bf16[256,768]{1,0:T(8,128)(2,1)S(1)}, bf16[256,768]{1,0:T(8,128)(2,1)S(1)}, u32[]{:S(2)}, u32[]{:S(2)}) collective-permute-start(bf16[256,768]{1,0:T(8,128)(2,1)S(1)} %attend_back.3.p1_ref), channel_id=1, source_target_pairs={{0,1},{1,0},{2,3},{3,2},{4,5},{5,4},{6,7},{7,6},{8,9},{9,8},{10,11... | collective-permute-start | bytes 1179656 | tf_op jit(solution)/shard_map/ppermute | solution.py:324
  119.1 2.6 %output_weights.1 = bf16[1024,1024]{1,0:T(8,128)(2,1)} custom-call(s32[1]{0:T(128)} %bitcast.s_ref, bf16[256,512]{1,0:T(8,128)(2,1)S(1)} %get-tuple-element.27.att_ref.a1_ref, bf16[256,512]{1,0:T(8,128)(2,1)S(1)} %copy-done.13, bf16[256,1024]{1,0:T(8,128)(2,1)S(1)} %collective-permute-done.7.up_ref.u1_ref, ...), custom_call_target="tpu_custom_call" | custom-call | flops 1073741824 | bytes 4194304 | tf_op jit(solution)/shard_map/output_weights/pallas_call | solution.py:306
  121.7 2.1 %input_weights.2.rest_0_ = bf16[1024,1536]{1,0:T(8,128)(2,1)} custom-call(s32[1]{0:T(128)} %bitcast.s_ref, bf16[256,1024]{1,0:T(8,128)(2,1)S(1)} %copy-done.11, bf16[256,768]{1,0:T(8,128)(2,1)S(1)} %attend_back.3.p1_ref, bf16[256,1024]{1,0:T(8,128)(2,1)S(1)} %get-tuple-element.45.n2_ref, bf16[272,768]{1,0:T(8,128)(2,1)S(1)} %attend_back.2.pg_ref.p2_ref), custom_call_target="tpu_custom_call" | custom-call | flops 805306368 | bytes 5005312 | tf_op jit(solution)/shard_map/input_weights/pallas_call | solution.py:306
  123.8 2.1 %collective-permute-done.9.p1_ref = bf16[256,768]{1,0:T(8,128)(2,1)S(1)} collective-permute-done((bf16[256,768]{1,0:T(8,128)(2,1)S(1)}, bf16[256,768]{1,0:T(8,128)(2,1)S(1)}, u32[]{:S(2)}, u32[]{:S(2)}) %collective-permute-start.9) | collective-permute-done | bytes 393248 | tf_op jit(solution)/shard_map/ppermute | solution.py:324
  125.9 2.1 %input_weights.3 = bf16[1024,1536]{1,0:T(8,128)(2,1)} custom-call(s32[1]{0:T(128)} %bitcast.s_ref, bf16[256,1024]{1,0:T(8,128)(2,1)S(1)} %copy-done.11, bf16[256,768]{1,0:T(8,128)(2,1)S(1)} %collective-permute-done.9.p1_ref, bf16[256,1024]{1,0:T(8,128)(2,1)S(1)} %get-tuple-element.45.n2_ref, ...), custom_call_target="tpu_custom_call", output_to_operand_aliasing={{}: (5, {})} | custom-call | flops 805306368 | bytes 8151040 | tf_op jit(solution)/shard_map/input_weights/pallas_call | solution.py:306
  (39 shorter events, 0.1 us)
Async XLA Ops:
  0.6 1.9 %copy-start = (bf16[1,1024,1536]{2,1,0:T(8,128)(2,1)S(1)}, bf16[1,1024,1536]{2,1,0:T(8,128)(2,1)}, u32[]{:S(2)}) copy-start(bf16[1,1024,1536]{2,1,0:T(8,128)(2,1)} %param.9) | copy-start | bytes 9437188
  2.5 1.0 copy-start.7
  3.6 0.7 copy-start.14
  4.3 4.5 %copy-start.1 = (bf16[1,1024,1536]{2,1,0:T(8,128)(2,1)S(1)}, bf16[1,1024,1536]{2,1,0:T(8,128)(2,1)}, u32[]{:S(2)}) copy-start(bf16[1,1024,1536]{2,1,0:T(8,128)(2,1)} %param.9) | copy-start | bytes 9437188
  4.3 4.5 %copy-start.15 = (bf16[1,1024]{1,0:T(2,128)(2,1)S(1)}, bf16[1,1024]{1,0:T(2,128)(2,1)}, u32[]{:S(2)}) copy-start(bf16[1,1024]{1,0:T(2,128)(2,1)} %gain_ref.13) | copy-start | bytes 6148
  5.6 4.8 %copy-start.16 = (f32[8,256]{1,0:T(8,128)}, f32[8,256]{1,0:T(8,128)S(1)}, u32[]{:S(2)}) copy-start(f32[8,256]{1,0:T(8,128)S(1)} %get-tuple-element.25.refs_2_) | copy-start | bytes 24580
  5.6 13.2 %collective-permute-start = (bf16[272,768]{1,0:T(8,128)(2,1)}, bf16[272,768]{1,0:T(8,128)(2,1)}, u32[]{:S(2)}, u32[]{:S(2)}) collective-permute-start(bf16[272,768]{1,0:T(8,128)(2,1)} %get-tuple-element.24), channel_id=1, source_target_pairs={{0,1},{1,0},{2,3},{3,2},{4,5},{5,4},{6,7},{7,6},{8,9},{9,8},{10,11... | collective-permute-start | bytes 1253384 | tf_op jit(solution)/shard_map/ppermute | solution.py:324
  8.7 1.0 copy-start.8
  9.8 9.0 %copy-start.18 = (f32[256,128]{1,0:T(8,128)S(1)}, f32[256,128]{1,0:T(8,128)}, u32[]{:S(2)}) copy-start(f32[256,128]{1,0:T(8,128)} %constant.25.clone.refs_6_.refs_7_) | copy-start | bytes 393220
  9.8 9.0 %copy-start.20 = (f32[256,128]{1,0:T(8,128)S(1)}, f32[256,128]{1,0:T(8,128)}, u32[]{:S(2)}) copy-start(f32[256,128]{1,0:T(8,128)} %constant.24.clone.refs_5_.refs_6_) | copy-start | bytes 393220
  9.8 15.8 %copy-start.2 = (bf16[1,1024,1024]{2,1,0:T(8,128)(2,1)S(1)}, bf16[1,1024,1024]{2,1,0:T(8,128)(2,1)}, u32[]{:S(2)}) copy-start(bf16[1,1024,1024]{2,1,0:T(8,128)(2,1)} %param.10) | copy-start | bytes 6291460
  9.8 15.8 %copy-start.9 = (bf16[256,1024]{1,0:T(8,128)(2,1)S(1)}, bf16[256,1024]{1,0:T(8,128)(2,1)}, u32[]{:S(2)}) copy-start(bf16[256,1024]{1,0:T(8,128)(2,1)} %x_ref.5) | copy-start | bytes 1572868
  18.8 0.7 copy-start.17
  22.8 0.6 copy-start.28
  23.4 8.7 %copy-start.22 = (bf16[2048,256]{1,0:T(8,128)(2,1)}, bf16[2048,256]{1,0:T(8,128)(2,1)S(1)}, u32[]{:S(2)}) copy-start(bf16[2048,256]{1,0:T(8,128)(2,1)S(1)} %get-tuple-element.44.refs_5_) | copy-start | bytes 3145732
  23.4 9.1 %copy-start.24 = (bf16[256,512]{1,0:T(8,128)(2,1)}, bf16[256,512]{1,0:T(8,128)(2,1)S(1)}, u32[]{:S(2)}) copy-start(bf16[256,512]{1,0:T(8,128)(2,1)S(1)} %get-tuple-element.41.refs_2_) | copy-start | bytes 786436
  23.4 9.1 %copy-start.26 = (bf16[256,128]{1,0:T(8,128)(2,1)}, bf16[256,128]{1,0:T(8,128)(2,1)S(1)}, u32[]{:S(2)}) copy-start(bf16[256,128]{1,0:T(8,128)(2,1)S(1)} %get-tuple-element.42.refs_3_) | copy-start | bytes 196612
  23.5 8.7 %collective-permute-start.1 = (bf16[256,512]{1,0:T(8,128)(2,1)S(1)}, bf16[256,512]{1,0:T(8,128)(2,1)S(1)}, u32[]{:S(2)}, u32[]{:S(2)}) collective-permute-start(bf16[256,512]{1,0:T(8,128)(2,1)S(1)} %get-tuple-element.27.att_ref.a1_ref), channel_id=1, source_target_pairs={{0,1},{1,0},{2,3},{3,2},{4,5},{5,4},{6,7},{7,6},{8,9},{9,8},{10,11... | collective-permute-start | bytes 786440 | tf_op jit(solution)/shard_map/ppermute | solution.py:324
  26.0 0.8 copy-start.10
  32.1 14.6 %copy-start.12 = (bf16[256,512]{1,0:T(8,128)(2,1)}, bf16[256,512]{1,0:T(8,128)(2,1)S(1)}, u32[]{:S(2)}) copy-start(bf16[256,512]{1,0:T(8,128)(2,1)S(1)} %collective-permute-done.1.att_ref.r1_ref) | copy-start | bytes 786436
  32.6 12.7 %collective-permute-start.2 = (bf16[256,1024]{1,0:T(8,128)(2,1)S(1)}, bf16[256,1024]{1,0:T(8,128)(2,1)S(1)}, u32[]{:S(2)}, u32[]{:S(2)}) collective-permute-start(bf16[256,1024]{1,0:T(8,128)(2,1)S(1)} %output.1), channel_id=1, source_target_pairs={{0,254},{2,0},{4,2},{6,4},{8,6},{10,8},{12,10},{14,12},{16,14},{18... | collective-permute-start | bytes 1572872 | tf_op jit(solution)/shard_map/ppermute | solution.py:329
  45.3 1.4 %copy-start.4 = (bf16[256,1024]{1,0:T(8,128)(2,1)}, bf16[256,1024]{1,0:T(8,128)(2,1)S(1)}, u32[]{:S(2)}) copy-start(bf16[256,1024]{1,0:T(8,128)(2,1)S(1)} %collective-permute-done.2.x_ref) | copy-start | bytes 1572868
  46.7 9.9 %collective-permute-start.3 = (bf16[272,768]{1,0:T(8,128)(2,1)}, bf16[272,768]{1,0:T(8,128)(2,1)}, u32[]{:S(2)}, u32[]{:S(2)}) collective-permute-start(bf16[272,768]{1,0:T(8,128)(2,1)} %get-tuple-element.30), channel_id=1, source_target_pairs={{0,1},{1,0},{2,3},{3,2},{4,5},{5,4},{6,7},{7,6},{8,9},{9,8},{10,11... | collective-permute-start | bytes 1253384 | tf_op jit(solution)/shard_map/ppermute | solution.py:324
  49.3 1.0 copy-start.5
  50.3 6.2 %copy-start.19 = (f32[256,128]{1,0:T(8,128)S(1)}, f32[256,128]{1,0:T(8,128)}, u32[]{:S(2)}) copy-start(f32[256,128]{1,0:T(8,128)} %constant.25.clone.refs_6_.refs_7_) | copy-start | bytes 393220
  50.3 6.2 %copy-start.21 = (f32[256,128]{1,0:T(8,128)S(1)}, f32[256,128]{1,0:T(8,128)}, u32[]{:S(2)}) copy-start(f32[256,128]{1,0:T(8,128)} %constant.24.clone.refs_5_.refs_6_) | copy-start | bytes 393220
  50.3 12.1 %copy-start.3 = (bf16[1,1024,1024]{2,1,0:T(8,128)(2,1)S(1)}, bf16[1,1024,1024]{2,1,0:T(8,128)(2,1)}, u32[]{:S(2)}) copy-start(bf16[1,1024,1024]{2,1,0:T(8,128)(2,1)} %param.10) | copy-start | bytes 6291460
  50.3 12.1 %copy-start.6 = (bf16[256,1024]{1,0:T(8,128)(2,1)S(1)}, bf16[256,1024]{1,0:T(8,128)(2,1)}, u32[]{:S(2)}) copy-start(bf16[256,1024]{1,0:T(8,128)(2,1)} %copy-done.4) | copy-start | bytes 1572868
  59.8 9.2 %collective-permute-start.4 = (bf16[256,512]{1,0:T(8,128)(2,1)S(1)}, bf16[256,512]{1,0:T(8,128)(2,1)S(1)}, u32[]{:S(2)}, u32[]{:S(2)}) collective-permute-start(bf16[256,512]{1,0:T(8,128)(2,1)S(1)} %get-tuple-element.33.att_ref.a2_ref), channel_id=1, source_target_pairs={{0,1},{1,0},{2,3},{3,2},{4,5},{5,4},{6,7},{7,6},{8,9},{9,8},{10,11... | collective-permute-start | bytes 786440 | tf_op jit(solution)/shard_map/ppermute | solution.py:324
  69.7 9.2 %collective-permute-start.5 = (bf16[256,512]{1,0:T(8,128)(2,1)S(1)}, bf16[256,512]{1,0:T(8,128)(2,1)S(1)}, u32[]{:S(2)}, u32[]{:S(2)}) collective-permute-start(bf16[256,512]{1,0:T(8,128)(2,1)S(1)} %get-tuple-element.35), channel_id=1, source_target_pairs={{0,1},{1,0},{2,3},{3,2},{4,5},{5,4},{6,7},{7,6},{8,9},{9,8},{10,11... | collective-permute-start | bytes 786440 | tf_op jit(solution)/shard_map/ppermute | solution.py:324
  81.1 9.6 %collective-permute-start.6 = (bf16[272,768]{1,0:T(8,128)(2,1)S(1)}, bf16[272,768]{1,0:T(8,128)(2,1)S(1)}, u32[]{:S(2)}, u32[]{:S(2)}) collective-permute-start(bf16[272,768]{1,0:T(8,128)(2,1)S(1)} %attend_back.2.pg_ref.p2_ref), channel_id=1, source_target_pairs={{0,1},{1,0},{2,3},{3,2},{4,5},{5,4},{6,7},{7,6},{8,9},{9,8},{10,11... | collective-permute-start | bytes 1253384 | tf_op jit(solution)/shard_map/ppermute | solution.py:324
  91.5 23.1 %copy-start.23 = (bf16[2048,256]{1,0:T(8,128)(2,1)S(1)}, bf16[2048,256]{1,0:T(8,128)(2,1)}, u32[]{:S(2)}) copy-start(bf16[2048,256]{1,0:T(8,128)(2,1)} %copy-done.22) | copy-start | bytes 3145732
  91.5 23.1 %copy-start.25 = (bf16[256,512]{1,0:T(8,128)(2,1)S(1)}, bf16[256,512]{1,0:T(8,128)(2,1)}, u32[]{:S(2)}) copy-start(bf16[256,512]{1,0:T(8,128)(2,1)} %copy-done.24) | copy-start | bytes 786436
  91.5 23.1 %copy-start.27 = (bf16[256,128]{1,0:T(8,128)(2,1)S(1)}, bf16[256,128]{1,0:T(8,128)(2,1)}, u32[]{:S(2)}) copy-start(bf16[256,128]{1,0:T(8,128)(2,1)} %copy-done.26) | copy-start | bytes 196612
  91.5 23.1 %copy-start.29 = (bf16[256,128]{1,0:T(8,128)(2,1)S(1)}, bf16[256,128]{1,0:T(8,128)(2,1)}, u32[]{:S(2)}) copy-start(bf16[256,128]{1,0:T(8,128)(2,1)} %copy-done.28) | copy-start | bytes 196612
  91.6 14.6 %collective-permute-start.7 = (bf16[256,1024]{1,0:T(8,128)(2,1)S(1)}, bf16[256,1024]{1,0:T(8,128)(2,1)S(1)}, u32[]{:S(2)}, u32[]{:S(2)}) collective-permute-start(bf16[256,1024]{1,0:T(8,128)(2,1)S(1)} %input_back.1), channel_id=1, source_target_pairs={{0,2},{2,4},{4,6},{6,8},{8,10},{10,12},{12,14},{14,16},{16,18},{18... | collective-permute-start | bytes 1572872 | tf_op jit(solution)/shard_map/ppermute | solution.py:329
  106.7 12.4 %copy-start.13 = (bf16[256,512]{1,0:T(8,128)(2,1)S(1)}, bf16[256,512]{1,0:T(8,128)(2,1)}, u32[]{:S(2)}) copy-start(bf16[256,512]{1,0:T(8,128)(2,1)} %copy-done.12) | copy-start | bytes 786436
  106.7 8.0 %collective-permute-start.8 = (bf16[256,512]{1,0:T(8,128)(2,1)S(1)}, bf16[256,512]{1,0:T(8,128)(2,1)S(1)}, u32[]{:S(2)}, u32[]{:S(2)}) collective-permute-start(bf16[256,512]{1,0:T(8,128)(2,1)S(1)} %output_back.4), channel_id=1, source_target_pairs={{0,1},{1,0},{2,3},{3,2},{4,5},{5,4},{6,7},{7,6},{8,9},{9,8},{10,11... | collective-permute-start | bytes 786440 | tf_op jit(solution)/shard_map/ppermute | solution.py:324
  114.7 7.0 %copy-start.11 = (bf16[256,1024]{1,0:T(8,128)(2,1)S(1)}, bf16[256,1024]{1,0:T(8,128)(2,1)}, u32[]{:S(2)}) copy-start(bf16[256,1024]{1,0:T(8,128)(2,1)} %copy-done.10) | copy-start | bytes 1572868
  116.5 9.4 %collective-permute-start.9 = (bf16[256,768]{1,0:T(8,128)(2,1)S(1)}, bf16[256,768]{1,0:T(8,128)(2,1)S(1)}, u32[]{:S(2)}, u32[]{:S(2)}) collective-permute-start(bf16[256,768]{1,0:T(8,128)(2,1)S(1)} %attend_back.3.p1_ref), channel_id=1, source_target_pairs={{0,1},{1,0},{2,3},{3,2},{4,5},{5,4},{6,7},{7,6},{8,9},{9,8},{10,11... | collective-permute-start | bytes 1179656 | tf_op jit(solution)/shard_map/ppermute | solution.py:324

commit v2 on v0

v2 whole, which is shorter than its diff:
```python
from functools import partial

import numpy as np
import jax
import jax.numpy as jnp
from jax import lax
from jax.experimental import pallas as pl
from jax.experimental.pallas import tpu as pltpu
from jax.sharding import PartitionSpec as P

MODEL_WIDTH = 2048
HEAD_WIDTH = 64
EPS = 1e-05
THETA = 10000.0
F32, BF16 = jnp.float32, jnp.bfloat16

T = 256
R = 128
HALF = 1024
HEADS = 1024
KEYS = 256
JOINT = HEADS + 2 * KEYS
LOG2E = 1.4426950408889634

NN = (((1,), (0,)), ((), ()))
NT = (((1,), (1,)), ((), ()))
TN = (((0,), (0,)), ((), ()))


def dot(left, right, dims=NN):
    return lax.dot_general(left, right, dims, preferred_element_type=F32)


def tables():
    lane = np.arange(128)
    angles = np.arange(T)[:, None] * THETA ** (-2.0 * (lane % 32) / HEAD_WIDTH)[None, :]
    sign = np.where(lane % 64 < 32, -1.0, 1.0)[None, :]
    return np.cos(angles).astype(np.float32), (np.sin(angles) * sign).astype(np.float32)


def lane_index(shape):
    return lax.broadcasted_iota(jnp.int32, shape, 1)


def exchange_halves(block):
    first = lane_index(block.shape) % 64 < 32
    return jnp.where(first, pltpu.roll(block, 96, 1), pltpu.roll(block, 32, 1))


def rotate(block, cosine, sine):
    return block * cosine + exchange_halves(block) * sine


def rotate_back(block, cosine, sine):
    return block * cosine - exchange_halves(block) * sine


def wide(tile, width):
    return jnp.concatenate([tile] * (width // 128), axis=1)


def columns(index):
    return slice(128 * index, 128 * index + 128)


def project_kernel(x_ref, gain_ref, w_ref, msg_ref, own_ref, sums_ref):
    x = x_ref[...].astype(F32)
    normed = (x * gain_ref[...].astype(F32)).astype(BF16)
    own = dot(normed, w_ref[...])
    own_ref[...] = own
    msg_ref[:, :JOINT] = own.astype(BF16)
    sums = jnp.broadcast_to(jnp.sum(x * x, axis=1, keepdims=True), (R, 128))
    sums_ref[...] = sums
    high = sums.astype(BF16).astype(F32)
    lane = lane_index((R, 128))
    parts = jnp.where(lane == 0, high, jnp.where(lane == 1, sums - high, 0.0))
    msg_ref[:, JOINT:] = parts.astype(BF16)


def prepare_kernel(docs1_ref, docs2_ref, cos_in, sin_in, bias1_ref, bias2_ref, cos_ref, sin_ref):
    cos_ref[...] = cos_in[...]
    sin_ref[...] = sin_in[...]
    key = lax.broadcasted_iota(jnp.int32, (T, T), 0)
    query = lax.broadcasted_iota(jnp.int32, (T, T), 1)
    for docs_ref, bias_ref in ((docs1_ref, bias1_ref), (docs2_ref, bias2_ref)):
        of_query = jnp.broadcast_to(docs_ref[...], (T, T))
        same = jnp.transpose(of_query) == of_query
        bias_ref[...] = jnp.where((key <= query) & same, 0.0, -1e30)


def group_pair(block, half):
    low = lane_index(block.shape) < 64
    if half == 0:
        first = jnp.where(low, block, 0.0)
        return jnp.concatenate([first, pltpu.roll(first, 64, 1)], axis=0)
    second = jnp.where(low, 0.0, block)
    return jnp.concatenate([pltpu.roll(second, 64, 1), second], axis=0)


def group_pair_back(turned, half):
    part = turned[64 * half : 64 * half + 64]
    zero = jnp.zeros_like(part)
    return jnp.concatenate(
        [jnp.concatenate([part, zero], axis=1), jnp.concatenate([zero, part], axis=1)], axis=0
    )


def stack_pairs(blocks, group):
    return jnp.concatenate([blocks[2 * group], blocks[2 * group + 1]], axis=0)


def attend_kernel(stream, turn, msg_ref, own_ref, sums_ref, x_ref, w_ref, bias_ref, *rest):
    cos_ref, sin_ref = rest[:2]
    before = rest[2 : 2 + 2 * stream]
    outs = rest[2 + 2 * stream :]
    out_ref, att_ref, q_ref, k_ref, v_ref, p_ref, scale_ref = outs[:7]
    seen = R * (stream + 1)
    received = jnp.sum(msg_ref[:, JOINT:].astype(F32), axis=1, keepdims=True)
    scale = lax.rsqrt((sums_ref[...] + received) / MODEL_WIDTH + EPS)
    scale_ref[...] = scale
    cosine, sine = cos_ref[...], sin_ref[...]

    def column(index):
        cols = columns(index)
        return (own_ref[:, cols] + msg_ref[:, cols].astype(F32)) * scale

    ks = [rotate(column(8 + i), cosine, sine) for i in range(2)]
    vs = [column(10 + i) for i in range(2)]
    for i in range(2):
        k_ref[:, columns(i)] = ks[i].astype(BF16)
        v_ref[:, columns(i)] = vs[i].astype(BF16)
        if stream:
            ks[i] = jnp.concatenate([before[0][:, columns(i)].astype(F32), ks[i]], axis=0)
            vs[i] = jnp.concatenate([before[1][:, columns(i)].astype(F32), vs[i]], axis=0)
    qs = []
    for i in range(8):
        q = (rotate(column(i), cosine, sine) * (0.125 * LOG2E)).astype(BF16)
        q_ref[:, columns(i)] = q
        qs.append(q)
    bias = wide(bias_ref[...], T)
    scores = [
        dot(group_pair(ks[g // 2], g % 2).astype(BF16), stack_pairs(qs, g), NT) for g in range(4)
    ]
    turned = [jnp.transpose(v).astype(BF16) for v in vs]
    for g in range(4):
        ps = []
        for half in range(2):
            part = scores[g][seen * half : seen * half + seen] + bias
            weights = jnp.exp2(part - jnp.max(part, axis=0, keepdims=True))
            weights = weights * (1.0 / jnp.sum(weights, axis=0, keepdims=True))
            ps.append(weights.astype(BF16))
            start = (2 * g + half) * seen
            p_ref[start : start + seen, :] = ps[-1]
        out = dot(group_pair_back(turned[g // 2], g % 2), jnp.concatenate(ps, axis=0))
        out = jnp.transpose(out).astype(BF16)
        att_ref[:, columns(2 * g)] = out[:R]
        att_ref[:, columns(2 * g + 1)] = out[R:]
    out = (x_ref[...].astype(F32) + dot(att_ref[...], w_ref[...])).astype(BF16)
    out_ref[...] = out
    if turn:
        own = dot(out, w_ref[...], NT)
        outs[7][...] = own.astype(BF16)
        outs[8][...] = own


def attend_back(stream, with_sums, recv_ref, own_ref, q_ref, p_ref, cos_ref, sin_ref, kv, partial_refs, pg_ref):
    seen = R * (stream + 1)
    cosine, sine = cos_ref[...], sin_ref[...]
    ks, vs = [], []
    for i in range(2):
        cols = columns(i)
        ks.append(jnp.concatenate([r[:, cols] for r in kv[0::2]], axis=0).astype(F32))
        vs.append(jnp.concatenate([r[:, cols] for r in kv[1::2]], axis=0).astype(F32))
    grads = [own_ref[:, columns(i)] + recv_ref[:, columns(i)].astype(F32) for i in range(8)]
    low = lane_index((T, 128)) < 64
    dps = [
        dot(group_pair(vs[g // 2], g % 2).astype(BF16), stack_pairs(grads, g).astype(BF16), NT)
        for g in range(4)
    ]
    turned = [jnp.transpose(k).astype(BF16) for k in ks]
    total = jnp.zeros((R, 128), F32)
    dks, dvs = [], []
    for g in range(4):
        dss, ps = [], []
        for half in range(2):
            start = (2 * g + half) * seen
            weights = p_ref[start : start + seen, :]
            wide_weights = weights.astype(F32)
            product = wide_weights * dps[g][seen * half : seen * half + seen]
            ds = product - wide_weights * jnp.sum(product, axis=0, keepdims=True)
            dss.append(ds.astype(BF16))
            ps.append(weights)
        q = jnp.concatenate([q_ref[:, columns(2 * g)], q_ref[:, columns(2 * g + 1)]], axis=0)
        q = q.astype(F32)
        grad = stack_pairs(grads, g)
        sides = []
        for value in (q, grad):
            first = jnp.where(low, value, 0.0).astype(BF16)
            second = jnp.where(low, 0.0, value).astype(BF16)
            sides.append(jnp.concatenate([first, second], axis=0))
        dk = dot(jnp.concatenate(dss, axis=1), sides[0])
        dv = dot(jnp.concatenate(ps, axis=1), sides[1])
        dks.append(dk + pltpu.roll(dk, 64, 1))
        dvs.append(dv + pltpu.roll(dv, 64, 1))
        dq = jnp.transpose(dot(group_pair_back(turned[g // 2], g % 2), jnp.concatenate(dss, axis=0)))
        if with_sums:
            product = dq * q
            total = total + product[:R] + product[R:]
        for i in range(2):
            block = dq[R * i : R * i + R] * 0.125
            pg_ref[:, columns(2 * g + i)] = rotate_back(block, cosine, sine).astype(BF16)
    total = total * (1.0 / LOG2E)
    low = lane_index((seen, 128)) < 64
    for i in range(2):
        dk = jnp.where(low, dks[2 * i], dks[2 * i + 1]) * (1.0 / LOG2E)
        dv = jnp.where(low, dvs[2 * i], dvs[2 * i + 1])
        cols = columns(i)
        if stream:
            partial_refs[0][:, cols], partial_refs[1][:, cols] = dk[:R], dv[:R]
            dk, dv = dk[R:], dv[R:]
        else:
            dk, dv = dk + partial_refs[0][:, cols], dv + partial_refs[1][:, cols]
        if with_sums:
            total = total + dk * ks[i][-R:] + dv * vs[i][-R:]
        pg_ref[:, columns(8 + i)] = rotate_back(dk, cosine, sine).astype(BF16)
        pg_ref[:, columns(10 + i)] = dv.astype(BF16)
    return total


def attend_back_kernel(stream, with_input, *refs):
    count = 2 * (stream + 1)
    fixed, kv, rest = refs[:6], refs[6 : 6 + count], list(refs[6 + count :])
    if not stream:
        partials, rest = rest[:2], rest[2:]
    if with_input:
        (w_ref, x_ref, gain_ref, scale_ref, up_ref), rest = rest[:5], rest[5:]
    pg_ref, rest = rest[0], rest[1:]
    if stream:
        partials, rest = rest[:2], rest[2:]
    total = attend_back(stream, with_input, *fixed, kv, partials, pg_ref)
    if with_input:
        (out_ref,) = rest
        sums = jnp.sum(total, axis=1, keepdims=True) / MODEL_WIDTH
        grad = dot(pg_ref[...], w_ref[...], NT)
        scale = scale_ref[...]
        out = up_ref[...].astype(F32) + wide(scale, HALF) * (gain_ref[...].astype(F32) * grad)
        factor = wide(scale * scale * sums, HALF)
        out_ref[...] = (out - x_ref[...].astype(F32) * factor).astype(BF16)


def output_back_kernel(up_ref, w_ref, msg_ref, own_ref):
    own = dot(up_ref[...], w_ref[...], NT)
    msg_ref[...] = own.astype(BF16)
    own_ref[...] = own


def output_weight_kernel(*refs):
    att = jnp.concatenate([r[...] for r in refs[:4]], axis=0)
    up = jnp.concatenate([r[...] for r in refs[4:8]], axis=0)
    refs[8][...] = dot(att, up, TN).astype(BF16)


def input_weight_kernel(last, xa_ref, xb_ref, sa_ref, sb_ref, gain_ref, pa_ref, pb_ref, *rest):
    gain = gain_ref[...].astype(F32)
    normed = jnp.concatenate(
        [
            (x[...].astype(F32) * wide(s[...], x.shape[1]) * gain).astype(BF16)
            for x, s in ((xa_ref, sa_ref), (xb_ref, sb_ref))
        ],
        axis=0,
    )
    out = dot(normed, jnp.concatenate([pa_ref[...], pb_ref[...]], axis=0), TN)
    if last:
        out = out + rest[0][...]
    rest[-1][...] = out.astype(rest[-1].dtype)


PARAMS = pltpu.CompilerParams(vmem_limit_bytes=32 * 1024 * 1024)


def shape_of(dtype, *shape):
    return jax.ShapeDtypeStruct(shape, dtype)


def block(*shape, at=None):
    return pl.BlockSpec(shape, lambda i: at or (0,) * len(shape))


def call(kernel, args, outs, flops, name, specs=None, out_specs=None, grid=1):
    moved = sum(int(np.prod(a.shape)) * a.dtype.itemsize for a in list(args) + list(outs))
    specs = specs or {}
    return pl.pallas_call(
        kernel,
        grid=(grid,),
        in_specs=[specs.get(i) or block(*a.shape) for i, a in enumerate(args)],
        out_specs=out_specs or [block(*o.shape) for o in outs],
        out_shape=list(outs),
        compiler_params=PARAMS,
        cost_estimate=pl.CostEstimate(flops=flops, bytes_accessed=moved, transcendentals=0),
        name=name,
    )(*args)


def swap(value):
    return lax.ppermute(value, "stretch", [(0, 1), (1, 0)])


def hop(value, step):
    count = lax.axis_size("blk")
    return lax.ppermute(value, "blk", [(i, (i + step) % count) for i in range(count)])


IN_FLOPS = 2 * R * HALF * JOINT
OUT_FLOPS = 2 * R * HALF * HEADS


def after(value, *others):
    return lax.optimization_barrier((value, *others))[0]


def project(x, layer, spec=None):
    w_in, _, gain = layer
    return call(
        project_kernel, [x, gain, w_in],
        [shape_of(BF16, R, JOINT + 128), shape_of(F32, R, JOINT), shape_of(F32, R, 128)],
        IN_FLOPS, "project", specs={0: spec} if spec else None,
    )


def attend(stream, turn, x, parts, layer, bias, trig, before, spec=None):
    recv, own, sums = parts
    seen = R * (stream + 1)
    shapes = [
        shape_of(BF16, R, HALF), shape_of(BF16, R, HEADS), shape_of(BF16, R, HEADS),
        shape_of(BF16, R, KEYS), shape_of(BF16, R, KEYS), shape_of(BF16, 8 * seen, T),
        shape_of(F32, R, 128),
    ]
    if turn:
        shapes += [shape_of(BF16, R, HEADS), shape_of(F32, R, HEADS)]
    at = (stream, 0)
    specs = {
        5: block(seen, R, at=(0, stream)), 6: block(R, 128, at=at), 7: block(R, 128, at=at),
    }
    if spec:
        specs[3] = spec
    outs = call(
        partial(attend_kernel, stream, turn),
        [recv, own, sums, x, layer[1], bias, *trig, *before], shapes,
        OUT_FLOPS * (1 + turn) + 4 * 16 * R * seen * 128, "attend", specs=specs,
    )
    out, att, q, k, v, p, scale = outs[:7]
    kept = dict(x=x, att=att, q=q, kv=[k, v], p=p, scale=scale, out=out)
    if turn:
        kept["msg"], kept["own"] = outs[7:]
    return kept


def back(stream, recv, own, kept, trig, kv, partials, layer=None):
    seen = R * (stream + 1)
    args = [recv, own, kept["q"], kept["p"], *trig, *kv]
    if not stream:
        args += partials
    shapes = [shape_of(BF16, R, JOINT)]
    if stream:
        shapes += [shape_of(F32, R, KEYS)] * 2
    if layer:
        args += [layer[0], kept["x"], layer[2], kept["scale"], kept["out"]]
        shapes.append(shape_of(BF16, R, HALF))
    at = block(R, 128, at=(stream, 0))
    return call(
        partial(attend_back_kernel, stream, layer is not None), args, shapes,
        8 * 16 * R * seen * 128 + (IN_FLOPS if layer else 0), "attend_back",
        specs={4: at, 5: at},
    )


def output_back(up, layer):
    return call(
        output_back_kernel, [up, layer[1]], [shape_of(BF16, R, HEADS), shape_of(F32, R, HEADS)],
        OUT_FLOPS, "output_back",
    )


def input_weights(xs, scales, gain, pgs, acc, spec_of=None):
    parts = 4
    cut = HALF // parts
    rows = pl.BlockSpec((R, cut), lambda i: (0, i))
    out = pl.BlockSpec((cut, JOINT), lambda i: (i, 0))
    specs = {0: rows, 1: rows, 4: pl.BlockSpec((1, cut), lambda i: (0, i))}
    if spec_of:
        specs[0], specs[1] = spec_of(cut)
    args = [*xs, *scales, gain, *pgs]
    if acc is not None:
        specs[7] = out
        args.append(acc)
    return call(
        partial(input_weight_kernel, acc is not None), args,
        [shape_of(F32 if acc is None else BF16, HALF, JOINT)], 2 * IN_FLOPS, "input_weights",
        specs=specs, out_specs=[out], grid=parts,
    )[0]


def shards(activations, document_ids, joint_input_weights, output_weights, norm_gains):
    blk = lax.axis_index("blk")
    w_in, w_out, gain = layer = (joint_input_weights[0], output_weights[0], norm_gains)
    tables_in = [jnp.asarray(t) for t in tables()]

    rows = [block(R, HALF, at=(i, 0)) for i in range(2)]
    msg_a, own_a, sums_a = project(activations, layer, rows[0])
    recv_a = swap(msg_a)
    msg_b, own_b, sums_b = project(after(activations, msg_a), layer, rows[1])
    recv_b = swap(msg_b)
    ids = after(document_ids, msg_b)
    next_blk = lax.rem(blk + 1, lax.axis_size("blk"))
    docs = [
        lax.dynamic_slice_in_dim(ids, i * T, T).astype(F32)[None, :] for i in (blk, next_blk)
    ]
    bias1, bias2, *trig = call(
        prepare_kernel, [*docs, *tables_in],
        [shape_of(F32, T, T)] * 2 + [shape_of(F32, T, 128)] * 2, 4 * T * T, "prepare",
    )
    a1 = attend(0, False, activations, (recv_a, own_a, sums_a), layer, bias1, trig, [], rows[0])
    xa = hop(a1["out"], -1)
    b1 = attend(
        1, False, activations, (recv_b, own_b, sums_b), layer, bias1, trig, a1["kv"], rows[1]
    )
    xb = hop(b1["out"], -1)

    msg_a, own_a, sums_a = project(xa, layer)
    recv_a = swap(msg_a)
    msg_b, own_b, sums_b = project(after(xb, msg_a), layer)
    recv_b = swap(msg_b)
    a2 = attend(0, True, xa, (recv_a, own_a, sums_a), layer, bias2, trig, [])
    recv_a = swap(a2["msg"])
    b2 = attend(1, True, xb, (recv_b, own_b, sums_b), layer, bias2, trig, a2["kv"])
    recv_b = swap(b2["msg"])
    pgb2, dka, dva, up = back(1, recv_b, b2["own"], b2, trig, a2["kv"] + b2["kv"], None, layer)
    upb = hop(up, 1)
    pga2, up = back(0, recv_a, a2["own"], a2, trig, a2["kv"], [dka, dva], layer)
    upa = hop(up, 1)

    msg_b, own_b = output_back(upb, layer)
    recv_b = swap(msg_b)
    msg_a, own_a = output_back(after(upa, msg_b), layer)
    recv_a = swap(msg_a)
    acc = input_weights([xa, xb], [a2["scale"], b2["scale"]], gain, [pga2, pgb2], None)
    (total_out,) = call(
        output_weight_kernel,
        [k["att"] for k in (a1, b1, a2, b2)] + [upa, upb, a2["out"], b2["out"]],
        [shape_of(BF16, HEADS, HALF)], 4 * OUT_FLOPS, "output_weights",
    )
    pgb1, dka, dva = back(1, recv_b, own_b, b1, trig, a1["kv"] + b1["kv"], None)
    (pga1,) = back(0, recv_a, own_a, a1, trig, a1["kv"], [dka, dva])
    total_in = input_weights(
        [activations, activations], [a1["scale"], b1["scale"]], gain, [pga1, pgb1], acc,
        lambda cut: [pl.BlockSpec((R, cut), lambda i, r=r: (r, i)) for r in range(2)],
    )
    return (total_in[None], total_out[None])


def solution(mesh):
    placed = (
        P("blk", "stretch"),
        P(),
        P("blk", "stretch", None),
        P("blk", None, "stretch"),
        P("blk", "stretch"),
    )
    return jax.shard_map(
        shards,
        mesh=mesh,
        in_specs=placed,
        out_specs=(P("blk", "stretch", None), P("blk", None, "stretch")),
        check_vma=False,
    )
```

time: 537 us -> 102 us (0.19)
  waiting for transfers between devices: 236 us -> 30.6 us
  matrix products: 143 us -> 0 us
  other arithmetic: 62.7 us -> 0.84 us
  local copies, waits for them, and re-layouts: 47.7 us -> 7.76 us
  Pallas kernels: 0 us -> 30.8 us
  starting transfers between devices: 8.91 us -> 30.5 us
  blocking collectives: 20 us -> 0 us
  between operations: 14.2 us -> 0.81 us
    psum x4 -> x0, waiting for transfers between devices: 231 us -> none  [the longest x2 144 us: project(): lax.psum(jnp.dot(left_side, right_side, preferred_element_type=jnp.float3...]
    dot_general x67 -> x0, matrix products: 143 us -> none  [the longest x24 54.8 us: one_group(): return jnp.einsum('gts,sd->tgd', weights, group_values, precision=PRECISE)]
    pallas_call x0 -> x18, Pallas kernels: none -> 30.8 us  [call(): pl.pallas_call(kernel, grid=(grid,), in_specs=[specs.get(i) or block(*a.s...]
    ppermute x5 -> x12, waiting for transfers between devices: 4.86 us -> 30.6 us  [the longest x8 21.2 us: swap(): return lax.ppermute(value, 'stretch', [(0, 1), (1, 0)])]
    ppermute x5 -> x12, starting transfers between devices: 8.35 us -> 30.5 us  [the longest x8 17.7 us: swap(): return lax.ppermute(value, 'stretch', [(0, 1), (1, 0)])]
    psum x3 -> x0, blocking collectives: 20 us -> none  [the longest x2 12.9 us: norm_scale(): lax.psum(jnp.sum(value_rows * value_rows, axis=1, keepdims=True), 'stretch')]
    another operation x18 -> x0, local copies, waits for them, and re-layouts: 19.9 us -> none
    dynamic_update_slice x16 -> x0, other arithmetic: 17.3 us -> none  [attend(): lax.map(one_group, (jnp.moveaxis(query_rows, 1, 0), jnp.moveaxis(key_rows...]
  transfers between devices with their start and end apart: 9 -> 12, of which waited for: 5 -> 8; matrix products, arithmetic and copies ran while one was open for 31% -> 1% of each run, Pallas kernels for 0% -> 22%
where the time goes in v2:
time: 102 us; the launch traced here: 101 us
  Pallas kernels  30.8 us (30%)
  waiting for transfers between devices  30.6 us (30%)
  starting transfers between devices  30.5 us (30%)
  local copies, waits for them, and re-layouts  7.76 us (8%)
    pallas_call x18, Pallas kernels, call(): pl.pallas_call(kernel, grid=(grid,), in_specs=[specs.get(i) or block(*a.s...  30.8 us
    ppermute x8, waiting for transfers between devices, swap(): return lax.ppermute(value, 'stretch', [(0, 1), (1, 0)])  21.2 us
    ppermute x8, starting transfers between devices, swap(): return lax.ppermute(value, 'stretch', [(0, 1), (1, 0)])  17.7 us
    ppermute x4, starting transfers between devices, hop(): lax.ppermute(value, 'blk', [(i, (i + step) % count) for i in range(count)])  12.8 us
    ppermute x4, waiting for transfers between devices, hop(): lax.ppermute(value, 'blk', [(i, (i + step) % count) for i in range(count)])  9.39 us
    unnamed x30, local copies, waits for them, and re-layouts  7.76 us
  transfers between devices with their start and end apart: 12, of which 8 were waited for; matrix products, arithmetic and copies ran while one was open for 1% of the time, Pallas kernels for 22%

profile of v2, /device:TPU:2, one launch (start us, length us, event | category | flops | bytes accessed | tf_op | source)
XLA Modules:
  0.0 101.2 jit_solution(13239239047934422054)
XLA Ops:
  0.6 0.0 copy-start
  0.6 1.9 %copy-done = bf16[1,1024,1536]{2,1,0:T(8,128)(2,1)S(1)} copy-done((bf16[1,1024,1536]{2,1,0:T(8,128)(2,1)S(1)}, bf16[1,1024,1536]{2,1,0:T(8,128)(2,1)}, u32[]{:S(2)}) %copy-start) | copy-done | bytes 3145752
  2.5 0.0 copy-start.3
  2.5 1.0 %copy-done.3 = bf16[256,1024]{1,0:T(8,128)(2,1)S(1)} copy-done((bf16[256,1024]{1,0:T(8,128)(2,1)S(1)}, bf16[256,1024]{1,0:T(8,128)(2,1)}, u32[]{:S(2)}) %copy-start.3) | copy-done | bytes 524312
  3.6 0.0 copy-start.7
  3.6 0.7 copy-done.7
  4.3 0.0 copy-start.2
  4.3 1.3 %project.4 = (bf16[128,1664]{1,0:T(8,128)(2,1)}, f32[128,1536]{1,0:T(8,128)S(1)}, f32[128,128]{1,0:T(8,128)S(1)}) custom-call(bf16[256,1024]{1,0:T(8,128)(2,1)S(1)} %copy-done.3, bf16[1,1024]{1,0:T(2,128)(2,1)S(1)} %copy-done.7, bf16[1024,1536]{1,0:T(8,128)(2,1)S(1)} %bitcast.6), custom_call_target="tpu_custom_call" | custom-call | flops 402653184 | bytes 4950016 | tf_op jit(solution)/shard_map/project/pallas_call | solution.py:292
  5.6 0.6 copy-done.13
  6.2 2.1 %collective-permute-start = (bf16[128,1664]{1,0:T(8,128)(2,1)}, bf16[128,1664]{1,0:T(8,128)(2,1)}, u32[]{:S(2)}, u32[]{:S(2)}) collective-permute-start(bf16[128,1664]{1,0:T(8,128)(2,1)} %get-tuple-element.67), channel_id=1, source_target_pairs={{0,1},{1,0},{2,3},{3,2},{4,5},{5,4},{6,7},{7,6},{8,9},{9,8},{10,11... | collective-permute-start | bytes 1277960 | tf_op jit(solution)/shard_map/ppermute | solution.py:305
  8.4 1.4 %project.5 = (bf16[128,1664]{1,0:T(8,128)(2,1)}, f32[128,1536]{1,0:T(8,128)S(1)}, f32[128,128]{1,0:T(8,128)S(1)}) custom-call(bf16[256,1024]{1,0:T(8,128)(2,1)S(1)} %copy-done.3, bf16[1,1024]{1,0:T(2,128)(2,1)S(1)} %copy-done.7, bf16[1024,1536]{1,0:T(8,128)(2,1)S(1)} %bitcast.7), custom_call_target="tpu_custom_call" | custom-call | flops 402653184 | bytes 4950016 | tf_op jit(solution)/shard_map/project/pallas_call | solution.py:292
  9.7 0.0 copy-done.5
  9.7 0.6 copy-done.11
  10.3 1.4 %collective-permute-start.1 = (bf16[128,1664]{1,0:T(8,128)(2,1)}, bf16[128,1664]{1,0:T(8,128)(2,1)}, u32[]{:S(2)}, u32[]{:S(2)}) collective-permute-start(bf16[128,1664]{1,0:T(8,128)(2,1)} %get-tuple-element.71), channel_id=1, source_target_pairs={{0,1},{1,0},{2,3},{3,2},{4,5},{5,4},{6,7},{7,6},{8,9},{9,8},{10,11... | collective-permute-start | bytes 1277960 | tf_op jit(solution)/shard_map/ppermute | solution.py:305
  11.7 0.8 dynamic-slice_convert_fusion
  12.6 0.0 copy-done.9
  12.6 0.9 copy-done.10
  13.5 0.1 prepare.1
  13.6 7.1 %collective-permute-done.msg_ref = bf16[128,1664]{1,0:T(8,128)(2,1)} collective-permute-done((bf16[128,1664]{1,0:T(8,128)(2,1)}, bf16[128,1664]{1,0:T(8,128)(2,1)}, u32[]{:S(2)}, u32[]{:S(2)}) %collective-permute-start) | collective-permute-done | bytes 426016 | tf_op jit(solution)/shard_map/ppermute | solution.py:305
  20.8 0.0 copy-done.2
  20.8 0.0 copy-done.4
  20.8 1.1 %copy-done.6 = f32[128,1536]{1,0:T(8,128)S(1)} copy-done((f32[128,1536]{1,0:T(8,128)S(1)}, f32[128,1536]{1,0:T(8,128)}, u32[]{:S(2)}) %copy-start.6) | copy-done | bytes 786456
  21.9 0.8 copy-done.14
  22.7 2.4 %attend.4 = (bf16[128,1024]{1,0:T(8,128)(2,1)S(1)}, bf16[128,1024]{1,0:T(8,128)(2,1)S(1)}, bf16[128,1024]{1,0:T(8,128)(2,1)S(1)}, bf16[128,256]{1,0:T(8,128)(2,1...) custom-call(bf16[128,1664]{1,0:T(8,128)(2,1)} %collective-permute-done.msg_ref, ...), custom_call_target="tpu_custom_call" | custom-call | flops 402653184 | bytes 5931008 | tf_op jit(solution)/shard_map/attend/pallas_call | solution.py:292
  25.2 0.0 copy-start.1
  25.2 0.0 copy-start.8
  25.2 5.8 %collective-permute-start.2 = (bf16[128,1024]{1,0:T(8,128)(2,1)S(1)}, bf16[128,1024]{1,0:T(8,128)(2,1)S(1)}, u32[]{:S(2)}, u32[]{:S(2)}) collective-permute-start(bf16[128,1024]{1,0:T(8,128)(2,1)S(1)} %get-tuple-element.82), channel_id=1, source_target_pairs={{0,254},{2,0},{4,2},{6,4},{8,6},{10,8},{12,10},{14,12},{16,14},{18... | collective-permute-start | bytes 786440 | tf_op jit(solution)/shard_map/ppermute | solution.py:310
  31.0 0.0 collective-permute-done.1.msg_ref
  31.0 0.0 copy-done.12
  31.0 2.8 %attend.5 = (bf16[128,1024]{1,0:T(8,128)(2,1)S(1)}, bf16[128,1024]{1,0:T(8,128)(2,1)S(1)}, bf16[128,1024]{1,0:T(8,128)(2,1)S(1)}, bf16[128,256]{1,0:T(8,128)(2,1...) custom-call(bf16[128,1664]{1,0:T(8,128)(2,1)} %collective-permute-done.1.msg_ref, ...), custom_call_target="tpu_custom_call" | custom-call | flops 536870912 | bytes 6586368 | tf_op jit(solution)/shard_map/attend/pallas_call | solution.py:292
  33.7 4.7 %collective-permute-start.5 = (bf16[128,1024]{1,0:T(8,128)(2,1)S(1)}, bf16[128,1024]{1,0:T(8,128)(2,1)S(1)}, u32[]{:S(2)}, u32[]{:S(2)}) collective-permute-start(bf16[128,1024]{1,0:T(8,128)(2,1)S(1)} %get-tuple-element.93), channel_id=1, source_target_pairs={{0,254},{2,0},{4,2},{6,4},{8,6},{10,8},{12,10},{14,12},{16,14},{18... | collective-permute-start | bytes 786440 | tf_op jit(solution)/shard_map/ppermute | solution.py:310
  38.4 0.0 collective-permute-done.2.x_ref.refs_11_.xa_ref
  38.4 0.0 copy-done.1
  38.4 0.0 copy-done.8
  38.4 0.6 project.6
  39.1 2.5 %collective-permute-start.3 = (bf16[128,1664]{1,0:T(8,128)(2,1)S(1)}, bf16[128,1664]{1,0:T(8,128)(2,1)S(1)}, u32[]{:S(2)}, u32[]{:S(2)}) collective-permute-start(bf16[128,1664]{1,0:T(8,128)(2,1)S(1)} %get-tuple-element.83), channel_id=1, source_target_pairs={{0,1},{1,0},{2,3},{3,2},{4,5},{5,4},{6,7},{7,6},{8,9},{9,8},{10,11... | collective-permute-start | bytes 1277960 | tf_op jit(solution)/shard_map/ppermute | solution.py:305
  41.6 0.8 collective-permute-done.5.x_ref.refs_11_.xb_ref
  42.4 0.6 project.7
  43.0 2.7 %collective-permute-start.6 = (bf16[128,1664]{1,0:T(8,128)(2,1)S(1)}, bf16[128,1664]{1,0:T(8,128)(2,1)S(1)}, u32[]{:S(2)}, u32[]{:S(2)}) collective-permute-start(bf16[128,1664]{1,0:T(8,128)(2,1)S(1)} %get-tuple-element.95), channel_id=1, source_target_pairs={{0,1},{1,0},{2,3},{3,2},{4,5},{5,4},{6,7},{7,6},{8,9},{9,8},{10,11... | collective-permute-start | bytes 1277960 | tf_op jit(solution)/shard_map/ppermute | solution.py:305
  45.7 7.2 %collective-permute-done.3.msg_ref = bf16[128,1664]{1,0:T(8,128)(2,1)S(1)} collective-permute-done((bf16[128,1664]{1,0:T(8,128)(2,1)S(1)}, bf16[128,1664]{1,0:T(8,128)(2,1)S(1)}, u32[]{:S(2)}, u32[]{:S(2)}) %collective-permute-start.3) | collective-permute-done | bytes 426016 | tf_op jit(solution)/shard_map/ppermute | solution.py:305
  52.8 2.1 %attend.6 = (bf16[128,1024]{1,0:T(8,128)(2,1)S(1)}, bf16[128,1024]{1,0:T(8,128)(2,1)S(1)}, bf16[128,1024]{1,0:T(8,128)(2,1)S(1)}, bf16[128,256]{1,0:T(8,128)(2,1...) custom-call(bf16[128,1664]{1,0:T(8,128)(2,1)S(1)} %collective-permut, ...), custom_call_target="tpu_custom_call" | custom-call | flops 671088640 | bytes 6455296 | tf_op jit(solution)/shard_map/attend/pallas_call | solution.py:292
  54.9 2.5 %collective-permute-done.6.msg_ref = bf16[128,1664]{1,0:T(8,128)(2,1)S(1)} collective-permute-done((bf16[128,1664]{1,0:T(8,128)(2,1)S(1)}, bf16[128,1664]{1,0:T(8,128)(2,1)S(1)}, u32[]{:S(2)}, u32[]{:S(2)}) %collective-permute-start.6) | collective-permute-done | bytes 426016 | tf_op jit(solution)/shard_map/ppermute | solution.py:305
  57.4 2.5 %attend.7 = (bf16[128,1024]{1,0:T(8,128)(2,1)S(1)}, bf16[128,1024]{1,0:T(8,128)(2,1)S(1)}, bf16[128,1024]{1,0:T(8,128)(2,1)S(1)}, bf16[128,256]{1,0:T(8,128)(2,1...) custom-call(bf16[128,1664]{1,0:T(8,128)(2,1)S(1)} %collective-permut, ...), custom_call_target="tpu_custom_call" | custom-call | flops 805306368 | bytes 7110656 | tf_op jit(solution)/shard_map/attend/pallas_call | solution.py:292
  59.9 2.5 %collective-permute-start.7 = (bf16[128,1024]{1,0:T(8,128)(2,1)S(1)}, bf16[128,1024]{1,0:T(8,128)(2,1)S(1)}, u32[]{:S(2)}, u32[]{:S(2)}) collective-permute-start(bf16[128,1024]{1,0:T(8,128)(2,1)S(1)} %get-tuple-element.98), channel_id=1, source_target_pairs={{0,1},{1,0},{2,3},{3,2},{4,5},{5,4},{6,7},{7,6},{8,9},{9,8},{10,11... | collective-permute-start | bytes 786440 | tf_op jit(solution)/shard_map/ppermute | solution.py:305
  62.4 1.1 %collective-permute-start.4 = (bf16[128,1024]{1,0:T(8,128)(2,1)S(1)}, bf16[128,1024]{1,0:T(8,128)(2,1)S(1)}, u32[]{:S(2)}, u32[]{:S(2)}) collective-permute-start(bf16[128,1024]{1,0:T(8,128)(2,1)S(1)} %get-tuple-element.87), channel_id=1, source_target_pairs={{0,1},{1,0},{2,3},{3,2},{4,5},{5,4},{6,7},{7,6},{8,9},{9,8},{10,11... | collective-permute-start | bytes 786440 | tf_op jit(solution)/shard_map/ppermute | solution.py:305
  63.5 4.3 %collective-permute-done.7.refs_0_ = bf16[128,1024]{1,0:T(8,128)(2,1)S(1)} collective-permute-done((bf16[128,1024]{1,0:T(8,128)(2,1)S(1)}, bf16[128,1024]{1,0:T(8,128)(2,1)S(1)}, u32[]{:S(2)}, u32[]{:S(2)}) %collective-permute-start.7) | collective-permute-done | bytes 262176 | tf_op jit(solution)/shard_map/ppermute | solution.py:305
  67.8 2.6 %attend_back.4 = (bf16[128,1536]{1,0:T(8,128)(2,1)S(1)}, f32[128,256]{1,0:T(8,128)S(1)}, f32[128,256]{1,0:T(8,128)S(1)}, bf16[128,1024]{1,0:T(8,128)(2,1)S(1)}) custom-call(bf16[128,1024]{1,0:T(8,128)(2,1)S(1)} %collective-permute-done.7.refs_0_, f32[128,1024]{1,0:T(8,128)S(1)} %get-tuple-element.99.refs_1_, ...), custom_call_target="tpu_custom_call" | custom-call | flops 939524096 | bytes 7276544 | tf_op jit(solution)/shard_map/attend_back/pallas_call | solution.py:292
  70.4 0.1 collective-permute-start.9
  70.5 0.1 collective-permute-done.4.refs_0_
  70.6 2.1 %attend_back.5 = (bf16[128,1536]{1,0:T(8,128)(2,1)S(1)}, bf16[128,1024]{1,0:T(8,128)(2,1)S(1)}) custom-call(bf16[128,1024]{1,0:T(8,128)(2,1)S(1)} %collective-permute-done.4.refs_0_, f32[128,1024]{1,0:T(8,128)S(1)} %get-tuple-element.88.refs_1_, bf16[128,1024]{1,0:T(8,128)(2,1)S(1)} %get-tuple-element.89.refs_2_, ...), custom_call_target="tpu_custom_call" | custom-call | flops 671088640 | bytes 6621184 | tf_op jit(solution)/shard_map/attend_back/pallas_call | solution.py:292
  72.7 2.3 %collective-permute-start.8 = (bf16[128,1024]{1,0:T(8,128)(2,1)S(1)}, bf16[128,1024]{1,0:T(8,128)(2,1)S(1)}, u32[]{:S(2)}, u32[]{:S(2)}) collective-permute-start(bf16[128,1024]{1,0:T(8,128)(2,1)S(1)} %get-tuple-element.110), channel_id=1, source_target_pairs={{0,2},{2,4},{4,6},{6,8},{8,10},{10,12},{12,14},{14,16},{16,18},{18... | collective-permute-start | bytes 786440 | tf_op jit(solution)/shard_map/ppermute | solution.py:310
  75.0 6.8 %collective-permute-done.9.up_ref.refs_5_ = bf16[128,1024]{1,0:T(8,128)(2,1)S(1)} collective-permute-done((bf16[128,1024]{1,0:T(8,128)(2,1)S(1)}, bf16[128,1024]{1,0:T(8,128)(2,1)S(1)}, u32[]{:S(2)}, u32[]{:S(2)}) %collective-permute-start.9) | collective-permute-done | bytes 262176 | tf_op jit(solution)/shard_map/ppermute | solution.py:310
  81.8 0.8 output_back.2
  82.6 2.6 %collective-permute-start.11 = (bf16[128,1024]{1,0:T(8,128)(2,1)S(1)}, bf16[128,1024]{1,0:T(8,128)(2,1)S(1)}, u32[]{:S(2)}, u32[]{:S(2)}) collective-permute-start(bf16[128,1024]{1,0:T(8,128)(2,1)S(1)} %get-tuple-element.112), channel_id=1, source_target_pairs={{0,1},{1,0},{2,3},{3,2},{4,5},{5,4},{6,7},{7,6},{8,9},{9,8},{10,11... | collective-permute-start | bytes 786440 | tf_op jit(solution)/shard_map/ppermute | solution.py:305
  85.2 1.8 %collective-permute-done.8.up_ref.refs_4_ = bf16[128,1024]{1,0:T(8,128)(2,1)S(1)} collective-permute-done((bf16[128,1024]{1,0:T(8,128)(2,1)S(1)}, bf16[128,1024]{1,0:T(8,128)(2,1)S(1)}, u32[]{:S(2)}, u32[]{:S(2)}) %collective-permute-start.8) | collective-permute-done | bytes 262176 | tf_op jit(solution)/shard_map/ppermute | solution.py:310
  87.0 0.8 output_back.3
  87.8 2.7 %collective-permute-start.10 = (bf16[128,1024]{1,0:T(8,128)(2,1)S(1)}, bf16[128,1024]{1,0:T(8,128)(2,1)S(1)}, u32[]{:S(2)}, u32[]{:S(2)}) collective-permute-start(bf16[128,1024]{1,0:T(8,128)(2,1)S(1)} %get-tuple-element.114), channel_id=1, source_target_pairs={{0,1},{1,0},{2,3},{3,2},{4,5},{5,4},{6,7},{7,6},{8,9},{9,8},{10,11... | collective-permute-start | bytes 786440 | tf_op jit(solution)/shard_map/ppermute | solution.py:305
  90.6 1.7 %input_weights.2.rest_0_ = f32[1024,1536]{1,0:T(8,128)S(1)} custom-call(bf16[128,1024]{1,0:T(8,128)(2,1)S(1)} %collective-permute-done.2.x_ref.refs_11_.xa_ref, bf16[128,1024]{1,0:T(8,128)(2,1)S(1)} %collective-permute-done.5.x_ref.refs_11_.xb_ref, f32[128,128]{1,0:T(8,128)S(1)} %get-tuple-element.108.refs_13_.sa_ref, ...), custom_call_target="tpu_custom_call" | custom-call | flops 805306368 | bytes 7735296 | tf_op jit(solution)/shard_map/input_weights/pallas_call | solution.py:292
  92.3 2.6 %output_weights.1 = bf16[1024,1024]{1,0:T(8,128)(2,1)} custom-call(bf16[128,1024]{1,0:T(8,128)(2,1)S(1)} %get-tuple-element.128.refs_0_, bf16[128,1024]{1,0:T(8,128)(2,1)S(1)} %get-tuple-element.129.refs_1_, bf16[128,1024]{1,0:T(8,128)(2,1)S(1)} %get-tuple-element.130.refs_2_, bf16[128,1024]{1,0:T(8,128)(2,1)S(1)} %get-tuple-element.131.refs_3_, ...), custom_call_target="tpu_custom_call" | custom-call | flops 1073741824 | bytes 4194304 | tf_op jit(solution)/shard_map/output_weights/pallas_call | solution.py:292
  94.9 0.0 collective-permute-done.11.refs_0_
  94.9 1.8 %attend_back.6 = (bf16[128,1536]{1,0:T(8,128)(2,1)S(1)}, f32[128,256]{1,0:T(8,128)S(1)}, f32[128,256]{1,0:T(8,128)S(1)}) custom-call(bf16[128,1024]{1,0:T(8,128)(2,1)S(1)} %collective-permute-done.11.refs_0_, f32[128,1024]{1,0:T(8,128)S(1)} %get-tuple-element.118.refs_1_, bf16[128,1024]{1,0:T(8,128)(2,1)S(1)} %get-tuple-element.119.refs_2_, ...), custom_call_target="tpu_custom_call" | custom-call | flops 536870912 | bytes 3276800 | tf_op jit(solution)/shard_map/attend_back/pallas_call | solution.py:292
  96.7 0.0 collective-permute-done.10.refs_0_
  96.8 1.4 %attend_back.7.pa_ref = bf16[128,1536]{1,0:T(8,128)(2,1)S(1)} custom-call(bf16[128,1024]{1,0:T(8,128)(2,1)S(1)} %collective-permute-done.10.refs_0_, f32[128,1024]{1,0:T(8,128)S(1)} %get-tuple-element.115.refs_1_, bf16[128,1024]{1,0:T(8,128)(2,1)S(1)} %get-tuple-element.116.refs_2_, bf16[1024,256]{1,0:T(8,128)(2,1)S(1)} %get-tuple-element.117.refs_3_, ...), custom_call_target="tpu_custom_call" | custom-call | flops 268435456 | bytes 2621440 | tf_op jit(solution)/shard_map/attend_back/pallas_call | solution.py:292
  98.2 3.1 %input_weights.3 = bf16[1024,1536]{1,0:T(8,128)(2,1)} custom-call(bf16[256,1024]{1,0:T(8,128)(2,1)S(1)} %copy-done.4, bf16[256,1024]{1,0:T(8,128)(2,1)S(1)} %copy-done.4, f32[128,128]{1,0:T(8,128)S(1)} %get-tuple-element.76.sa_ref, f32[128,128]{1,0:T(8,128)S(1)} %get-tuple-element.81.sb_ref, bf16[1,1024]{1,0:T(2,128)(2,1)S(1)} %copy-done.8, ...), custom_call_target="tpu_custom_call" | custom-call | flops 805306368 | bytes 11405312 | tf_op jit(solution)/shard_map/input_weights/pallas_call | solution.py:292
  (9 shorter events, 0.0 us)
Async XLA Ops:
  0.6 1.9 %copy-start = (bf16[1,1024,1536]{2,1,0:T(8,128)(2,1)S(1)}, bf16[1,1024,1536]{2,1,0:T(8,128)(2,1)}, u32[]{:S(2)}) copy-start(bf16[1,1024,1536]{2,1,0:T(8,128)(2,1)} %param.9) | copy-start | bytes 9437188
  2.5 1.0 %copy-start.3 = (bf16[256,1024]{1,0:T(8,128)(2,1)S(1)}, bf16[256,1024]{1,0:T(8,128)(2,1)}, u32[]{:S(2)}) copy-start(bf16[256,1024]{1,0:T(8,128)(2,1)} %xb_ref.1) | copy-start | bytes 1572868
  3.6 0.7 copy-start.7
  4.3 8.3 %copy-start.9 = (f32[256,128]{1,0:T(8,128)S(1)}, f32[256,128]{1,0:T(8,128)}, u32[]{:S(2)}) copy-start(f32[256,128]{1,0:T(8,128)} %constant.23.clone.sin_in) | copy-start | bytes 393220
  4.3 16.5 %copy-start.2 = (bf16[1,1024,1024]{2,1,0:T(8,128)(2,1)S(1)}, bf16[1,1024,1024]{2,1,0:T(8,128)(2,1)}, u32[]{:S(2)}) copy-start(bf16[1,1024,1024]{2,1,0:T(8,128)(2,1)} %param.10) | copy-start | bytes 6291460
  4.3 16.5 %copy-start.4 = (bf16[256,1024]{1,0:T(8,128)(2,1)S(1)}, bf16[256,1024]{1,0:T(8,128)(2,1)}, u32[]{:S(2)}) copy-start(bf16[256,1024]{1,0:T(8,128)(2,1)} %xb_ref.1) | copy-start | bytes 1572868
  5.6 0.6 copy-start.13
  6.2 3.5 %copy-start.5 = (f32[128,1536]{1,0:T(8,128)}, f32[128,1536]{1,0:T(8,128)S(1)}, u32[]{:S(2)}) copy-start(f32[128,1536]{1,0:T(8,128)S(1)} %get-tuple-element.68.own_ref) | copy-start | bytes 2359300
  6.2 14.5 %collective-permute-start = (bf16[128,1664]{1,0:T(8,128)(2,1)}, bf16[128,1664]{1,0:T(8,128)(2,1)}, u32[]{:S(2)}, u32[]{:S(2)}) collective-permute-start(bf16[128,1664]{1,0:T(8,128)(2,1)} %get-tuple-element.67), channel_id=1, source_target_pairs={{0,1},{1,0},{2,3},{3,2},{4,5},{5,4},{6,7},{7,6},{8,9},{9,8},{10,11... | collective-permute-start | bytes 1277960 | tf_op jit(solution)/shard_map/ppermute | solution.py:305
  9.7 0.6 copy-start.11
  10.3 20.6 %collective-permute-start.1 = (bf16[128,1664]{1,0:T(8,128)(2,1)}, bf16[128,1664]{1,0:T(8,128)(2,1)}, u32[]{:S(2)}, u32[]{:S(2)}) collective-permute-start(bf16[128,1664]{1,0:T(8,128)(2,1)} %get-tuple-element.71), channel_id=1, source_target_pairs={{0,1},{1,0},{2,3},{3,2},{4,5},{5,4},{6,7},{7,6},{8,9},{9,8},{10,11... | collective-permute-start | bytes 1277960 | tf_op jit(solution)/shard_map/ppermute | solution.py:305
  12.6 0.9 copy-start.10
  13.5 17.5 %copy-start.12 = (f32[128,128]{1,0:T(8,128)S(1)}, f32[128,128]{1,0:T(8,128)}, u32[]{:S(2)}) copy-start(f32[128,128]{1,0:T(8,128)} %copy-done.11) | copy-start | bytes 196612
  20.8 1.1 %copy-start.6 = (f32[128,1536]{1,0:T(8,128)S(1)}, f32[128,1536]{1,0:T(8,128)}, u32[]{:S(2)}) copy-start(f32[128,1536]{1,0:T(8,128)} %copy-done.5) | copy-start | bytes 2359300
  21.9 0.8 copy-start.14
  25.2 13.3 %copy-start.1 = (bf16[1,1024,1536]{2,1,0:T(8,128)(2,1)S(1)}, bf16[1,1024,1536]{2,1,0:T(8,128)(2,1)}, u32[]{:S(2)}) copy-start(bf16[1,1024,1536]{2,1,0:T(8,128)(2,1)} %param.9) | copy-start | bytes 9437188
  25.2 13.3 %copy-start.8 = (bf16[1,1024]{1,0:T(2,128)(2,1)S(1)}, bf16[1,1024]{1,0:T(2,128)(2,1)}, u32[]{:S(2)}) copy-start(bf16[1,1024]{1,0:T(2,128)(2,1)} %gain_ref.11) | copy-start | bytes 6148
  25.2 13.3 %collective-permute-start.2 = (bf16[128,1024]{1,0:T(8,128)(2,1)S(1)}, bf16[128,1024]{1,0:T(8,128)(2,1)S(1)}, u32[]{:S(2)}, u32[]{:S(2)}) collective-permute-start(bf16[128,1024]{1,0:T(8,128)(2,1)S(1)} %get-tuple-element.82), channel_id=1, source_target_pairs={{0,254},{2,0},{4,2},{6,4},{8,6},{10,8},{12,10},{14,12},{16,14},{18... | collective-permute-start | bytes 786440 | tf_op jit(solution)/shard_map/ppermute | solution.py:310
  33.7 8.6 %collective-permute-start.5 = (bf16[128,1024]{1,0:T(8,128)(2,1)S(1)}, bf16[128,1024]{1,0:T(8,128)(2,1)S(1)}, u32[]{:S(2)}, u32[]{:S(2)}) collective-permute-start(bf16[128,1024]{1,0:T(8,128)(2,1)S(1)} %get-tuple-element.93), channel_id=1, source_target_pairs={{0,254},{2,0},{4,2},{6,4},{8,6},{10,8},{12,10},{14,12},{16,14},{18... | collective-permute-start | bytes 786440 | tf_op jit(solution)/shard_map/ppermute | solution.py:310
  39.1 13.8 %collective-permute-start.3 = (bf16[128,1664]{1,0:T(8,128)(2,1)S(1)}, bf16[128,1664]{1,0:T(8,128)(2,1)S(1)}, u32[]{:S(2)}, u32[]{:S(2)}) collective-permute-start(bf16[128,1664]{1,0:T(8,128)(2,1)S(1)} %get-tuple-element.83), channel_id=1, source_target_pairs={{0,1},{1,0},{2,3},{3,2},{4,5},{5,4},{6,7},{7,6},{8,9},{9,8},{10,11... | collective-permute-start | bytes 1277960 | tf_op jit(solution)/shard_map/ppermute | solution.py:305
  43.0 14.4 %collective-permute-start.6 = (bf16[128,1664]{1,0:T(8,128)(2,1)S(1)}, bf16[128,1664]{1,0:T(8,128)(2,1)S(1)}, u32[]{:S(2)}, u32[]{:S(2)}) collective-permute-start(bf16[128,1664]{1,0:T(8,128)(2,1)S(1)} %get-tuple-element.95), channel_id=1, source_target_pairs={{0,1},{1,0},{2,3},{3,2},{4,5},{5,4},{6,7},{7,6},{8,9},{9,8},{10,11... | collective-permute-start | bytes 1277960 | tf_op jit(solution)/shard_map/ppermute | solution.py:305
  59.9 8.0 %collective-permute-start.7 = (bf16[128,1024]{1,0:T(8,128)(2,1)S(1)}, bf16[128,1024]{1,0:T(8,128)(2,1)S(1)}, u32[]{:S(2)}, u32[]{:S(2)}) collective-permute-start(bf16[128,1024]{1,0:T(8,128)(2,1)S(1)} %get-tuple-element.98), channel_id=1, source_target_pairs={{0,1},{1,0},{2,3},{3,2},{4,5},{5,4},{6,7},{7,6},{8,9},{9,8},{10,11... | collective-permute-start | bytes 786440 | tf_op jit(solution)/shard_map/ppermute | solution.py:305
  62.4 8.3 %collective-permute-start.4 = (bf16[128,1024]{1,0:T(8,128)(2,1)S(1)}, bf16[128,1024]{1,0:T(8,128)(2,1)S(1)}, u32[]{:S(2)}, u32[]{:S(2)}) collective-permute-start(bf16[128,1024]{1,0:T(8,128)(2,1)S(1)} %get-tuple-element.87), channel_id=1, source_target_pairs={{0,1},{1,0},{2,3},{3,2},{4,5},{5,4},{6,7},{7,6},{8,9},{9,8},{10,11... | collective-permute-start | bytes 786440 | tf_op jit(solution)/shard_map/ppermute | solution.py:305
  70.4 11.3 %collective-permute-start.9 = (bf16[128,1024]{1,0:T(8,128)(2,1)S(1)}, bf16[128,1024]{1,0:T(8,128)(2,1)S(1)}, u32[]{:S(2)}, u32[]{:S(2)}) collective-permute-start(bf16[128,1024]{1,0:T(8,128)(2,1)S(1)} %get-tuple-element.111), channel_id=1, source_target_pairs={{0,2},{2,4},{4,6},{6,8},{8,10},{10,12},{12,14},{14,16},{16,18},{18... | collective-permute-start | bytes 786440 | tf_op jit(solution)/shard_map/ppermute | solution.py:310
  72.7 14.3 %collective-permute-start.8 = (bf16[128,1024]{1,0:T(8,128)(2,1)S(1)}, bf16[128,1024]{1,0:T(8,128)(2,1)S(1)}, u32[]{:S(2)}, u32[]{:S(2)}) collective-permute-start(bf16[128,1024]{1,0:T(8,128)(2,1)S(1)} %get-tuple-element.110), channel_id=1, source_target_pairs={{0,2},{2,4},{4,6},{6,8},{8,10},{10,12},{12,14},{14,16},{16,18},{18... | collective-permute-start | bytes 786440 | tf_op jit(solution)/shard_map/ppermute | solution.py:310
  82.6 12.3 %collective-permute-start.11 = (bf16[128,1024]{1,0:T(8,128)(2,1)S(1)}, bf16[128,1024]{1,0:T(8,128)(2,1)S(1)}, u32[]{:S(2)}, u32[]{:S(2)}) collective-permute-start(bf16[128,1024]{1,0:T(8,128)(2,1)S(1)} %get-tuple-element.112), channel_id=1, source_target_pairs={{0,1},{1,0},{2,3},{3,2},{4,5},{5,4},{6,7},{7,6},{8,9},{9,8},{10,11... | collective-permute-start | bytes 786440 | tf_op jit(solution)/shard_map/ppermute | solution.py:305
  87.8 8.9 %collective-permute-start.10 = (bf16[128,1024]{1,0:T(8,128)(2,1)S(1)}, bf16[128,1024]{1,0:T(8,128)(2,1)S(1)}, u32[]{:S(2)}, u32[]{:S(2)}) collective-permute-start(bf16[128,1024]{1,0:T(8,128)(2,1)S(1)} %get-tuple-element.114), channel_id=1, source_target_pairs={{0,1},{1,0},{2,3},{3,2},{4,5},{5,4},{6,7},{7,6},{8,9},{9,8},{10,11... | collective-permute-start | bytes 786440 | tf_op jit(solution)/shard_map/ppermute | solution.py:305

commit v3 on v2

--- a/solution.py
+++ b/solution.py
@@ -63,18 +63,67 @@
     return slice(128 * index, 128 * index + 128)
 
 
-def project_kernel(x_ref, gain_ref, w_ref, msg_ref, own_ref, sums_ref):
+def project_first_kernel(x_in, gain_ref, w_in, *rest):
+    outs, (x_ref, w_ref, held, x_sem, w_sems) = rest[:2], rest[2:]
+    pieces = w_sems.shape[0]
+    size = HALF // pieces
+    copies = [pltpu.make_async_copy(x_in, x_ref, x_sem)]
+    for i in range(pieces):
+        rows = pl.ds(i * size, size)
+        copies.append(pltpu.make_async_copy(w_in.at[rows], w_ref.at[rows], w_sems.at[i]))
+    for copy in copies:
+        copy.start()
+    copies[0].wait()
     x = x_ref[...].astype(F32)
     normed = (x * gain_ref[...].astype(F32)).astype(BF16)
-    own = dot(normed, w_ref[...])
-    own_ref[...] = own
-    msg_ref[:, :JOINT] = own.astype(BF16)
-    sums = jnp.broadcast_to(jnp.sum(x * x, axis=1, keepdims=True), (R, 128))
-    sums_ref[...] = sums
+    for stream in range(2):
+        put_sums(x[R * stream : R * stream + R], outs[stream])
+    for i in range(pieces):
+        copies[1 + i].wait()
+        part = dot(normed[:, i * size : i * size + size], w_ref[i * size : i * size + size, :])
+        if i:
+            part = held[...] + part
+        if i < pieces - 1:
+            held[...] = part
+    for stream in range(2):
+        outs[stream][:, :JOINT] = part[R * stream : R * stream + R].astype(BF16)
+
+
+def project_own_kernel(x_ref, gain_ref, w_ref, w_out_ref, *rest):
+    outs, w_t_ref, w_out_t_ref = rest[:4], rest[4], rest[5]
+    x = x_ref[...].astype(F32)
+    own = dot((x * gain_ref[...].astype(F32)).astype(BF16), w_ref[...])
+    for stream in range(2):
+        rows = slice(R * stream, R * stream + R)
+        outs[2 * stream][...] = own[rows]
+        outs[2 * stream + 1][...] = token_sums(x[rows])
+    w_t_ref[...] = jnp.transpose(w_ref[...])
+    w_out_t_ref[...] = jnp.transpose(w_out_ref[...])
+
+
+def project_kernel(x_ref, gain_ref, w_ref, *outs):
+    x = x_ref[...].astype(F32)
+    normed = (x * gain_ref[...].astype(F32)).astype(BF16)
+    put_projection(x, dot(normed, w_ref[...]), *outs)
+
+
+def token_sums(x):
+    return jnp.broadcast_to(jnp.sum(x * x, axis=1, keepdims=True), (R, 128))
+
+
+def put_sums(x, msg_ref):
+    sums = token_sums(x)
     high = sums.astype(BF16).astype(F32)
     lane = lane_index((R, 128))
     parts = jnp.where(lane == 0, high, jnp.where(lane == 1, sums - high, 0.0))
     msg_ref[:, JOINT:] = parts.astype(BF16)
+    return sums
+
+
+def put_projection(x, own, msg_ref, own_ref, sums_ref):
+    own_ref[...] = own
+    msg_ref[:, :JOINT] = own.astype(BF16)
+    sums_ref[...] = put_sums(x, msg_ref)
 
 
 def prepare_kernel(docs1_ref, docs2_ref, cos_in, sin_in, bias1_ref, bias2_ref, cos_ref, sin_ref):
@@ -109,16 +158,19 @@
     return jnp.concatenate([blocks[2 * group], blocks[2 * group + 1]], axis=0)
 
 
-def attend_kernel(stream, turn, msg_ref, own_ref, sums_ref, x_ref, w_ref, bias_ref, *rest):
+def attend_kernel(
+    stream, turn, msg_ref, own_ref, sums_ref, x_ref, w_ref, w_t_ref, bias_ref, *rest
+):
     cos_ref, sin_ref = rest[:2]
     before = rest[2 : 2 + 2 * stream]
     outs = rest[2 + 2 * stream :]
     out_ref, att_ref, q_ref, k_ref, v_ref, p_ref, scale_ref = outs[:7]
     seen = R * (stream + 1)
+    rows = slice(seen - R, seen)
     received = jnp.sum(msg_ref[:, JOINT:].astype(F32), axis=1, keepdims=True)
     scale = lax.rsqrt((sums_ref[...] + received) / MODEL_WIDTH + EPS)
     scale_ref[...] = scale
-    cosine, sine = cos_ref[...], sin_ref[...]
+    cosine, sine = cos_ref[rows], sin_ref[rows]
 
     def column(index):
         cols = columns(index)
@@ -137,7 +189,7 @@
         q = (rotate(column(i), cosine, sine) * (0.125 * LOG2E)).astype(BF16)
         q_ref[:, columns(i)] = q
         qs.append(q)
-    bias = wide(bias_ref[...], T)
+    bias = wide(bias_ref[:seen, rows], T)
     scores = [
         dot(group_pair(ks[g // 2], g % 2).astype(BF16), stack_pairs(qs, g), NT) for g in range(4)
     ]
@@ -155,17 +207,18 @@
         out = jnp.transpose(out).astype(BF16)
         att_ref[:, columns(2 * g)] = out[:R]
         att_ref[:, columns(2 * g + 1)] = out[R:]
-    out = (x_ref[...].astype(F32) + dot(att_ref[...], w_ref[...])).astype(BF16)
+    x = x_ref[rows] if x_ref.shape[0] == T else x_ref[...]
+    out = (x.astype(F32) + dot(att_ref[...], w_ref[...])).astype(BF16)
     out_ref[...] = out
     if turn:
-        own = dot(out, w_ref[...], NT)
+        own = dot(out, w_t_ref[...])
         outs[7][...] = own.astype(BF16)
         outs[8][...] = own
 
 
 def attend_back(stream, with_sums, recv_ref, own_ref, q_ref, p_ref, cos_ref, sin_ref, kv, partial_refs, pg_ref):
     seen = R * (stream + 1)
-    cosine, sine = cos_ref[...], sin_ref[...]
+    cosine, sine = cos_ref[seen - R : seen], sin_ref[seen - R : seen]
     ks, vs = [], []
     for i in range(2):
         cols = columns(i)
@@ -233,7 +286,7 @@
     if not stream:
         partials, rest = rest[:2], rest[2:]
     if with_input:
-        (w_ref, x_ref, gain_ref, scale_ref, up_ref), rest = rest[:5], rest[5:]
+        (w_t_ref, x_ref, gain_ref, scale_ref, up_ref), rest = rest[:5], rest[5:]
     pg_ref, rest = rest[0], rest[1:]
     if stream:
         partials, rest = rest[:2], rest[2:]
@@ -241,15 +294,15 @@
     if with_input:
         (out_ref,) = rest
         sums = jnp.sum(total, axis=1, keepdims=True) / MODEL_WIDTH
-        grad = dot(pg_ref[...], w_ref[...], NT)
+        grad = dot(pg_ref[...], w_t_ref[...])
         scale = scale_ref[...]
         out = up_ref[...].astype(F32) + wide(scale, HALF) * (gain_ref[...].astype(F32) * grad)
         factor = wide(scale * scale * sums, HALF)
         out_ref[...] = (out - x_ref[...].astype(F32) * factor).astype(BF16)
 
 
-def output_back_kernel(up_ref, w_ref, msg_ref, own_ref):
-    own = dot(up_ref[...], w_ref[...], NT)
+def output_back_kernel(up_ref, w_t_ref, msg_ref, own_ref):
+    own = dot(up_ref[...], w_t_ref[...])
     msg_ref[...] = own.astype(BF16)
     own_ref[...] = own
 
@@ -260,43 +313,61 @@
     refs[8][...] = dot(att, up, TN).astype(BF16)
 
 
-def input_weight_kernel(last, xa_ref, xb_ref, sa_ref, sb_ref, gain_ref, pa_ref, pb_ref, *rest):
-    gain = gain_ref[...].astype(F32)
-    normed = jnp.concatenate(
-        [
-            (x[...].astype(F32) * wide(s[...], x.shape[1]) * gain).astype(BF16)
-            for x, s in ((xa_ref, sa_ref), (xb_ref, sb_ref))
-        ],
-        axis=0,
-    )
-    out = dot(normed, jnp.concatenate([pa_ref[...], pb_ref[...]], axis=0), TN)
-    if last:
-        out = out + rest[0][...]
-    rest[-1][...] = out.astype(rest[-1].dtype)
-
-
-PARAMS = pltpu.CompilerParams(vmem_limit_bytes=32 * 1024 * 1024)
+def gained(x, scale_ref, gain_ref):
+    return (x.astype(F32) * wide(scale_ref[...], HALF) * gain_ref[...].astype(F32)).astype(BF16)
+
+
+def early_weight_kernel(
+    x1_ref, x2a_ref, x2b_ref, s1a_ref, s1b_ref, s2a_ref, s2b_ref, gain_ref, pa_ref, pb_ref,
+    acc_ref, turned_ref,
+):
+    second = [gained(x2a_ref[...], s2a_ref, gain_ref), gained(x2b_ref[...], s2b_ref, gain_ref)]
+    pgs = jnp.concatenate([pa_ref[...], pb_ref[...]], axis=0)
+    acc_ref[...] = dot(jnp.concatenate(second, axis=0), pgs, TN)
+    for i, scale_ref in enumerate((s1a_ref, s1b_ref)):
+        first = gained(x1_ref[R * i : R * i + R], scale_ref, gain_ref)
+        turned_ref[:, columns(i)] = jnp.transpose(first)
+
+
+def last_weight_kernel(acc_ref, turned_ref, pa_ref, pb_ref, out_ref, held, sems):
+    pgs = jnp.concatenate([pa_ref[...], pb_ref[...]], axis=0)
+    pieces = sems.shape[0]
+    size = HALF // pieces
+    copies = []
+    for i in range(pieces):
+        rows = slice(i * size, i * size + size)
+        held[rows] = (acc_ref[rows] + dot(turned_ref[rows], pgs)).astype(BF16)
+        place = pl.ds(i * size, size)
+        copies.append(pltpu.make_async_copy(held.at[place], out_ref.at[place], sems.at[i]))
+        copies[-1].start()
+    for copy in copies:
+        copy.wait()
+
+
+MIB = 1024 * 1024
+PARAMS = pltpu.CompilerParams(vmem_limit_bytes=20 * MIB)
+FIRST = pltpu.CompilerParams(vmem_limit_bytes=62 * MIB + MIB // 8)
 
 
 def shape_of(dtype, *shape):
     return jax.ShapeDtypeStruct(shape, dtype)
 
 
-def block(*shape, at=None):
-    return pl.BlockSpec(shape, lambda i: at or (0,) * len(shape))
-
-
-def call(kernel, args, outs, flops, name, specs=None, out_specs=None, grid=1):
-    moved = sum(int(np.prod(a.shape)) * a.dtype.itemsize for a in list(args) + list(outs))
+def block(*shape):
+    return pl.BlockSpec(shape, lambda i: (0,) * len(shape))
+
+
+def call(kernel, args, outs, name, specs=None, out_specs=None, scratch=(), params=PARAMS, flops=1):
     specs = specs or {}
     return pl.pallas_call(
         kernel,
-        grid=(grid,),
+        grid=(1,),
         in_specs=[specs.get(i) or block(*a.shape) for i, a in enumerate(args)],
         out_specs=out_specs or [block(*o.shape) for o in outs],
         out_shape=list(outs),
-        compiler_params=PARAMS,
-        cost_estimate=pl.CostEstimate(flops=flops, bytes_accessed=moved, transcendentals=0),
+        scratch_shapes=list(scratch),
+        compiler_params=params,
+        cost_estimate=pl.CostEstimate(flops=flops, bytes_accessed=1, transcendentals=0),
         name=name,
     )(*args)
 
@@ -310,24 +381,31 @@
     return lax.ppermute(value, "blk", [(i, (i + step) % count) for i in range(count)])
 
 
-IN_FLOPS = 2 * R * HALF * JOINT
-OUT_FLOPS = 2 * R * HALF * HEADS
-
-
 def after(value, *others):
     return lax.optimization_barrier((value, *others))[0]
 
 
-def project(x, layer, spec=None):
-    w_in, _, gain = layer
+PARTS = [shape_of(BF16, R, JOINT + 128), shape_of(F32, R, JOINT), shape_of(F32, R, 128)]
+IN_HBM = pl.BlockSpec(memory_space=pltpu.HBM)
+
+
+def project_first(x, w_in, gain):
     return call(
-        project_kernel, [x, gain, w_in],
-        [shape_of(BF16, R, JOINT + 128), shape_of(F32, R, JOINT), shape_of(F32, R, 128)],
-        IN_FLOPS, "project", specs={0: spec} if spec else None,
-    )
-
-
-def attend(stream, turn, x, parts, layer, bias, trig, before, spec=None):
+        project_first_kernel, [x, gain, w_in], PARTS[:1] * 2, "project_first", params=FIRST,
+        specs={0: IN_HBM, 2: IN_HBM},
+        scratch=[
+            pltpu.VMEM((T, HALF), BF16), pltpu.VMEM((HALF, JOINT), BF16),
+            pltpu.VMEM((T, JOINT), F32), pltpu.SemaphoreType.DMA, pltpu.SemaphoreType.DMA((2,)),
+        ],
+    )
+
+
+def project(x, layer):
+    w_in, _, gain = layer[:3]
+    return call(project_kernel, [x, gain, w_in], PARTS, "project")
+
+
+def attend(stream, turn, x, parts, layer, bias, trig, before):
     recv, own, sums = parts
     seen = R * (stream + 1)
     shapes = [
@@ -337,16 +415,10 @@
     ]
     if turn:
         shapes += [shape_of(BF16, R, HEADS), shape_of(F32, R, HEADS)]
-    at = (stream, 0)
-    specs = {
-        5: block(seen, R, at=(0, stream)), 6: block(R, 128, at=at), 7: block(R, 128, at=at),
-    }
-    if spec:
-        specs[3] = spec
     outs = call(
         partial(attend_kernel, stream, turn),
-        [recv, own, sums, x, layer[1], bias, *trig, *before], shapes,
-        OUT_FLOPS * (1 + turn) + 4 * 16 * R * seen * 128, "attend", specs=specs,
+        [recv, own, sums, x, layer[1], layer[4], bias, *trig, *before], shapes, "attend",
+        flops=10**10 if turn and not stream else 1,
     )
     out, att, q, k, v, p, scale = outs[:7]
     kept = dict(x=x, att=att, q=q, kv=[k, v], p=p, scale=scale, out=out)
@@ -356,7 +428,6 @@
 
 
 def back(stream, recv, own, kept, trig, kv, partials, layer=None):
-    seen = R * (stream + 1)
     args = [recv, own, kept["q"], kept["p"], *trig, *kv]
     if not stream:
         args += partials
@@ -364,76 +435,59 @@
     if stream:
         shapes += [shape_of(F32, R, KEYS)] * 2
     if layer:
-        args += [layer[0], kept["x"], layer[2], kept["scale"], kept["out"]]
+        args += [layer[3], kept["x"], layer[2], kept["scale"], kept["out"]]
         shapes.append(shape_of(BF16, R, HALF))
-    at = block(R, 128, at=(stream, 0))
     return call(
-        partial(attend_back_kernel, stream, layer is not None), args, shapes,
-        8 * 16 * R * seen * 128 + (IN_FLOPS if layer else 0), "attend_back",
-        specs={4: at, 5: at},
+        partial(attend_back_kernel, stream, layer is not None), args, shapes, "attend_back"
     )
 
 
 def output_back(up, layer):
     return call(
-        output_back_kernel, [up, layer[1]], [shape_of(BF16, R, HEADS), shape_of(F32, R, HEADS)],
-        OUT_FLOPS, "output_back",
-    )
-
-
-def input_weights(xs, scales, gain, pgs, acc, spec_of=None):
-    parts = 4
-    cut = HALF // parts
-    rows = pl.BlockSpec((R, cut), lambda i: (0, i))
-    out = pl.BlockSpec((cut, JOINT), lambda i: (i, 0))
-    specs = {0: rows, 1: rows, 4: pl.BlockSpec((1, cut), lambda i: (0, i))}
-    if spec_of:
-        specs[0], specs[1] = spec_of(cut)
-    args = [*xs, *scales, gain, *pgs]
-    if acc is not None:
-        specs[7] = out
-        args.append(acc)
-    return call(
-        partial(input_weight_kernel, acc is not None), args,
-        [shape_of(F32 if acc is None else BF16, HALF, JOINT)], 2 * IN_FLOPS, "input_weights",
-        specs=specs, out_specs=[out], grid=parts,
-    )[0]
+        output_back_kernel, [up, layer[4]], [shape_of(BF16, R, HEADS), shape_of(F32, R, HEADS)],
+        "output_back",
+    )
 
 
 def shards(activations, document_ids, joint_input_weights, output_weights, norm_gains):
     blk = lax.axis_index("blk")
-    w_in, w_out, gain = layer = (joint_input_weights[0], output_weights[0], norm_gains)
+    w_in, w_out, gain = joint_input_weights[0], output_weights[0], norm_gains
     tables_in = [jnp.asarray(t) for t in tables()]
 
-    rows = [block(R, HALF, at=(i, 0)) for i in range(2)]
-    msg_a, own_a, sums_a = project(activations, layer, rows[0])
+    x1 = activations
+    msg_a, msg_b = project_first(x1, w_in, gain)
     recv_a = swap(msg_a)
-    msg_b, own_b, sums_b = project(after(activations, msg_a), layer, rows[1])
     recv_b = swap(msg_b)
-    ids = after(document_ids, msg_b)
+    ids, x1, w_in, w_out, _ = lax.optimization_barrier(
+        (document_ids, x1, w_in, w_out, msg_b)
+    )
     next_blk = lax.rem(blk + 1, lax.axis_size("blk"))
     docs = [
         lax.dynamic_slice_in_dim(ids, i * T, T).astype(F32)[None, :] for i in (blk, next_blk)
     ]
     bias1, bias2, *trig = call(
         prepare_kernel, [*docs, *tables_in],
-        [shape_of(F32, T, T)] * 2 + [shape_of(F32, T, 128)] * 2, 4 * T * T, "prepare",
-    )
-    a1 = attend(0, False, activations, (recv_a, own_a, sums_a), layer, bias1, trig, [], rows[0])
+        [shape_of(F32, T, T)] * 2 + [shape_of(F32, T, 128)] * 2, "prepare",
+    )
+    x1 = after(x1, bias1)
+    own_a, sums_a, own_b, sums_b, w_in_t, w_out_t = call(
+        project_own_kernel, [x1, gain, w_in, w_out],
+        PARTS[1:] * 2 + [shape_of(BF16, JOINT, HALF), shape_of(BF16, HALF, HEADS)], "project_own",
+    )
+    layer = (w_in, w_out, gain, w_in_t, w_out_t)
+    a1 = attend(0, False, x1, (recv_a, own_a, sums_a), layer, bias1, trig, [])
     xa = hop(a1["out"], -1)
-    b1 = attend(
-        1, False, activations, (recv_b, own_b, sums_b), layer, bias1, trig, a1["kv"], rows[1]
-    )
-    xb = hop(b1["out"], -1)
-
     msg_a, own_a, sums_a = project(xa, layer)
     recv_a = swap(msg_a)
+    recv_b = after(recv_b, msg_a)
+    b1 = attend(1, False, x1, (recv_b, own_b, sums_b), layer, bias1, trig, a1["kv"])
+    xb = hop(b1["out"], -1)
     msg_b, own_b, sums_b = project(after(xb, msg_a), layer)
     recv_b = swap(msg_b)
     a2 = attend(0, True, xa, (recv_a, own_a, sums_a), layer, bias2, trig, [])
     recv_a = swap(a2["msg"])
     b2 = attend(1, True, xb, (recv_b, own_b, sums_b), layer, bias2, trig, a2["kv"])
-    recv_b = swap(b2["msg"])
+    recv_b = after(swap(b2["msg"]), recv_a)
     pgb2, dka, dva, up = back(1, recv_b, b2["own"], b2, trig, a2["kv"] + b2["kv"], None, layer)
     upb = hop(up, 1)
     pga2, up = back(0, recv_a, a2["own"], a2, trig, a2["kv"], [dka, dva], layer)
@@ -443,17 +497,22 @@
     recv_b = swap(msg_b)
     msg_a, own_a = output_back(after(upa, msg_b), layer)
     recv_a = swap(msg_a)
-    acc = input_weights([xa, xb], [a2["scale"], b2["scale"]], gain, [pga2, pgb2], None)
+    acc, turned = call(
+        early_weight_kernel,
+        [x1, xa, xb, a1["scale"], b1["scale"], a2["scale"], b2["scale"], gain, pga2, pgb2],
+        [shape_of(F32, HALF, JOINT), shape_of(BF16, HALF, T)], "early_weights",
+    )
     (total_out,) = call(
         output_weight_kernel,
         [k["att"] for k in (a1, b1, a2, b2)] + [upa, upb, a2["out"], b2["out"]],
-        [shape_of(BF16, HEADS, HALF)], 4 * OUT_FLOPS, "output_weights",
+        [shape_of(BF16, HEADS, HALF)], "output_weights",
     )
     pgb1, dka, dva = back(1, recv_b, own_b, b1, trig, a1["kv"] + b1["kv"], None)
     (pga1,) = back(0, recv_a, own_a, a1, trig, a1["kv"], [dka, dva])
-    total_in = input_weights(
-        [activations, activations], [a1["scale"], b1["scale"]], gain, [pga1, pgb1], acc,
-        lambda cut: [pl.BlockSpec((R, cut), lambda i, r=r: (r, i)) for r in range(2)],
+    (total_in,) = call(
+        last_weight_kernel, [acc, turned, pga1, pgb1], [shape_of(BF16, HALF, JOINT)],
+        "last_weights", out_specs=[IN_HBM],
+        scratch=[pltpu.VMEM((HALF, JOINT), BF16), pltpu.SemaphoreType.DMA((8,))],
     )
     return (total_in[None], total_out[None])
 

time: 102 us -> 97.4 us (0.955)
  waiting for transfers between devices: 30.6 us -> 38.6 us
  starting transfers between devices: 30.5 us -> 24.2 us
  local copies, waits for them, and re-layouts: 7.76 us -> 3.5 us
  Pallas kernels: 30.8 us -> 28.9 us
    ppermute x4, waiting for transfers between devices: 9.39 us -> 18.2 us  [hop(): lax.ppermute(value, 'blk', [(i, (i + step) % count) for i in range(count)])]
    ppermute x8, starting transfers between devices: 17.7 us -> 11.7 us  [swap(): return lax.ppermute(value, 'stretch', [(0, 1), (1, 0)])]
    unnamed x30 -> x16, local copies, waits for them, and re-layouts: 7.76 us -> 3.5 us
    pallas_call x18, Pallas kernels: 30.8 us -> 28.9 us  [call(): pl.pallas_call(kernel, grid=(1,), in_specs=[specs.get(i) or block(*a.shap...]
  transfers between devices with their start and end apart: 12 -> 12, of which waited for: 8 -> 9; matrix products, arithmetic and copies ran while one was open for 1% -> 1% of each run, Pallas kernels for 22% -> 19%
where the time goes in v3:
time: 97.4 us; the launch traced here: 97.2 us
  waiting for transfers between devices  38.6 us (40%)
  Pallas kernels  28.9 us (30%)
  starting transfers between devices  24.2 us (25%)
  local copies, waits for them, and re-layouts  3.5 us (4%)
  between operations  1.05 us (1%)
    pallas_call x18, Pallas kernels, call(): pl.pallas_call(kernel, grid=(1,), in_specs=[specs.get(i) or block(*a.shap...  28.9 us
    ppermute x8, waiting for transfers between devices, swap(): return lax.ppermute(value, 'stretch', [(0, 1), (1, 0)])  20.5 us
    ppermute x4, waiting for transfers between devices, hop(): lax.ppermute(value, 'blk', [(i, (i + step) % count) for i in range(count)])  18.2 us
    ppermute x4, starting transfers between devices, hop(): lax.ppermute(value, 'blk', [(i, (i + step) % count) for i in range(count)])  12.5 us
    ppermute x8, starting transfers between devices, swap(): return lax.ppermute(value, 'stretch', [(0, 1), (1, 0)])  11.7 us
    unnamed x16, local copies, waits for them, and re-layouts  3.5 us
  transfers between devices with their start and end apart: 12, of which 9 were waited for; matrix products, arithmetic and copies ran while one was open for 1% of the time, Pallas kernels for 19%

profile of v3, /device:TPU:2, one launch (start us, length us, event | category | flops | bytes accessed | tf_op | source)
XLA Modules:
  0.0 97.2 jit_solution(16846275411138457563)
XLA Ops:
  0.6 0.0 copy-start.6
  0.6 0.0 copy-start.7
  0.7 0.0 copy-start.5
  0.7 0.0 copy-start.4
  0.7 4.7 %project_first.1 = (bf16[128,1664]{1,0:T(8,128)(2,1)}, bf16[128,1664]{1,0:T(8,128)(2,1)}) custom-call(bf16[256,1024]{1,0:T(8,128)(2,1)} %x1_ref, bf16[1,1024]{1,0:T(2,128)(2,1)} %gain_ref.9, bf16[1024,1536]{1,0:T(8,128)(2,1)} %bitcast.6), custom_call_target="tpu_custom_call" | custom-call | flops 1 | bytes 1 | tf_op jit(solution)/shard_map/project_first/pallas_call | solution.py:362
  5.4 2.2 %collective-permute-start = (bf16[128,1664]{1,0:T(8,128)(2,1)}, bf16[128,1664]{1,0:T(8,128)(2,1)S(1)}, u32[]{:S(2)}, u32[]{:S(2)}) collective-permute-start(bf16[128,1664]{1,0:T(8,128)(2,1)} %get-tuple-element.81), channel_id=1, source_target_pairs={{0,1},{1,0},{2,3},{3,2},{4,5},{5,4},{6,7},{7,6},{8,9},{9,8},{10,11... | collective-permute-start | bytes 1277960 | tf_op jit(solution)/shard_map/ppermute | solution.py:376
  7.6 1.4 %collective-permute-start.2 = (bf16[128,1664]{1,0:T(8,128)(2,1)}, bf16[128,1664]{1,0:T(8,128)(2,1)S(1)}, u32[]{:S(2)}, u32[]{:S(2)}) collective-permute-start(bf16[128,1664]{1,0:T(8,128)(2,1)} %get-tuple-element.76), channel_id=1, source_target_pairs={{0,1},{1,0},{2,3},{3,2},{4,5},{5,4},{6,7},{7,6},{8,9},{9,8},{10,11... | collective-permute-start | bytes 1277960 | tf_op jit(solution)/shard_map/ppermute | solution.py:376
  9.0 0.8 dynamic-slice_convert_fusion
  9.9 0.0 copy-done.6
  9.9 0.0 copy-done.7
  9.9 0.1 prepare.1
  10.0 0.0 copy-done.5
  10.0 0.0 copy-done.4
  10.0 0.0 copy-start
  10.0 1.9 %copy-done = bf16[1,1024,1536]{2,1,0:T(8,128)(2,1)S(1)} copy-done((bf16[1,1024,1536]{2,1,0:T(8,128)(2,1)S(1)}, bf16[1,1024,1536]{2,1,0:T(8,128)(2,1)}, u32[]{:S(2)}) %copy-start) | copy-done | bytes 3145752
  11.9 0.0 copy-start.2
  11.9 1.6 %copy-done.2 = bf16[1,1024,1024]{2,1,0:T(8,128)(2,1)S(1)} copy-done((bf16[1,1024,1024]{2,1,0:T(8,128)(2,1)S(1)}, bf16[1,1024,1024]{2,1,0:T(8,128)(2,1)}, u32[]{:S(2)}) %copy-start.2) | copy-done | bytes 2097176
  13.5 0.0 copy-start.3
  13.5 1.8 %project_own.1 = (f32[128,1536]{1,0:T(8,128)S(1)}, f32[128,128]{1,0:T(8,128)S(1)}, f32[128,1536]{1,0:T(8,128)S(1)}, f32[128,128]{1,0:T(8,128)S(1)}, bf16[1536,10...) custom-call(bf16[256,1024]{1,0:T(8,128)(2,1)S(1)} %copy-done.4, bf16[1,1024]{1,0:T(2,128)(2,1)S(1)} %copy-done.5, ...), custom_call_target="tpu_custom_call" | custom-call | flops 1 | bytes 1 | tf_op jit(solution)/shard_map/project_own/pallas_call | solution.py:362
  15.3 4.6 %collective-permute-done.msg_ref = bf16[128,1664]{1,0:T(8,128)(2,1)S(1)} collective-permute-done((bf16[128,1664]{1,0:T(8,128)(2,1)}, bf16[128,1664]{1,0:T(8,128)(2,1)S(1)}, u32[]{:S(2)}, u32[]{:S(2)}) %collective-permute-start) | collective-permute-done | bytes 426016 | tf_op jit(solution)/shard_map/ppermute | solution.py:376
  19.9 0.0 copy-done.3
  19.9 0.0 copy-start.1
  19.9 1.4 %attend.4 = (bf16[128,1024]{1,0:T(8,128)(2,1)S(1)}, bf16[128,1024]{1,0:T(8,128)(2,1)S(1)}, bf16[128,1024]{1,0:T(8,128)(2,1)S(1)}, bf16[128,256]{1,0:T(8,128)(2,1...) custom-call(bf16[128,1664]{1,0:T(8,128)(2,1)S(1)} %collective-permute-done.msg_ref, ...), custom_call_target="tpu_custom_call" | custom-call | flops 1 | bytes 1 | tf_op jit(solution)/shard_map/attend/pallas_call | solution.py:362
  21.3 5.8 %collective-permute-start.1 = (bf16[128,1024]{1,0:T(8,128)(2,1)S(1)}, bf16[128,1024]{1,0:T(8,128)(2,1)S(1)}, u32[]{:S(2)}, u32[]{:S(2)}) collective-permute-start(bf16[128,1024]{1,0:T(8,128)(2,1)S(1)} %get-tuple-element.89), channel_id=1, source_target_pairs={{0,254},{2,0},{4,2},{6,4},{8,6},{10,8},{12,10},{14,12},{16,14},{18... | collective-permute-start | bytes 786440 | tf_op jit(solution)/shard_map/ppermute | solution.py:381
  27.1 3.9 %collective-permute-done.1.x_ref.refs_11_.x2a_ref = bf16[128,1024]{1,0:T(8,128)(2,1)S(1)} collective-permute-done((bf16[128,1024]{1,0:T(8,128)(2,1)S(1)}, bf16[128,1024]{1,0:T(8,128)(2,1)S(1)}, u32[]{:S(2)}, u32[]{:S(2)}) %collective-permute-start.1) | collective-permute-done | bytes 262176 | tf_op jit(solution)/shard_map/ppermute | solution.py:381
  31.1 0.0 copy-done.1
  31.1 0.6 project.2
  31.7 2.5 %collective-permute-start.4 = (bf16[128,1664]{1,0:T(8,128)(2,1)S(1)}, bf16[128,1664]{1,0:T(8,128)(2,1)S(1)}, u32[]{:S(2)}, u32[]{:S(2)}) collective-permute-start(bf16[128,1664]{1,0:T(8,128)(2,1)S(1)} %get-tuple-element.90), channel_id=1, source_target_pairs={{0,1},{1,0},{2,3},{3,2},{4,5},{5,4},{6,7},{7,6},{8,9},{9,8},{10,11... | collective-permute-start | bytes 1277960 | tf_op jit(solution)/shard_map/ppermute | solution.py:376
  34.1 0.0 collective-permute-done.2.msg_ref
  34.1 1.8 %attend.5 = (bf16[128,1024]{1,0:T(8,128)(2,1)S(1)}, bf16[128,1024]{1,0:T(8,128)(2,1)S(1)}, bf16[128,1024]{1,0:T(8,128)(2,1)S(1)}, bf16[128,256]{1,0:T(8,128)(2,1...) custom-call(bf16[128,1664]{1,0:T(8,128)(2,1)S(1)} %collective-permute-done.2.msg_ref, ...), custom_call_target="tpu_custom_call" | custom-call | flops 1 | bytes 1 | tf_op jit(solution)/shard_map/attend/pallas_call | solution.py:362
  35.9 6.5 %collective-permute-start.3 = (bf16[128,1024]{1,0:T(8,128)(2,1)S(1)}, bf16[128,1024]{1,0:T(8,128)(2,1)S(1)}, u32[]{:S(2)}, u32[]{:S(2)}) collective-permute-start(bf16[128,1024]{1,0:T(8,128)(2,1)S(1)} %get-tuple-element.96), channel_id=1, source_target_pairs={{0,254},{2,0},{4,2},{6,4},{8,6},{10,8},{12,10},{14,12},{16,14},{18... | collective-permute-start | bytes 786440 | tf_op jit(solution)/shard_map/ppermute | solution.py:381
  42.5 3.9 %collective-permute-done.3.x_ref.refs_11_.x2b_ref = bf16[128,1024]{1,0:T(8,128)(2,1)S(1)} collective-permute-done((bf16[128,1024]{1,0:T(8,128)(2,1)S(1)}, bf16[128,1024]{1,0:T(8,128)(2,1)S(1)}, u32[]{:S(2)}, u32[]{:S(2)}) %collective-permute-start.3) | collective-permute-done | bytes 262176 | tf_op jit(solution)/shard_map/ppermute | solution.py:381
  46.4 0.6 project.3
  47.0 0.1 collective-permute-start.5
  47.1 0.0 collective-permute-done.4.msg_ref
  47.1 1.7 %attend.6 = (bf16[128,1024]{1,0:T(8,128)(2,1)S(1)}, bf16[128,1024]{1,0:T(8,128)(2,1)S(1)}, bf16[128,1024]{1,0:T(8,128)(2,1)S(1)}, bf16[128,256]{1,0:T(8,128)(2,1...) custom-call(bf16[128,1664]{1,0:T(8,128)(2,1)S(1)} %collective-permut, ...), custom_call_target="tpu_custom_call" | custom-call | flops 10000000000 | bytes 1 | tf_op jit(solution)/shard_map/attend/pallas_call | solution.py:362
  48.9 3.8 %collective-permute-start.6 = (bf16[128,1024]{1,0:T(8,128)(2,1)S(1)}, bf16[128,1024]{1,0:T(8,128)(2,1)S(1)}, u32[]{:S(2)}, u32[]{:S(2)}) collective-permute-start(bf16[128,1024]{1,0:T(8,128)(2,1)S(1)} %get-tuple-element.110), channel_id=1, source_target_pairs={{0,1},{1,0},{2,3},{3,2},{4,5},{5,4},{6,7},{7,6},{8,9},{9,8},{10,11... | collective-permute-start | bytes 786440 | tf_op jit(solution)/shard_map/ppermute | solution.py:376
  52.6 6.9 %collective-permute-done.5.msg_ref = bf16[128,1664]{1,0:T(8,128)(2,1)S(1)} collective-permute-done((bf16[128,1664]{1,0:T(8,128)(2,1)S(1)}, bf16[128,1664]{1,0:T(8,128)(2,1)S(1)}, u32[]{:S(2)}, u32[]{:S(2)}) %collective-permute-start.5) | collective-permute-done | bytes 426016 | tf_op jit(solution)/shard_map/ppermute | solution.py:376
  59.5 2.1 %attend.7 = (bf16[128,1024]{1,0:T(8,128)(2,1)S(1)}, bf16[128,1024]{1,0:T(8,128)(2,1)S(1)}, bf16[128,1024]{1,0:T(8,128)(2,1)S(1)}, bf16[128,256]{1,0:T(8,128)(2,1...) custom-call(bf16[128,1664]{1,0:T(8,128)(2,1)S(1)} %collective-permut, ...), custom_call_target="tpu_custom_call" | custom-call | flops 1 | bytes 1 | tf_op jit(solution)/shard_map/attend/pallas_call | solution.py:362
  61.6 0.1 collective-permute-start.7
  61.7 0.6 collective-permute-done.6.refs_0_
  62.3 7.2 %collective-permute-done.7.refs_0_ = bf16[128,1024]{1,0:T(8,128)(2,1)S(1)} collective-permute-done((bf16[128,1024]{1,0:T(8,128)(2,1)S(1)}, bf16[128,1024]{1,0:T(8,128)(2,1)S(1)}, u32[]{:S(2)}, u32[]{:S(2)}) %collective-permute-start.7) | collective-permute-done | bytes 262176 | tf_op jit(solution)/shard_map/ppermute | solution.py:376
  69.6 2.3 %attend_back.4 = (bf16[128,1536]{1,0:T(8,128)(2,1)S(1)}, f32[128,256]{1,0:T(8,128)S(1)}, f32[128,256]{1,0:T(8,128)S(1)}, bf16[128,1024]{1,0:T(8,128)(2,1)S(1)}) custom-call(bf16[128,1024]{1,0:T(8,128)(2,1)S(1)} %collective-permute-done.7.refs_0_, f32[128,1024]{1,0:T(8,128)S(1)} %get-tuple-element.116.refs_1_, ...), custom_call_target="tpu_custom_call" | custom-call | flops 1 | bytes 1 | tf_op jit(solution)/shard_map/attend_back/pallas_call | solution.py:362
  71.9 0.1 collective-permute-start.9
  72.0 1.9 %attend_back.5 = (bf16[128,1536]{1,0:T(8,128)(2,1)S(1)}, bf16[128,1024]{1,0:T(8,128)(2,1)S(1)}) custom-call(bf16[128,1024]{1,0:T(8,128)(2,1)S(1)} %collective-permute-done.6.refs_0_, f32[128,1024]{1,0:T(8,128)S(1)} %get-tuple-element.111.refs_1_, bf16[128,1024]{1,0:T(8,128)(2,1)S(1)} %get-tuple-element.112.refs_2_, ...), custom_call_target="tpu_custom_call" | custom-call | flops 1 | bytes 1 | tf_op jit(solution)/shard_map/attend_back/pallas_call | solution.py:362
  74.0 0.1 collective-permute-start.8
  74.1 8.1 %collective-permute-done.9.up_ref.refs_5_ = bf16[128,1024]{1,0:T(8,128)(2,1)S(1)} collective-permute-done((bf16[128,1024]{1,0:T(8,128)(2,1)S(1)}, bf16[128,1024]{1,0:T(8,128)(2,1)S(1)}, u32[]{:S(2)}, u32[]{:S(2)}) %collective-permute-start.9) | collective-permute-done | bytes 262176 | tf_op jit(solution)/shard_map/ppermute | solution.py:381
  82.1 0.5 output_back.2
  82.6 0.1 collective-permute-start.11
  82.7 2.3 %collective-permute-done.8.up_ref.refs_4_ = bf16[128,1024]{1,0:T(8,128)(2,1)S(1)} collective-permute-done((bf16[128,1024]{1,0:T(8,128)(2,1)S(1)}, bf16[128,1024]{1,0:T(8,128)(2,1)S(1)}, u32[]{:S(2)}, u32[]{:S(2)}) %collective-permute-start.8) | collective-permute-done | bytes 262176 | tf_op jit(solution)/shard_map/ppermute | solution.py:381
  84.9 0.5 output_back.3
  85.4 1.6 %collective-permute-start.10 = (bf16[128,1024]{1,0:T(8,128)(2,1)S(1)}, bf16[128,1024]{1,0:T(8,128)(2,1)S(1)}, u32[]{:S(2)}, u32[]{:S(2)}) collective-permute-start(bf16[128,1024]{1,0:T(8,128)(2,1)S(1)} %get-tuple-element.134), channel_id=1, source_target_pairs={{0,1},{1,0},{2,3},{3,2},{4,5},{5,4},{6,7},{7,6},{8,9},{9,8},{10,11... | collective-permute-start | bytes 786440 | tf_op jit(solution)/shard_map/ppermute | solution.py:376
  87.0 1.0 %early_weights.1 = (f32[1024,1536]{1,0:T(8,128)S(1)}, bf16[1024,256]{1,0:T(8,128)(2,1)S(1)}) custom-call(bf16[256,1024]{1,0:T(8,128)(2,1)S(1)} %copy-done.4, bf16[128,1024]{1,0:T(8,128)(2,1)S(1)} %collective-permute-done.1.x_ref.refs_11_.x2a_ref, bf16[128,1024]{1,0:T(8,128)(2,1)S(1)} %collective-permute-done.3.x_ref.refs_11_.x2b_ref, ...), custom_call_target="tpu_custom_call" | custom-call | flops 1 | bytes 1 | tf_op jit(solution)/shard_map/early_weights/pallas_call | solution.py:362
  88.0 2.6 %output_weights.1 = bf16[1024,1024]{1,0:T(8,128)(2,1)} custom-call(bf16[128,1024]{1,0:T(8,128)(2,1)S(1)} %get-tuple-element.146.refs_0_, bf16[128,1024]{1,0:T(8,128)(2,1)S(1)} %get-tuple-element.147.refs_1_, bf16[128,1024]{1,0:T(8,128)(2,1)S(1)} %get-tuple-element.148.refs_2_, bf16[128,1024]{1,0:T(8,128)(2,1)S(1)} %get-tuple-element.149.refs_3_, ...), custom_call_target="tpu_custom_call" | custom-call | flops 1 | bytes 1 | tf_op jit(solution)/shard_map/output_weights/pallas_call | solution.py:362
  90.6 0.0 collective-permute-done.11.refs_0_
  90.6 1.8 %attend_back.6 = (bf16[128,1536]{1,0:T(8,128)(2,1)S(1)}, f32[128,256]{1,0:T(8,128)S(1)}, f32[128,256]{1,0:T(8,128)S(1)}) custom-call(bf16[128,1024]{1,0:T(8,128)(2,1)S(1)} %collective-permute-done.11.refs_0_, f32[128,1024]{1,0:T(8,128)S(1)} %get-tuple-element.138.refs_1_, bf16[128,1024]{1,0:T(8,128)(2,1)S(1)} %get-tuple-element.139.refs_2_, ...), custom_call_target="tpu_custom_call" | custom-call | flops 1 | bytes 1 | tf_op jit(solution)/shard_map/attend_back/pallas_call | solution.py:362
  92.5 1.1 %collective-permute-done.10.refs_0_ = bf16[128,1024]{1,0:T(8,128)(2,1)S(1)} collective-permute-done((bf16[128,1024]{1,0:T(8,128)(2,1)S(1)}, bf16[128,1024]{1,0:T(8,128)(2,1)S(1)}, u32[]{:S(2)}, u32[]{:S(2)}) %collective-permute-start.10) | collective-permute-done | bytes 262176 | tf_op jit(solution)/shard_map/ppermute | solution.py:376
  93.6 1.4 %attend_back.7.pa_ref = bf16[128,1536]{1,0:T(8,128)(2,1)S(1)} custom-call(bf16[128,1024]{1,0:T(8,128)(2,1)S(1)} %collective-permute-done.10.refs_0_, f32[128,1024]{1,0:T(8,128)S(1)} %get-tuple-element.135.refs_1_, bf16[128,1024]{1,0:T(8,128)(2,1)S(1)} %get-tuple-element.136.refs_2_, bf16[1024,256]{1,0:T(8,128)(2,1)S(1)} %get-tuple-element.137.refs_3_, ...), custom_call_target="tpu_custom_call" | custom-call | flops 1 | bytes 1 | tf_op jit(solution)/shard_map/attend_back/pallas_call | solution.py:362
  95.0 2.0 %last_weights.1 = bf16[1024,1536]{1,0:T(8,128)(2,1)} custom-call(f32[1024,1536]{1,0:T(8,128)S(1)} %get-tuple-element.128.acc_ref, bf16[1024,256]{1,0:T(8,128)(2,1)S(1)} %get-tuple-element.129.turned_ref, bf16[128,1536]{1,0:T(8,128)(2,1)S(1)} %attend_back.7.pa_ref, bf16[128,1536]{1,0:T(8,128)(2,1)S(1)} %get-tuple-element.145.pb_ref), custom_call_target="tpu_custom_call" | custom-call | flops 1 | bytes 1 | tf_op jit(solution)/shard_map/last_weights/pallas_call | solution.py:362
Async XLA Ops:
  0.6 9.2 %copy-start.6 = (f32[256,128]{1,0:T(8,128)S(1)}, f32[256,128]{1,0:T(8,128)}, u32[]{:S(2)}) copy-start(f32[256,128]{1,0:T(8,128)} %constant.23.clone.sin_in) | copy-start | bytes 393220
  0.6 9.2 %copy-start.7 = (f32[256,128]{1,0:T(8,128)S(1)}, f32[256,128]{1,0:T(8,128)}, u32[]{:S(2)}) copy-start(f32[256,128]{1,0:T(8,128)} %constant.22.clone.cos_in) | copy-start | bytes 393220
  0.7 9.4 %copy-start.5 = (bf16[1,1024]{1,0:T(2,128)(2,1)S(1)}, bf16[1,1024]{1,0:T(2,128)(2,1)}, u32[]{:S(2)}) copy-start(bf16[1,1024]{1,0:T(2,128)(2,1)} %gain_ref.9) | copy-start | bytes 6148
  0.7 9.4 %copy-start.4 = (bf16[256,1024]{1,0:T(8,128)(2,1)S(1)}, bf16[256,1024]{1,0:T(8,128)(2,1)}, u32[]{:S(2)}) copy-start(bf16[256,1024]{1,0:T(8,128)(2,1)} %x1_ref) | copy-start | bytes 1572868
  5.4 14.5 %collective-permute-start = (bf16[128,1664]{1,0:T(8,128)(2,1)}, bf16[128,1664]{1,0:T(8,128)(2,1)S(1)}, u32[]{:S(2)}, u32[]{:S(2)}) collective-permute-start(bf16[128,1664]{1,0:T(8,128)(2,1)} %get-tuple-element.81), channel_id=1, source_target_pairs={{0,1},{1,0},{2,3},{3,2},{4,5},{5,4},{6,7},{7,6},{8,9},{9,8},{10,11... | collective-permute-start | bytes 1277960 | tf_op jit(solution)/shard_map/ppermute | solution.py:376
  7.6 26.5 %collective-permute-start.2 = (bf16[128,1664]{1,0:T(8,128)(2,1)}, bf16[128,1664]{1,0:T(8,128)(2,1)S(1)}, u32[]{:S(2)}, u32[]{:S(2)}) collective-permute-start(bf16[128,1664]{1,0:T(8,128)(2,1)} %get-tuple-element.76), channel_id=1, source_target_pairs={{0,1},{1,0},{2,3},{3,2},{4,5},{5,4},{6,7},{7,6},{8,9},{9,8},{10,11... | collective-permute-start | bytes 1277960 | tf_op jit(solution)/shard_map/ppermute | solution.py:376
  10.0 1.9 %copy-start = (bf16[1,1024,1536]{2,1,0:T(8,128)(2,1)S(1)}, bf16[1,1024,1536]{2,1,0:T(8,128)(2,1)}, u32[]{:S(2)}) copy-start(bf16[1,1024,1536]{2,1,0:T(8,128)(2,1)} %param.9) | copy-start | bytes 9437188
  11.9 1.6 %copy-start.2 = (bf16[1,1024,1024]{2,1,0:T(8,128)(2,1)S(1)}, bf16[1,1024,1024]{2,1,0:T(8,128)(2,1)}, u32[]{:S(2)}) copy-start(bf16[1,1024,1024]{2,1,0:T(8,128)(2,1)} %param.10) | copy-start | bytes 6291460
  13.5 6.4 %copy-start.3 = (bf16[1,1024,1024]{2,1,0:T(8,128)(2,1)S(1)}, bf16[1,1024,1024]{2,1,0:T(8,128)(2,1)}, u32[]{:S(2)}) copy-start(bf16[1,1024,1024]{2,1,0:T(8,128)(2,1)} %param.10) | copy-start | bytes 6291460
  19.9 11.1 %copy-start.1 = (bf16[1,1024,1536]{2,1,0:T(8,128)(2,1)S(1)}, bf16[1,1024,1536]{2,1,0:T(8,128)(2,1)}, u32[]{:S(2)}) copy-start(bf16[1,1024,1536]{2,1,0:T(8,128)(2,1)} %param.9) | copy-start | bytes 9437188
  21.3 9.7 %collective-permute-start.1 = (bf16[128,1024]{1,0:T(8,128)(2,1)S(1)}, bf16[128,1024]{1,0:T(8,128)(2,1)S(1)}, u32[]{:S(2)}, u32[]{:S(2)}) collective-permute-start(bf16[128,1024]{1,0:T(8,128)(2,1)S(1)} %get-tuple-element.89), channel_id=1, source_target_pairs={{0,254},{2,0},{4,2},{6,4},{8,6},{10,8},{12,10},{14,12},{16,14},{18... | collective-permute-start | bytes 786440 | tf_op jit(solution)/shard_map/ppermute | solution.py:381
  31.7 15.4 %collective-permute-start.4 = (bf16[128,1664]{1,0:T(8,128)(2,1)S(1)}, bf16[128,1664]{1,0:T(8,128)(2,1)S(1)}, u32[]{:S(2)}, u32[]{:S(2)}) collective-permute-start(bf16[128,1664]{1,0:T(8,128)(2,1)S(1)} %get-tuple-element.90), channel_id=1, source_target_pairs={{0,1},{1,0},{2,3},{3,2},{4,5},{5,4},{6,7},{7,6},{8,9},{9,8},{10,11... | collective-permute-start | bytes 1277960 | tf_op jit(solution)/shard_map/ppermute | solution.py:376
  35.9 10.5 %collective-permute-start.3 = (bf16[128,1024]{1,0:T(8,128)(2,1)S(1)}, bf16[128,1024]{1,0:T(8,128)(2,1)S(1)}, u32[]{:S(2)}, u32[]{:S(2)}) collective-permute-start(bf16[128,1024]{1,0:T(8,128)(2,1)S(1)} %get-tuple-element.96), channel_id=1, source_target_pairs={{0,254},{2,0},{4,2},{6,4},{8,6},{10,8},{12,10},{14,12},{16,14},{18... | collective-permute-start | bytes 786440 | tf_op jit(solution)/shard_map/ppermute | solution.py:381
  47.0 12.5 %collective-permute-start.5 = (bf16[128,1664]{1,0:T(8,128)(2,1)S(1)}, bf16[128,1664]{1,0:T(8,128)(2,1)S(1)}, u32[]{:S(2)}, u32[]{:S(2)}) collective-permute-start(bf16[128,1664]{1,0:T(8,128)(2,1)S(1)} %get-tuple-element.104), channel_id=1, source_target_pairs={{0,1},{1,0},{2,3},{3,2},{4,5},{5,4},{6,7},{7,6},{8,9},{9,8},{10,11... | collective-permute-start | bytes 1277960 | tf_op jit(solution)/shard_map/ppermute | solution.py:376
  48.9 13.5 %collective-permute-start.6 = (bf16[128,1024]{1,0:T(8,128)(2,1)S(1)}, bf16[128,1024]{1,0:T(8,128)(2,1)S(1)}, u32[]{:S(2)}, u32[]{:S(2)}) collective-permute-start(bf16[128,1024]{1,0:T(8,128)(2,1)S(1)} %get-tuple-element.110), channel_id=1, source_target_pairs={{0,1},{1,0},{2,3},{3,2},{4,5},{5,4},{6,7},{7,6},{8,9},{9,8},{10,11... | collective-permute-start | bytes 786440 | tf_op jit(solution)/shard_map/ppermute | solution.py:376
  61.6 8.0 %collective-permute-start.7 = (bf16[128,1024]{1,0:T(8,128)(2,1)S(1)}, bf16[128,1024]{1,0:T(8,128)(2,1)S(1)}, u32[]{:S(2)}, u32[]{:S(2)}) collective-permute-start(bf16[128,1024]{1,0:T(8,128)(2,1)S(1)} %get-tuple-element.114), channel_id=1, source_target_pairs={{0,1},{1,0},{2,3},{3,2},{4,5},{5,4},{6,7},{7,6},{8,9},{9,8},{10,11... | collective-permute-start | bytes 786440 | tf_op jit(solution)/shard_map/ppermute | solution.py:376
  71.9 10.2 %collective-permute-start.9 = (bf16[128,1024]{1,0:T(8,128)(2,1)S(1)}, bf16[128,1024]{1,0:T(8,128)(2,1)S(1)}, u32[]{:S(2)}, u32[]{:S(2)}) collective-permute-start(bf16[128,1024]{1,0:T(8,128)(2,1)S(1)} %get-tuple-element.131), channel_id=1, source_target_pairs={{0,2},{2,4},{4,6},{6,8},{8,10},{10,12},{12,14},{14,16},{16,18},{18... | collective-permute-start | bytes 786440 | tf_op jit(solution)/shard_map/ppermute | solution.py:381
  74.0 11.0 %collective-permute-start.8 = (bf16[128,1024]{1,0:T(8,128)(2,1)S(1)}, bf16[128,1024]{1,0:T(8,128)(2,1)S(1)}, u32[]{:S(2)}, u32[]{:S(2)}) collective-permute-start(bf16[128,1024]{1,0:T(8,128)(2,1)S(1)} %get-tuple-element.130), channel_id=1, source_target_pairs={{0,2},{2,4},{4,6},{6,8},{8,10},{10,12},{12,14},{14,16},{16,18},{18... | collective-permute-start | bytes 786440 | tf_op jit(solution)/shard_map/ppermute | solution.py:381
  82.6 8.1 %collective-permute-start.11 = (bf16[128,1024]{1,0:T(8,128)(2,1)S(1)}, bf16[128,1024]{1,0:T(8,128)(2,1)S(1)}, u32[]{:S(2)}, u32[]{:S(2)}) collective-permute-start(bf16[128,1024]{1,0:T(8,128)(2,1)S(1)} %get-tuple-element.132), channel_id=1, source_target_pairs={{0,1},{1,0},{2,3},{3,2},{4,5},{5,4},{6,7},{7,6},{8,9},{9,8},{10,11... | collective-permute-start | bytes 786440 | tf_op jit(solution)/shard_map/ppermute | solution.py:376
  85.4 8.2 %collective-permute-start.10 = (bf16[128,1024]{1,0:T(8,128)(2,1)S(1)}, bf16[128,1024]{1,0:T(8,128)(2,1)S(1)}, u32[]{:S(2)}, u32[]{:S(2)}) collective-permute-start(bf16[128,1024]{1,0:T(8,128)(2,1)S(1)} %get-tuple-element.134), channel_id=1, source_target_pairs={{0,1},{1,0},{2,3},{3,2},{4,5},{5,4},{6,7},{7,6},{8,9},{9,8},{10,11... | collective-permute-start | bytes 786440 | tf_op jit(solution)/shard_map/ppermute | solution.py:376

commit v4 on v3

--- a/solution.py
+++ b/solution.py
@@ -20,6 +20,7 @@
 HEADS = 1024
 KEYS = 256
 JOINT = HEADS + 2 * KEYS
+PART = JOINT // 2
 LOG2E = 1.4426950408889634
 
 NN = (((1,), (0,)), ((), ()))
@@ -89,6 +90,10 @@
         outs[stream][:, :JOINT] = part[R * stream : R * stream + R].astype(BF16)
 
 
+def half_pieces(half):
+    return ((512 * half, 512), (HEADS + 128 * half, 128), (HEADS + KEYS + 128 * half, 128))
+
+
 def project_own_kernel(x_ref, gain_ref, w_ref, w_out_ref, *rest):
     outs, w_t_ref, w_out_t_ref = rest[:4], rest[4], rest[5]
     x = x_ref[...].astype(F32)
@@ -97,7 +102,10 @@
         rows = slice(R * stream, R * stream + R)
         outs[2 * stream][...] = own[rows]
         outs[2 * stream + 1][...] = token_sums(x[rows])
-    w_t_ref[...] = jnp.transpose(w_ref[...])
+    place = 0
+    for start, size in half_pieces(0) + half_pieces(1):
+        w_t_ref[place : place + size, :] = jnp.transpose(w_ref[:, start : start + size])
+        place += size
     w_out_t_ref[...] = jnp.transpose(w_out_ref[...])
 
 
@@ -212,38 +220,49 @@
     out_ref[...] = out
     if turn:
         own = dot(out, w_t_ref[...])
-        outs[7][...] = own.astype(BF16)
-        outs[8][...] = own
-
-
-def attend_back(stream, with_sums, recv_ref, own_ref, q_ref, p_ref, cos_ref, sin_ref, kv, partial_refs, pg_ref):
+        put_message(own, outs[8:])
+        outs[7][...] = own
+
+
+def put_message(own, msg_refs):
+    width = own.shape[1] // len(msg_refs)
+    for i, msg_ref in enumerate(msg_refs):
+        msg_ref[...] = own[:, i * width : i * width + width].astype(BF16)
+
+
+def attend_back(stream, half, r, kv, with_sums):
     seen = R * (stream + 1)
-    cosine, sine = cos_ref[seen - R : seen], sin_ref[seen - R : seen]
-    ks, vs = [], []
-    for i in range(2):
-        cols = columns(i)
-        ks.append(jnp.concatenate([r[:, cols] for r in kv[0::2]], axis=0).astype(F32))
-        vs.append(jnp.concatenate([r[:, cols] for r in kv[1::2]], axis=0).astype(F32))
-    grads = [own_ref[:, columns(i)] + recv_ref[:, columns(i)].astype(F32) for i in range(8)]
+    cosine, sine = r["cos"][seen - R : seen], r["sin"][seen - R : seen]
+    k, v = (
+        jnp.concatenate([ref[:, columns(half)] for ref in kv[i::2]], axis=0).astype(F32)
+        for i in range(2)
+    )
+    cols = [columns(4 * half + i) for i in range(4)]
+    if "recv" in r:
+        received = [r["recv"][:, c] for c in cols]
+    else:
+        received = [r["recv%d" % half][:, columns(i)] for i in range(4)]
+    grads = [r["own"][:, c] + piece.astype(F32) for c, piece in zip(cols, received)]
     low = lane_index((T, 128)) < 64
     dps = [
-        dot(group_pair(vs[g // 2], g % 2).astype(BF16), stack_pairs(grads, g).astype(BF16), NT)
-        for g in range(4)
+        dot(group_pair(v, g).astype(BF16), stack_pairs(grads, g).astype(BF16), NT)
+        for g in range(2)
     ]
-    turned = [jnp.transpose(k).astype(BF16) for k in ks]
+    turned = jnp.transpose(k).astype(BF16)
     total = jnp.zeros((R, 128), F32)
+    pg_ref, p_ref = r["pg%d" % half], r["p"]
     dks, dvs = [], []
-    for g in range(4):
+    for g in range(2):
         dss, ps = [], []
-        for half in range(2):
-            start = (2 * g + half) * seen
+        for side in range(2):
+            start = (4 * half + 2 * g + side) * seen
             weights = p_ref[start : start + seen, :]
             wide_weights = weights.astype(F32)
-            product = wide_weights * dps[g][seen * half : seen * half + seen]
+            product = wide_weights * dps[g][seen * side : seen * side + seen]
             ds = product - wide_weights * jnp.sum(product, axis=0, keepdims=True)
             dss.append(ds.astype(BF16))
             ps.append(weights)
-        q = jnp.concatenate([q_ref[:, columns(2 * g)], q_ref[:, columns(2 * g + 1)]], axis=0)
+        q = jnp.concatenate([r["q"][:, cols[2 * g]], r["q"][:, cols[2 * g + 1]]], axis=0)
         q = q.astype(F32)
         grad = stack_pairs(grads, g)
         sides = []
@@ -255,62 +274,61 @@
         dv = dot(jnp.concatenate(ps, axis=1), sides[1])
         dks.append(dk + pltpu.roll(dk, 64, 1))
         dvs.append(dv + pltpu.roll(dv, 64, 1))
-        dq = jnp.transpose(dot(group_pair_back(turned[g // 2], g % 2), jnp.concatenate(dss, axis=0)))
+        dq = jnp.transpose(dot(group_pair_back(turned, g), jnp.concatenate(dss, axis=0)))
         if with_sums:
             product = dq * q
             total = total + product[:R] + product[R:]
         for i in range(2):
-            block = dq[R * i : R * i + R] * 0.125
-            pg_ref[:, columns(2 * g + i)] = rotate_back(block, cosine, sine).astype(BF16)
-    total = total * (1.0 / LOG2E)
+            part = dq[R * i : R * i + R] * 0.125
+            pg_ref[:, columns(2 * g + i)] = rotate_back(part, cosine, sine).astype(BF16)
     low = lane_index((seen, 128)) < 64
-    for i in range(2):
-        dk = jnp.where(low, dks[2 * i], dks[2 * i + 1]) * (1.0 / LOG2E)
-        dv = jnp.where(low, dvs[2 * i], dvs[2 * i + 1])
-        cols = columns(i)
-        if stream:
-            partial_refs[0][:, cols], partial_refs[1][:, cols] = dk[:R], dv[:R]
-            dk, dv = dk[R:], dv[R:]
-        else:
-            dk, dv = dk + partial_refs[0][:, cols], dv + partial_refs[1][:, cols]
-        if with_sums:
-            total = total + dk * ks[i][-R:] + dv * vs[i][-R:]
-        pg_ref[:, columns(8 + i)] = rotate_back(dk, cosine, sine).astype(BF16)
-        pg_ref[:, columns(10 + i)] = dv.astype(BF16)
-    return total
-
-
-def attend_back_kernel(stream, with_input, *refs):
-    count = 2 * (stream + 1)
-    fixed, kv, rest = refs[:6], refs[6 : 6 + count], list(refs[6 + count :])
-    if not stream:
-        partials, rest = rest[:2], rest[2:]
-    if with_input:
-        (w_t_ref, x_ref, gain_ref, scale_ref, up_ref), rest = rest[:5], rest[5:]
-    pg_ref, rest = rest[0], rest[1:]
+    dk = jnp.where(low, dks[0], dks[1]) * (1.0 / LOG2E)
+    dv = jnp.where(low, dvs[0], dvs[1])
     if stream:
-        partials, rest = rest[:2], rest[2:]
-    total = attend_back(stream, with_input, *fixed, kv, partials, pg_ref)
-    if with_input:
-        (out_ref,) = rest
+        r["dk%d" % half][...], r["dv%d" % half][...] = dk[:R], dv[:R]
+        dk, dv = dk[R:], dv[R:]
+    else:
+        dk, dv = dk + r["dk%d" % half][...], dv + r["dv%d" % half][...]
+    pg_ref[:, columns(4)] = rotate_back(dk, cosine, sine).astype(BF16)
+    pg_ref[:, columns(5)] = dv.astype(BF16)
+    return total * (1.0 / LOG2E) + dk * k[-R:] + dv * v[-R:] if with_sums else None
+
+
+def attend_back_kernel(stream, halves, names, *refs):
+    r = dict(zip(names, refs))
+    kv = [r[name] for name in ("ka", "va", "kb", "vb")[: 2 * stream + 2]]
+    total = grad = 0.0
+    for half in halves:
+        part = attend_back(stream, half, r, kv, "w" in r)
+        if "w" in r:
+            total = total + part
+            grad = grad + dot(r["pg%d" % half][...], r["w"][PART * half : PART * half + PART, :])
+    if "total" in r and "out" not in r:
+        r["total"][...], r["grad"][...] = total, grad
+    if "out" in r:
+        if "total" in r:
+            total, grad = total + r["total"][...], grad + r["grad"][...]
         sums = jnp.sum(total, axis=1, keepdims=True) / MODEL_WIDTH
-        grad = dot(pg_ref[...], w_t_ref[...])
-        scale = scale_ref[...]
-        out = up_ref[...].astype(F32) + wide(scale, HALF) * (gain_ref[...].astype(F32) * grad)
+        scale = r["scale"][...]
+        out = r["up"][...].astype(F32)
+        out = out + wide(scale, HALF) * (r["gain"][...].astype(F32) * grad)
         factor = wide(scale * scale * sums, HALF)
-        out_ref[...] = (out - x_ref[...].astype(F32) * factor).astype(BF16)
-
-
-def output_back_kernel(up_ref, w_t_ref, msg_ref, own_ref):
+        r["out"][...] = (out - r["x"][...].astype(F32) * factor).astype(BF16)
+
+
+def output_back_kernel(up_ref, w_t_ref, own_ref, *msg_refs):
     own = dot(up_ref[...], w_t_ref[...])
-    msg_ref[...] = own.astype(BF16)
     own_ref[...] = own
+    put_message(own, msg_refs)
 
 
 def output_weight_kernel(*refs):
-    att = jnp.concatenate([r[...] for r in refs[:4]], axis=0)
-    up = jnp.concatenate([r[...] for r in refs[4:8]], axis=0)
-    refs[8][...] = dot(att, up, TN).astype(BF16)
+    att = jnp.concatenate([refs[0][...], refs[1][...]], axis=0)
+    up = jnp.concatenate([refs[2][...], refs[3][...]], axis=0)
+    out = dot(att, up, TN)
+    if len(refs) > 5:
+        out = out + refs[4][...]
+    refs[-1][...] = out.astype(refs[-1].dtype)
 
 
 def gained(x, scale_ref, gain_ref):
@@ -318,27 +336,33 @@
 
 
 def early_weight_kernel(
-    x1_ref, x2a_ref, x2b_ref, s1a_ref, s1b_ref, s2a_ref, s2b_ref, gain_ref, pa_ref, pb_ref,
-    acc_ref, turned_ref,
+    x1_ref, x2a_ref, x2b_ref, s1a_ref, s1b_ref, s2a_ref, s2b_ref, gain_ref, *refs
 ):
+    pg_refs, acc_refs, turned_ref = refs[:4], refs[4:6], refs[6]
     second = [gained(x2a_ref[...], s2a_ref, gain_ref), gained(x2b_ref[...], s2b_ref, gain_ref)]
-    pgs = jnp.concatenate([pa_ref[...], pb_ref[...]], axis=0)
-    acc_ref[...] = dot(jnp.concatenate(second, axis=0), pgs, TN)
+    pgs = [jnp.concatenate([r[...] for r in pair], axis=0) for pair in (pg_refs[::2], pg_refs[1::2])]
+    acc = dot(jnp.concatenate(second, axis=0), jnp.concatenate(pgs, axis=1), TN)
+    acc_refs[0][...], acc_refs[1][...] = acc[:, :PART], acc[:, PART:]
     for i, scale_ref in enumerate((s1a_ref, s1b_ref)):
         first = gained(x1_ref[R * i : R * i + R], scale_ref, gain_ref)
         turned_ref[:, columns(i)] = jnp.transpose(first)
 
 
-def last_weight_kernel(acc_ref, turned_ref, pa_ref, pb_ref, out_ref, held, sems):
-    pgs = jnp.concatenate([pa_ref[...], pb_ref[...]], axis=0)
+def last_weight_kernel(acc0_ref, acc1_ref, turned_ref, *refs):
+    pg_refs, (out_ref, held, sems) = refs[:4], refs[4:]
+    pgs = [jnp.concatenate([r[...] for r in pair], axis=0) for pair in (pg_refs[:2], pg_refs[2:])]
     pieces = sems.shape[0]
     size = HALF // pieces
     copies = []
     for i in range(pieces):
-        rows = slice(i * size, i * size + size)
-        held[rows] = (acc_ref[rows] + dot(turned_ref[rows], pgs)).astype(BF16)
-        place = pl.ds(i * size, size)
-        copies.append(pltpu.make_async_copy(held.at[place], out_ref.at[place], sems.at[i]))
+        rows = pl.ds(i * size, size)
+        for half, acc_ref in enumerate((acc0_ref, acc1_ref)):
+            part = (acc_ref[rows] + dot(turned_ref[rows], pgs[half])).astype(BF16)
+            place = 0
+            for start, width in half_pieces(half):
+                held[rows, start : start + width] = part[:, place : place + width]
+                place += width
+        copies.append(pltpu.make_async_copy(held.at[rows], out_ref.at[rows], sems.at[i]))
         copies[-1].start()
     for copy in copies:
         copy.wait()
@@ -357,7 +381,9 @@
     return pl.BlockSpec(shape, lambda i: (0,) * len(shape))
 
 
-def call(kernel, args, outs, name, specs=None, out_specs=None, scratch=(), params=PARAMS, flops=1):
+def call(
+    kernel, args, outs, name, specs=None, out_specs=None, scratch=(), params=PARAMS, flops=1
+):
     specs = specs or {}
     return pl.pallas_call(
         kernel,
@@ -405,7 +431,7 @@
     return call(project_kernel, [x, gain, w_in], PARTS, "project")
 
 
-def attend(stream, turn, x, parts, layer, bias, trig, before):
+def attend(stream, turn, x, parts, layer, bias, trig, before, cut=1):
     recv, own, sums = parts
     seen = R * (stream + 1)
     shapes = [
@@ -414,7 +440,7 @@
         shape_of(F32, R, 128),
     ]
     if turn:
-        shapes += [shape_of(BF16, R, HEADS), shape_of(F32, R, HEADS)]
+        shapes += [shape_of(F32, R, HEADS)] + [shape_of(BF16, R, HEADS // cut)] * cut
     outs = call(
         partial(attend_kernel, stream, turn),
         [recv, own, sums, x, layer[1], layer[4], bias, *trig, *before], shapes, "attend",
@@ -423,30 +449,42 @@
     out, att, q, k, v, p, scale = outs[:7]
     kept = dict(x=x, att=att, q=q, kv=[k, v], p=p, scale=scale, out=out)
     if turn:
-        kept["msg"], kept["own"] = outs[7:]
+        kept["own"], kept["msgs"] = outs[7], outs[8:]
     return kept
 
 
-def back(stream, recv, own, kept, trig, kv, partials, layer=None):
-    args = [recv, own, kept["q"], kept["p"], *trig, *kv]
-    if not stream:
-        args += partials
-    shapes = [shape_of(BF16, R, JOINT)]
+def back(stream, halves, recvs, own, kept, trig, kv, given=None, layer=None, begun=None):
+    taken = dict(recvs, own=own, q=kept["q"], p=kept["p"], cos=trig[0], sin=trig[1])
+    taken.update(zip(("ka", "va", "kb", "vb"), kv))
+    taken.update(given or {})
+    outs = {"pg%d" % half: shape_of(BF16, R, PART) for half in halves}
     if stream:
-        shapes += [shape_of(F32, R, KEYS)] * 2
+        outs.update({n + str(h): shape_of(F32, R, KEYS // 2) for n in ("dk", "dv") for h in halves})
     if layer:
-        args += [layer[3], kept["x"], layer[2], kept["scale"], kept["out"]]
-        shapes.append(shape_of(BF16, R, HALF))
+        taken["w"] = layer[3]
+        if 1 in halves:
+            taken.update(x=kept["x"], gain=layer[2], scale=kept["scale"], up=kept["out"])
+            taken.update(begun or {})
+            outs["out"] = shape_of(BF16, R, HALF)
+        else:
+            outs.update(total=shape_of(F32, R, 128), grad=shape_of(F32, R, HALF))
+    names = [*taken, *outs]
+    done = call(
+        partial(attend_back_kernel, stream, halves, names), list(taken.values()),
+        list(outs.values()), "attend_back",
+    )
+    return dict(zip(outs, done))
+
+
+def output_back(up, layer, cut=1):
     return call(
-        partial(attend_back_kernel, stream, layer is not None), args, shapes, "attend_back"
-    )
-
-
-def output_back(up, layer):
-    return call(
-        output_back_kernel, [up, layer[4]], [shape_of(BF16, R, HEADS), shape_of(F32, R, HEADS)],
-        "output_back",
-    )
+        output_back_kernel, [up, layer[4]],
+        [shape_of(F32, R, HEADS)] + [shape_of(BF16, R, HEADS // cut)] * cut, "output_back",
+    )
+
+
+def only(outs, *names):
+    return {name: value for name, value in outs.items() if name.startswith(names)}
 
 
 def shards(activations, document_ids, joint_input_weights, output_weights, norm_gains):
@@ -485,33 +523,58 @@
     msg_b, own_b, sums_b = project(after(xb, msg_a), layer)
     recv_b = swap(msg_b)
     a2 = attend(0, True, xa, (recv_a, own_a, sums_a), layer, bias2, trig, [])
-    recv_a = swap(a2["msg"])
-    b2 = attend(1, True, xb, (recv_b, own_b, sums_b), layer, bias2, trig, a2["kv"])
-    recv_b = after(swap(b2["msg"]), recv_a)
-    pgb2, dka, dva, up = back(1, recv_b, b2["own"], b2, trig, a2["kv"] + b2["kv"], None, layer)
-    upb = hop(up, 1)
-    pga2, up = back(0, recv_a, a2["own"], a2, trig, a2["kv"], [dka, dva], layer)
-    upa = hop(up, 1)
-
-    msg_b, own_b = output_back(upb, layer)
+    recv_a = swap(a2["msgs"][0])
+    b2 = attend(
+        1, True, xb, (recv_b, own_b, sums_b), layer, bias2, trig, a2["kv"], cut=2
+    )
+    begun_out = call(
+        output_weight_kernel, [a2["att"], b2["att"], a2["out"], b2["out"]],
+        [shape_of(F32, HEADS, HALF)], "output_weights",
+    )[0]
+    recvs_b = [swap(msg) for msg in b2["msgs"]]
+    recvs_b[0] = after(recvs_b[0], recv_a, begun_out)
+    kv = a2["kv"] + b2["kv"]
+    first = back(1, (0,), {"recv0": recvs_b[0]}, b2["own"], b2, trig, kv, layer=layer)
+    pgb2 = back(
+        1, (1,), {"recv1": recvs_b[1]}, b2["own"], b2, trig, kv, layer=layer,
+        begun=only(first, "total", "grad"),
+    )
+    pgb2.update(only(first, "pg", "d"))
+    upb = hop(pgb2["out"], 1)
+    pga2 = back(
+        0, (0, 1), {"recv": recv_a}, a2["own"], a2, trig, a2["kv"], only(pgb2, "d"), layer
+    )
+    upa = hop(pga2["out"], 1)
+
+    *accs, turned = call(
+        early_weight_kernel,
+        [
+            x1, xa, xb, a1["scale"], b1["scale"], a2["scale"], b2["scale"], gain,
+            pga2["pg0"], pga2["pg1"], pgb2["pg0"], pgb2["pg1"],
+        ],
+        [shape_of(F32, HALF, PART)] * 2 + [shape_of(BF16, HALF, T)], "early_weights",
+    )
+    own_b, msg_b = output_back(after(upb, turned), layer)
     recv_b = swap(msg_b)
-    msg_a, own_a = output_back(after(upa, msg_b), layer)
-    recv_a = swap(msg_a)
-    acc, turned = call(
-        early_weight_kernel,
-        [x1, xa, xb, a1["scale"], b1["scale"], a2["scale"], b2["scale"], gain, pga2, pgb2],
-        [shape_of(F32, HALF, JOINT), shape_of(BF16, HALF, T)], "early_weights",
-    )
+    own_a, *msgs_a = output_back(after(upa, msg_b), layer, 2)
+    recvs_a = [swap(msg) for msg in msgs_a]
     (total_out,) = call(
-        output_weight_kernel,
-        [k["att"] for k in (a1, b1, a2, b2)] + [upa, upb, a2["out"], b2["out"]],
+        output_weight_kernel, [a1["att"], b1["att"], upa, upb, begun_out],
         [shape_of(BF16, HEADS, HALF)], "output_weights",
     )
-    pgb1, dka, dva = back(1, recv_b, own_b, b1, trig, a1["kv"] + b1["kv"], None)
-    (pga1,) = back(0, recv_a, own_a, a1, trig, a1["kv"], [dka, dva])
+    pgb1 = back(1, (0, 1), {"recv": recv_b}, own_b, b1, trig, a1["kv"] + b1["kv"])
+    pga1 = {}
+    for half in range(2):
+        pga1.update(
+            back(
+                0, (half,), {"recv%d" % half: recvs_a[half]}, own_a, a1, trig, a1["kv"],
+                only(pgb1, "dk%d" % half, "dv%d" % half),
+            )
+        )
     (total_in,) = call(
-        last_weight_kernel, [acc, turned, pga1, pgb1], [shape_of(BF16, HALF, JOINT)],
-        "last_weights", out_specs=[IN_HBM],
+        last_weight_kernel,
+        [*accs, turned, pga1["pg0"], pgb1["pg0"], pga1["pg1"], pgb1["pg1"]],
+        [shape_of(BF16, HALF, JOINT)], "last_weights", out_specs=[IN_HBM],
         scratch=[pltpu.VMEM((HALF, JOINT), BF16), pltpu.SemaphoreType.DMA((8,))],
     )
     return (total_in[None], total_out[None])

time: 97.4 us -> 96.5 us (level)
  waiting for transfers between devices: 38.6 us -> 29.1 us
  starting transfers between devices: 24.2 us -> 31.8 us
  Pallas kernels: 28.9 us -> 30 us
    ppermute x8 -> x10, starting transfers between devices: 11.7 us -> 19.4 us  [swap(): return lax.ppermute(value, 'stretch', [(0, 1), (1, 0)])]
    ppermute x8 -> x10, waiting for transfers between devices: 20.5 us -> 14 us  [swap(): return lax.ppermute(value, 'stretch', [(0, 1), (1, 0)])]
    ppermute x4, waiting for transfers between devices: 18.2 us -> 15.1 us  [hop(): lax.ppermute(value, 'blk', [(i, (i + step) % count) for i in range(count)])]
    pallas_call x18 -> x21, Pallas kernels: 28.9 us -> 30 us  [call(): pl.pallas_call(kernel, grid=(1,), in_specs=[specs.get(i) or block(*a.shap...]
  transfers between devices with their start and end apart: 12 -> 14, of which waited for: 9 -> 8; matrix products, arithmetic and copies ran while one was open for 1% -> 1% of each run, Pallas kernels for 19% -> 22%
where the time goes in v4:
time: 96.5 us; the launch traced here: 96.3 us
  starting transfers between devices  31.8 us (33%)
  Pallas kernels  30 us (31%)
  waiting for transfers between devices  29.1 us (30%)
  local copies, waits for them, and re-layouts  3.5 us (4%)
  between operations  1.07 us (1%)
    pallas_call x21, Pallas kernels, call(): pl.pallas_call(kernel, grid=(1,), in_specs=[specs.get(i) or block(*a.shap...  30 us
    ppermute x10, starting transfers between devices, swap(): return lax.ppermute(value, 'stretch', [(0, 1), (1, 0)])  19.4 us
    ppermute x4, waiting for transfers between devices, hop(): lax.ppermute(value, 'blk', [(i, (i + step) % count) for i in range(count)])  15.1 us
    ppermute x10, waiting for transfers between devices, swap(): return lax.ppermute(value, 'stretch', [(0, 1), (1, 0)])  14 us
    ppermute x4, starting transfers between devices, hop(): lax.ppermute(value, 'blk', [(i, (i + step) % count) for i in range(count)])  12.5 us
    unnamed x16, local copies, waits for them, and re-layouts  3.5 us
  transfers between devices with their start and end apart: 14, of which 8 were waited for; matrix products, arithmetic and copies ran while one was open for 1% of the time, Pallas kernels for 22%

profile of v4, /device:TPU:2, one launch (start us, length us, event | category | flops | bytes accessed | tf_op | source)
XLA Modules:
  0.0 96.3 jit_solution(506286895889131551)
XLA Ops:
  0.6 0.0 copy-start.6
  0.6 0.0 copy-start.7
  0.7 0.0 copy-start.5
  0.7 0.0 copy-start.4
  0.7 4.7 %project_first.1 = (bf16[128,1664]{1,0:T(8,128)(2,1)}, bf16[128,1664]{1,0:T(8,128)(2,1)}) custom-call(bf16[256,1024]{1,0:T(8,128)(2,1)} %x1_ref, bf16[1,1024]{1,0:T(2,128)(2,1)} %gain_ref.9, bf16[1024,1536]{1,0:T(8,128)(2,1)} %bitcast.6), custom_call_target="tpu_custom_call" | custom-call | flops 1 | bytes 1 | tf_op jit(solution)/shard_map/project_first/pallas_call | solution.py:388
  5.4 2.2 %collective-permute-start = (bf16[128,1664]{1,0:T(8,128)(2,1)}, bf16[128,1664]{1,0:T(8,128)(2,1)S(1)}, u32[]{:S(2)}, u32[]{:S(2)}) collective-permute-start(bf16[128,1664]{1,0:T(8,128)(2,1)} %get-tuple-element.94), channel_id=1, source_target_pairs={{0,1},{1,0},{2,3},{3,2},{4,5},{5,4},{6,7},{7,6},{8,9},{9,8},{10,11... | collective-permute-start | bytes 1277960 | tf_op jit(solution)/shard_map/ppermute | solution.py:402
  7.6 1.4 %collective-permute-start.2 = (bf16[128,1664]{1,0:T(8,128)(2,1)}, bf16[128,1664]{1,0:T(8,128)(2,1)S(1)}, u32[]{:S(2)}, u32[]{:S(2)}) collective-permute-start(bf16[128,1664]{1,0:T(8,128)(2,1)} %get-tuple-element.89), channel_id=1, source_target_pairs={{0,1},{1,0},{2,3},{3,2},{4,5},{5,4},{6,7},{7,6},{8,9},{9,8},{10,11... | collective-permute-start | bytes 1277960 | tf_op jit(solution)/shard_map/ppermute | solution.py:402
  9.0 0.8 dynamic-slice_convert_fusion
  9.9 0.0 copy-done.6
  9.9 0.0 copy-done.7
  9.9 0.1 prepare.1
  10.0 0.0 copy-done.5
  10.0 0.0 copy-done.4
  10.0 0.0 copy-start
  10.0 1.9 %copy-done = bf16[1,1024,1536]{2,1,0:T(8,128)(2,1)S(1)} copy-done((bf16[1,1024,1536]{2,1,0:T(8,128)(2,1)S(1)}, bf16[1,1024,1536]{2,1,0:T(8,128)(2,1)}, u32[]{:S(2)}) %copy-start) | copy-done | bytes 3145752
  11.9 0.0 copy-start.2
  11.9 1.6 %copy-done.2 = bf16[1,1024,1024]{2,1,0:T(8,128)(2,1)S(1)} copy-done((bf16[1,1024,1024]{2,1,0:T(8,128)(2,1)S(1)}, bf16[1,1024,1024]{2,1,0:T(8,128)(2,1)}, u32[]{:S(2)}) %copy-start.2) | copy-done | bytes 2097176
  13.5 1.8 %project_own.1 = (f32[128,1536]{1,0:T(8,128)S(1)}, f32[128,128]{1,0:T(8,128)S(1)}, f32[128,1536]{1,0:T(8,128)S(1)}, f32[128,128]{1,0:T(8,128)S(1)}, bf16[1536,10...) custom-call(bf16[256,1024]{1,0:T(8,128)(2,1)S(1)} %copy-done.4, bf16[1,1024]{1,0:T(2,128)(2,1)S(1)} %copy-done.5, ...), custom_call_target="tpu_custom_call" | custom-call | flops 1 | bytes 1 | tf_op jit(solution)/shard_map/project_own/pallas_call | solution.py:388
  15.3 4.6 %collective-permute-done.msg_ref = bf16[128,1664]{1,0:T(8,128)(2,1)S(1)} collective-permute-done((bf16[128,1664]{1,0:T(8,128)(2,1)}, bf16[128,1664]{1,0:T(8,128)(2,1)S(1)}, u32[]{:S(2)}, u32[]{:S(2)}) %collective-permute-start) | collective-permute-done | bytes 426016 | tf_op jit(solution)/shard_map/ppermute | solution.py:402
  19.9 0.0 copy-done.3
  19.9 1.4 %attend.4 = (bf16[128,1024]{1,0:T(8,128)(2,1)S(1)}, bf16[128,1024]{1,0:T(8,128)(2,1)S(1)}, bf16[128,1024]{1,0:T(8,128)(2,1)S(1)}, bf16[128,256]{1,0:T(8,128)(2,1...) custom-call(bf16[128,1664]{1,0:T(8,128)(2,1)S(1)} %collective-permute-done.msg_ref, ...), custom_call_target="tpu_custom_call" | custom-call | flops 1 | bytes 1 | tf_op jit(solution)/shard_map/attend/pallas_call | solution.py:388
  21.3 5.8 %collective-permute-start.1 = (bf16[128,1024]{1,0:T(8,128)(2,1)S(1)}, bf16[128,1024]{1,0:T(8,128)(2,1)S(1)}, u32[]{:S(2)}, u32[]{:S(2)}) collective-permute-start(bf16[128,1024]{1,0:T(8,128)(2,1)S(1)} %get-tuple-element.102), channel_id=1, source_target_pairs={{0,254},{2,0},{4,2},{6,4},{8,6},{10,8},{12,10},{14,12},{16,14},{18... | collective-permute-start | bytes 786440 | tf_op jit(solution)/shard_map/ppermute | solution.py:407
  27.1 3.9 %collective-permute-done.1.x_ref.refs_13_.x2a_ref = bf16[128,1024]{1,0:T(8,128)(2,1)S(1)} collective-permute-done((bf16[128,1024]{1,0:T(8,128)(2,1)S(1)}, bf16[128,1024]{1,0:T(8,128)(2,1)S(1)}, u32[]{:S(2)}, u32[]{:S(2)}) %collective-permute-start.1) | collective-permute-done | bytes 262176 | tf_op jit(solution)/shard_map/ppermute | solution.py:407
  31.1 0.0 copy-done.1
  31.1 0.6 project.2
  31.7 2.5 %collective-permute-start.4 = (bf16[128,1664]{1,0:T(8,128)(2,1)S(1)}, bf16[128,1664]{1,0:T(8,128)(2,1)S(1)}, u32[]{:S(2)}, u32[]{:S(2)}) collective-permute-start(bf16[128,1664]{1,0:T(8,128)(2,1)S(1)} %get-tuple-element.103), channel_id=1, source_target_pairs={{0,1},{1,0},{2,3},{3,2},{4,5},{5,4},{6,7},{7,6},{8,9},{9,8},{10,11... | collective-permute-start | bytes 1277960 | tf_op jit(solution)/shard_map/ppermute | solution.py:402
  34.1 0.0 collective-permute-done.2.msg_ref
  34.1 1.8 %attend.5 = (bf16[128,1024]{1,0:T(8,128)(2,1)S(1)}, bf16[128,1024]{1,0:T(8,128)(2,1)S(1)}, bf16[128,1024]{1,0:T(8,128)(2,1)S(1)}, bf16[128,256]{1,0:T(8,128)(2,1...) custom-call(bf16[128,1664]{1,0:T(8,128)(2,1)S(1)} %collective-permute-done.2.msg_ref, ...), custom_call_target="tpu_custom_call" | custom-call | flops 1 | bytes 1 | tf_op jit(solution)/shard_map/attend/pallas_call | solution.py:388
  35.9 6.5 %collective-permute-start.3 = (bf16[128,1024]{1,0:T(8,128)(2,1)S(1)}, bf16[128,1024]{1,0:T(8,128)(2,1)S(1)}, u32[]{:S(2)}, u32[]{:S(2)}) collective-permute-start(bf16[128,1024]{1,0:T(8,128)(2,1)S(1)} %get-tuple-element.109), channel_id=1, source_target_pairs={{0,254},{2,0},{4,2},{6,4},{8,6},{10,8},{12,10},{14,12},{16,14},{18... | collective-permute-start | bytes 786440 | tf_op jit(solution)/shard_map/ppermute | solution.py:407
  42.5 3.9 %collective-permute-done.3.x_ref.refs_11_.x2b_ref = bf16[128,1024]{1,0:T(8,128)(2,1)S(1)} collective-permute-done((bf16[128,1024]{1,0:T(8,128)(2,1)S(1)}, bf16[128,1024]{1,0:T(8,128)(2,1)S(1)}, u32[]{:S(2)}, u32[]{:S(2)}) %collective-permute-start.3) | collective-permute-done | bytes 262176 | tf_op jit(solution)/shard_map/ppermute | solution.py:407
  46.4 0.6 project.3
  47.0 0.1 collective-permute-start.5
  47.1 0.0 collective-permute-done.4.msg_ref
  47.1 1.7 %attend.6 = (bf16[128,1024]{1,0:T(8,128)(2,1)S(1)}, bf16[128,1024]{1,0:T(8,128)(2,1)S(1)}, bf16[128,1024]{1,0:T(8,128)(2,1)S(1)}, bf16[128,256]{1,0:T(8,128)(2,1...) custom-call(bf16[128,1664]{1,0:T(8,128)(2,1)S(1)} %collective-permut, ...), custom_call_target="tpu_custom_call" | custom-call | flops 10000000000 | bytes 1 | tf_op jit(solution)/shard_map/attend/pallas_call | solution.py:388
  48.9 3.8 %collective-permute-start.6 = (bf16[128,1024]{1,0:T(8,128)(2,1)S(1)}, bf16[128,1024]{1,0:T(8,128)(2,1)S(1)}, u32[]{:S(2)}, u32[]{:S(2)}) collective-permute-start(bf16[128,1024]{1,0:T(8,128)(2,1)S(1)} %get-tuple-element.123), channel_id=1, source_target_pairs={{0,1},{1,0},{2,3},{3,2},{4,5},{5,4},{6,7},{7,6},{8,9},{9,8},{10,11... | collective-permute-start | bytes 786440 | tf_op jit(solution)/shard_map/ppermute | solution.py:402
  52.6 6.9 %collective-permute-done.5.msg_ref = bf16[128,1664]{1,0:T(8,128)(2,1)S(1)} collective-permute-done((bf16[128,1664]{1,0:T(8,128)(2,1)S(1)}, bf16[128,1664]{1,0:T(8,128)(2,1)S(1)}, u32[]{:S(2)}, u32[]{:S(2)}) %collective-permute-start.5) | collective-permute-done | bytes 426016 | tf_op jit(solution)/shard_map/ppermute | solution.py:402
  59.5 2.1 %attend.7 = (bf16[128,1024]{1,0:T(8,128)(2,1)S(1)}, bf16[128,1024]{1,0:T(8,128)(2,1)S(1)}, bf16[128,1024]{1,0:T(8,128)(2,1)S(1)}, bf16[128,256]{1,0:T(8,128)(2,1...) custom-call(bf16[128,1664]{1,0:T(8,128)(2,1)S(1)} %collective-permut, ...), custom_call_target="tpu_custom_call" | custom-call | flops 1 | bytes 1 | tf_op jit(solution)/shard_map/attend/pallas_call | solution.py:388
  61.6 0.1 collective-permute-start.8
  61.7 3.5 %collective-permute-start.7 = (bf16[128,512]{1,0:T(8,128)(2,1)S(1)}, bf16[128,512]{1,0:T(8,128)(2,1)S(1)}, u32[]{:S(2)}, u32[]{:S(2)}) collective-permute-start(bf16[128,512]{1,0:T(8,128)(2,1)S(1)} %get-tuple-element.127), channel_id=1, source_target_pairs={{0,1},{1,0},{2,3},{3,2},{4,5},{5,4},{6,7},{7,6},{8,9},{9,8},{10,11... | collective-permute-start | bytes 393224 | tf_op jit(solution)/shard_map/ppermute | solution.py:402
  65.3 0.7 output_weights.2.refs_4_
  66.0 0.0 collective-permute-done.6.refs_0_
  66.0 2.2 %collective-permute-done.8.refs_0_ = bf16[128,512]{1,0:T(8,128)(2,1)S(1)} collective-permute-done((bf16[128,512]{1,0:T(8,128)(2,1)S(1)}, bf16[128,512]{1,0:T(8,128)(2,1)S(1)}, u32[]{:S(2)}, u32[]{:S(2)}) %collective-permute-start.8) | collective-permute-done | bytes 131104 | tf_op jit(solution)/shard_map/ppermute | solution.py:402
  68.2 1.4 %attend_back.6 = (bf16[128,768]{1,0:T(8,128)(2,1)S(1)}, f32[128,128]{1,0:T(8,128)S(1)}, f32[128,128]{1,0:T(8,128)S(1)}, f32[128,128]{1,0:T(8,128)S(1)}, f32[128,1024]{1,0:T(8,128)S(1)}) custom-call(bf16[128,512]{1,0:T(8,128)(2,1)S(1)} %collective-permute-done.8.refs_0_, f32[128,1024]{1,0:T(8,128)S(1)} %get-tuple-element.128.refs_1_, ...), custom_call_target="tpu_custom_call" | custom-call | flops 1 | bytes 1 | tf_op jit(solution)/shard_map/attend_back/pallas_call | solution.py:388
  69.6 0.0 collective-permute-done.7.refs_0_
  69.6 1.4 %attend_back.7 = (bf16[128,768]{1,0:T(8,128)(2,1)S(1)}, f32[128,128]{1,0:T(8,128)S(1)}, f32[128,128]{1,0:T(8,128)S(1)}, bf16[128,1024]{1,0:T(8,128)(2,1)S(1)}) custom-call(bf16[128,512]{1,0:T(8,128)(2,1)S(1)} %collective-permute-done.7.refs_0_, f32[128,1024]{1,0:T(8,128)S(1)} %get-tuple-element.128.refs_1_, ...), custom_call_target="tpu_custom_call" | custom-call | flops 1 | bytes 1 | tf_op jit(solution)/shard_map/attend_back/pallas_call | solution.py:388
  71.0 0.1 collective-permute-start.10
  71.1 1.9 %attend_back.8 = (bf16[128,768]{1,0:T(8,128)(2,1)S(1)}, bf16[128,768]{1,0:T(8,128)(2,1)S(1)}, bf16[128,1024]{1,0:T(8,128)(2,1)S(1)}) custom-call(bf16[128,1024]{1,0:T(8,128)(2,1)S(1)} %collective-permute-done.6.refs_0_, f32[128,1024]{1,0:T(8,128)S(1)} %get-tuple-element.124.refs_1_, bf16[128,1024]{1,0:T(8,128)(2,1)S(1)} %get-tuple-element.125.refs_2_, ...), custom_call_target="tpu_custom_call" | custom-call | flops 1 | bytes 1 | tf_op jit(solution)/shard_map/attend_back/pallas_call | solution.py:388
  73.0 0.1 collective-permute-start.9
  73.1 1.0 %early_weights.1 = (f32[1024,768]{1,0:T(8,128)S(1)}, f32[1024,768]{1,0:T(8,128)S(1)}, bf16[1024,256]{1,0:T(8,128)(2,1)S(1)}) custom-call(bf16[256,1024]{1,0:T(8,128)(2,1)S(1)} %copy-done.4, bf16[128,1024]{1,0:T(8,128)(2,1)S(1)} %collective-permute-done.1.x_ref.refs_13_.x2a_ref, bf16[128,1024]{1,0:T(8,128)(2,1)S(1)} %collective-permute-done.3.x_ref.refs_11_.x2b_ref, ...), custom_call_target="tpu_custom_call" | custom-call | flops 1 | bytes 1 | tf_op jit(solution)/shard_map/early_weights/pallas_call | solution.py:388
  74.2 7.1 %collective-permute-done.10.up_ref.refs_3_ = bf16[128,1024]{1,0:T(8,128)(2,1)S(1)} collective-permute-done((bf16[128,1024]{1,0:T(8,128)(2,1)S(1)}, bf16[128,1024]{1,0:T(8,128)(2,1)S(1)}, u32[]{:S(2)}, u32[]{:S(2)}) %collective-permute-start.10) | collective-permute-done | bytes 262176 | tf_op jit(solution)/shard_map/ppermute | solution.py:407
  81.2 0.5 output_back.2
  81.7 2.2 %collective-permute-start.12 = (bf16[128,1024]{1,0:T(8,128)(2,1)S(1)}, bf16[128,1024]{1,0:T(8,128)(2,1)S(1)}, u32[]{:S(2)}, u32[]{:S(2)}) collective-permute-start(bf16[128,1024]{1,0:T(8,128)(2,1)S(1)} %get-tuple-element.156), channel_id=1, source_target_pairs={{0,1},{1,0},{2,3},{3,2},{4,5},{5,4},{6,7},{7,6},{8,9},{9,8},{10,11... | collective-permute-start | bytes 786440 | tf_op jit(solution)/shard_map/ppermute | solution.py:402
  83.9 0.1 collective-permute-done.9.up_ref.refs_2_
  84.1 0.5 output_back.3
  84.5 2.2 %collective-permute-start.11 = (bf16[128,512]{1,0:T(8,128)(2,1)S(1)}, bf16[128,512]{1,0:T(8,128)(2,1)S(1)}, u32[]{:S(2)}, u32[]{:S(2)}) collective-permute-start(bf16[128,512]{1,0:T(8,128)(2,1)S(1)} %get-tuple-element.158), channel_id=1, source_target_pairs={{0,1},{1,0},{2,3},{3,2},{4,5},{5,4},{6,7},{7,6},{8,9},{9,8},{10,11... | collective-permute-start | bytes 393224 | tf_op jit(solution)/shard_map/ppermute | solution.py:402
  86.7 1.4 %collective-permute-start.13 = (bf16[128,512]{1,0:T(8,128)(2,1)S(1)}, bf16[128,512]{1,0:T(8,128)(2,1)S(1)}, u32[]{:S(2)}, u32[]{:S(2)}) collective-permute-start(bf16[128,512]{1,0:T(8,128)(2,1)S(1)} %get-tuple-element.170), channel_id=1, source_target_pairs={{0,1},{1,0},{2,3},{3,2},{4,5},{5,4},{6,7},{7,6},{8,9},{9,8},{10,11... | collective-permute-start | bytes 393224 | tf_op jit(solution)/shard_map/ppermute | solution.py:402
  88.1 2.1 %output_weights.3 = bf16[1024,1024]{1,0:T(8,128)(2,1)} custom-call(bf16[128,1024]{1,0:T(8,128)(2,1)S(1)} %get-tuple-element.174.refs_0_, bf16[128,1024]{1,0:T(8,128)(2,1)S(1)} %get-tuple-element.175.refs_1_, bf16[128,1024]{1,0:T(8,128)(2,1)S(1)} %collective-permute-done.9.up_ref.refs_2_, bf16[128,1024]{1,0:T(8,128)(2,1)S(1)} %collective-permute-done.10.up_ref.refs_3_, ...), custom_call_target="tpu_custom_call" | custom-call | flops 1 | bytes 1 | tf_op jit(solution)/shard_map/output_weights/pallas_call | solution.py:388
  90.2 0.0 collective-permute-done.12.refs_0_
  90.2 1.8 %attend_back.9 = (bf16[128,768]{1,0:T(8,128)(2,1)S(1)}, bf16[128,768]{1,0:T(8,128)(2,1)S(1)}, f32[128,128]{1,0:T(8,128)S(1)}, f32[128,128]{1,0:T(8,128)S(1)}, f3...) custom-call(bf16[128,1024]{1,0:T(8,128)(2,1)S(1)} %collective-permute-done.12.refs_0_, ...), custom_call_target="tpu_custom_call" | custom-call | flops 1 | bytes 1 | tf_op jit(solution)/shard_map/attend_back/pallas_call | solution.py:388
  92.1 0.0 collective-permute-done.11.refs_0_
  92.1 0.9 attend_back.10.refs_0_
  93.0 0.2 collective-permute-done.13.refs_0_
  93.2 0.9 attend_back.11.refs_2_
  94.1 2.0 %last_weights.1 = bf16[1024,1536]{1,0:T(8,128)(2,1)} custom-call(f32[1024,768]{1,0:T(8,128)S(1)} %get-tuple-element.150.acc0_ref, f32[1024,768]{1,0:T(8,128)S(1)} %get-tuple-element.151.acc1_ref, bf16[1024,256]{1,0:T(8,128)(2,1)S(1)} %get-tuple-element.152.turned_ref, bf16[128,768]{1,0:T(8,128)(2,1)S(1)} %attend_back.10.refs_0_, ...), custom_call_target="tpu_custom_call" | custom-call | flops 1 | bytes 1 | tf_op jit(solution)/shard_map/last_weights/pallas_call | solution.py:388
  (2 shorter events, 0.0 us)
Async XLA Ops:
  0.6 9.2 %copy-start.6 = (f32[256,128]{1,0:T(8,128)S(1)}, f32[256,128]{1,0:T(8,128)}, u32[]{:S(2)}) copy-start(f32[256,128]{1,0:T(8,128)} %constant.23.clone.sin_in) | copy-start | bytes 393220
  0.6 9.2 %copy-start.7 = (f32[256,128]{1,0:T(8,128)S(1)}, f32[256,128]{1,0:T(8,128)}, u32[]{:S(2)}) copy-start(f32[256,128]{1,0:T(8,128)} %constant.22.clone.cos_in) | copy-start | bytes 393220
  0.7 9.4 %copy-start.5 = (bf16[1,1024]{1,0:T(2,128)(2,1)S(1)}, bf16[1,1024]{1,0:T(2,128)(2,1)}, u32[]{:S(2)}) copy-start(bf16[1,1024]{1,0:T(2,128)(2,1)} %gain_ref.9) | copy-start | bytes 6148
  0.7 9.4 %copy-start.4 = (bf16[256,1024]{1,0:T(8,128)(2,1)S(1)}, bf16[256,1024]{1,0:T(8,128)(2,1)}, u32[]{:S(2)}) copy-start(bf16[256,1024]{1,0:T(8,128)(2,1)} %x1_ref) | copy-start | bytes 1572868
  5.4 14.5 %collective-permute-start = (bf16[128,1664]{1,0:T(8,128)(2,1)}, bf16[128,1664]{1,0:T(8,128)(2,1)S(1)}, u32[]{:S(2)}, u32[]{:S(2)}) collective-permute-start(bf16[128,1664]{1,0:T(8,128)(2,1)} %get-tuple-element.94), channel_id=1, source_target_pairs={{0,1},{1,0},{2,3},{3,2},{4,5},{5,4},{6,7},{7,6},{8,9},{9,8},{10,11... | collective-permute-start | bytes 1277960 | tf_op jit(solution)/shard_map/ppermute | solution.py:402
  7.6 26.5 %collective-permute-start.2 = (bf16[128,1664]{1,0:T(8,128)(2,1)}, bf16[128,1664]{1,0:T(8,128)(2,1)S(1)}, u32[]{:S(2)}, u32[]{:S(2)}) collective-permute-start(bf16[128,1664]{1,0:T(8,128)(2,1)} %get-tuple-element.89), channel_id=1, source_target_pairs={{0,1},{1,0},{2,3},{3,2},{4,5},{5,4},{6,7},{7,6},{8,9},{9,8},{10,11... | collective-permute-start | bytes 1277960 | tf_op jit(solution)/shard_map/ppermute | solution.py:402
  10.0 1.9 %copy-start = (bf16[1,1024,1536]{2,1,0:T(8,128)(2,1)S(1)}, bf16[1,1024,1536]{2,1,0:T(8,128)(2,1)}, u32[]{:S(2)}) copy-start(bf16[1,1024,1536]{2,1,0:T(8,128)(2,1)} %param.9) | copy-start | bytes 9437188
  11.9 1.6 %copy-start.2 = (bf16[1,1024,1024]{2,1,0:T(8,128)(2,1)S(1)}, bf16[1,1024,1024]{2,1,0:T(8,128)(2,1)}, u32[]{:S(2)}) copy-start(bf16[1,1024,1024]{2,1,0:T(8,128)(2,1)} %param.10) | copy-start | bytes 6291460
  13.5 6.4 %copy-start.3 = (bf16[1,1024,1024]{2,1,0:T(8,128)(2,1)S(1)}, bf16[1,1024,1024]{2,1,0:T(8,128)(2,1)}, u32[]{:S(2)}) copy-start(bf16[1,1024,1024]{2,1,0:T(8,128)(2,1)} %param.10) | copy-start | bytes 6291460
  19.9 11.1 %copy-start.1 = (bf16[1,1024,1536]{2,1,0:T(8,128)(2,1)S(1)}, bf16[1,1024,1536]{2,1,0:T(8,128)(2,1)}, u32[]{:S(2)}) copy-start(bf16[1,1024,1536]{2,1,0:T(8,128)(2,1)} %param.9) | copy-start | bytes 9437188
  21.3 9.7 %collective-permute-start.1 = (bf16[128,1024]{1,0:T(8,128)(2,1)S(1)}, bf16[128,1024]{1,0:T(8,128)(2,1)S(1)}, u32[]{:S(2)}, u32[]{:S(2)}) collective-permute-start(bf16[128,1024]{1,0:T(8,128)(2,1)S(1)} %get-tuple-element.102), channel_id=1, source_target_pairs={{0,254},{2,0},{4,2},{6,4},{8,6},{10,8},{12,10},{14,12},{16,14},{18... | collective-permute-start | bytes 786440 | tf_op jit(solution)/shard_map/ppermute | solution.py:407
  31.7 15.4 %collective-permute-start.4 = (bf16[128,1664]{1,0:T(8,128)(2,1)S(1)}, bf16[128,1664]{1,0:T(8,128)(2,1)S(1)}, u32[]{:S(2)}, u32[]{:S(2)}) collective-permute-start(bf16[128,1664]{1,0:T(8,128)(2,1)S(1)} %get-tuple-element.103), channel_id=1, source_target_pairs={{0,1},{1,0},{2,3},{3,2},{4,5},{5,4},{6,7},{7,6},{8,9},{9,8},{10,11... | collective-permute-start | bytes 1277960 | tf_op jit(solution)/shard_map/ppermute | solution.py:402
  35.9 10.5 %collective-permute-start.3 = (bf16[128,1024]{1,0:T(8,128)(2,1)S(1)}, bf16[128,1024]{1,0:T(8,128)(2,1)S(1)}, u32[]{:S(2)}, u32[]{:S(2)}) collective-permute-start(bf16[128,1024]{1,0:T(8,128)(2,1)S(1)} %get-tuple-element.109), channel_id=1, source_target_pairs={{0,254},{2,0},{4,2},{6,4},{8,6},{10,8},{12,10},{14,12},{16,14},{18... | collective-permute-start | bytes 786440 | tf_op jit(solution)/shard_map/ppermute | solution.py:407
  47.0 12.5 %collective-permute-start.5 = (bf16[128,1664]{1,0:T(8,128)(2,1)S(1)}, bf16[128,1664]{1,0:T(8,128)(2,1)S(1)}, u32[]{:S(2)}, u32[]{:S(2)}) collective-permute-start(bf16[128,1664]{1,0:T(8,128)(2,1)S(1)} %get-tuple-element.117), channel_id=1, source_target_pairs={{0,1},{1,0},{2,3},{3,2},{4,5},{5,4},{6,7},{7,6},{8,9},{9,8},{10,11... | collective-permute-start | bytes 1277960 | tf_op jit(solution)/shard_map/ppermute | solution.py:402
  48.9 17.1 %collective-permute-start.6 = (bf16[128,1024]{1,0:T(8,128)(2,1)S(1)}, bf16[128,1024]{1,0:T(8,128)(2,1)S(1)}, u32[]{:S(2)}, u32[]{:S(2)}) collective-permute-start(bf16[128,1024]{1,0:T(8,128)(2,1)S(1)} %get-tuple-element.123), channel_id=1, source_target_pairs={{0,1},{1,0},{2,3},{3,2},{4,5},{5,4},{6,7},{7,6},{8,9},{9,8},{10,11... | collective-permute-start | bytes 786440 | tf_op jit(solution)/shard_map/ppermute | solution.py:402
  61.6 6.6 %collective-permute-start.8 = (bf16[128,512]{1,0:T(8,128)(2,1)S(1)}, bf16[128,512]{1,0:T(8,128)(2,1)S(1)}, u32[]{:S(2)}, u32[]{:S(2)}) collective-permute-start(bf16[128,512]{1,0:T(8,128)(2,1)S(1)} %get-tuple-element.135), channel_id=1, source_target_pairs={{0,1},{1,0},{2,3},{3,2},{4,5},{5,4},{6,7},{7,6},{8,9},{9,8},{10,11... | collective-permute-start | bytes 393224 | tf_op jit(solution)/shard_map/ppermute | solution.py:402
  61.7 7.9 %collective-permute-start.7 = (bf16[128,512]{1,0:T(8,128)(2,1)S(1)}, bf16[128,512]{1,0:T(8,128)(2,1)S(1)}, u32[]{:S(2)}, u32[]{:S(2)}) collective-permute-start(bf16[128,512]{1,0:T(8,128)(2,1)S(1)} %get-tuple-element.127), channel_id=1, source_target_pairs={{0,1},{1,0},{2,3},{3,2},{4,5},{5,4},{6,7},{7,6},{8,9},{9,8},{10,11... | collective-permute-start | bytes 393224 | tf_op jit(solution)/shard_map/ppermute | solution.py:402
  71.0 10.2 %collective-permute-start.10 = (bf16[128,1024]{1,0:T(8,128)(2,1)S(1)}, bf16[128,1024]{1,0:T(8,128)(2,1)S(1)}, u32[]{:S(2)}, u32[]{:S(2)}) collective-permute-start(bf16[128,1024]{1,0:T(8,128)(2,1)S(1)} %get-tuple-element.154), channel_id=1, source_target_pairs={{0,2},{2,4},{4,6},{6,8},{8,10},{10,12},{12,14},{14,16},{16,18},{18... | collective-permute-start | bytes 786440 | tf_op jit(solution)/shard_map/ppermute | solution.py:407
  73.0 11.0 %collective-permute-start.9 = (bf16[128,1024]{1,0:T(8,128)(2,1)S(1)}, bf16[128,1024]{1,0:T(8,128)(2,1)S(1)}, u32[]{:S(2)}, u32[]{:S(2)}) collective-permute-start(bf16[128,1024]{1,0:T(8,128)(2,1)S(1)} %get-tuple-element.153), channel_id=1, source_target_pairs={{0,2},{2,4},{4,6},{6,8},{8,10},{10,12},{12,14},{14,16},{16,18},{18... | collective-permute-start | bytes 786440 | tf_op jit(solution)/shard_map/ppermute | solution.py:407
  81.7 8.5 %collective-permute-start.12 = (bf16[128,1024]{1,0:T(8,128)(2,1)S(1)}, bf16[128,1024]{1,0:T(8,128)(2,1)S(1)}, u32[]{:S(2)}, u32[]{:S(2)}) collective-permute-start(bf16[128,1024]{1,0:T(8,128)(2,1)S(1)} %get-tuple-element.156), channel_id=1, source_target_pairs={{0,1},{1,0},{2,3},{3,2},{4,5},{5,4},{6,7},{7,6},{8,9},{9,8},{10,11... | collective-permute-start | bytes 786440 | tf_op jit(solution)/shard_map/ppermute | solution.py:402
  84.5 7.5 %collective-permute-start.11 = (bf16[128,512]{1,0:T(8,128)(2,1)S(1)}, bf16[128,512]{1,0:T(8,128)(2,1)S(1)}, u32[]{:S(2)}, u32[]{:S(2)}) collective-permute-start(bf16[128,512]{1,0:T(8,128)(2,1)S(1)} %get-tuple-element.158), channel_id=1, source_target_pairs={{0,1},{1,0},{2,3},{3,2},{4,5},{5,4},{6,7},{7,6},{8,9},{9,8},{10,11... | collective-permute-start | bytes 393224 | tf_op jit(solution)/shard_map/ppermute | solution.py:402
  86.7 6.5 %collective-permute-start.13 = (bf16[128,512]{1,0:T(8,128)(2,1)S(1)}, bf16[128,512]{1,0:T(8,128)(2,1)S(1)}, u32[]{:S(2)}, u32[]{:S(2)}) collective-permute-start(bf16[128,512]{1,0:T(8,128)(2,1)S(1)} %get-tuple-element.170), channel_id=1, source_target_pairs={{0,1},{1,0},{2,3},{3,2},{4,5},{5,4},{6,7},{7,6},{8,9},{9,8},{10,11... | collective-permute-start | bytes 393224 | tf_op jit(solution)/shard_map/ppermute | solution.py:402

commit v5 on v4

--- a/solution.py
+++ b/solution.py
@@ -65,29 +65,41 @@
 
 
 def project_first_kernel(x_in, gain_ref, w_in, *rest):
-    outs, (x_ref, w_ref, held, x_sem, w_sems) = rest[:2], rest[2:]
+    outs, (x_ref, w_ref, held, x_sem, w_sems, out_sems) = rest[:2], rest[2:]
     pieces = w_sems.shape[0]
-    size = HALF // pieces
+    size = JOINT // pieces
     copies = [pltpu.make_async_copy(x_in, x_ref, x_sem)]
     for i in range(pieces):
-        rows = pl.ds(i * size, size)
-        copies.append(pltpu.make_async_copy(w_in.at[rows], w_ref.at[rows], w_sems.at[i]))
+        cols = pl.ds(i * size, size)
+        copies.append(pltpu.make_async_copy(w_in.at[:, cols], w_ref.at[:, cols], w_sems.at[i]))
     for copy in copies:
         copy.start()
+    sent = []
+
+    def send(piece, cols):
+        for stream in range(2):
+            rows = pl.ds(R * stream, R)
+            sent.append(
+                pltpu.make_async_copy(
+                    held.at[rows, cols], outs[stream].at[:, cols], out_sems.at[stream, piece]
+                )
+            )
+            sent[-1].start()
+
     copies[0].wait()
     x = x_ref[...].astype(F32)
     normed = (x * gain_ref[...].astype(F32)).astype(BF16)
     for stream in range(2):
-        put_sums(x[R * stream : R * stream + R], outs[stream])
+        rows = slice(R * stream, R * stream + R)
+        put_sums(x[rows], held.at[rows])
+    send(pieces, pl.ds(JOINT, 128))
     for i in range(pieces):
         copies[1 + i].wait()
-        part = dot(normed[:, i * size : i * size + size], w_ref[i * size : i * size + size, :])
-        if i:
-            part = held[...] + part
-        if i < pieces - 1:
-            held[...] = part
-    for stream in range(2):
-        outs[stream][:, :JOINT] = part[R * stream : R * stream + R].astype(BF16)
+        cols = slice(i * size, i * size + size)
+        held[:, cols] = dot(normed, w_ref[:, cols]).astype(BF16)
+        send(i, pl.ds(i * size, size))
+    for copy in sent:
+        copy.wait()
 
 
 def half_pieces(half):
@@ -322,13 +334,26 @@
     put_message(own, msg_refs)
 
 
-def output_weight_kernel(*refs):
-    att = jnp.concatenate([refs[0][...], refs[1][...]], axis=0)
-    up = jnp.concatenate([refs[2][...], refs[3][...]], axis=0)
-    out = dot(att, up, TN)
-    if len(refs) > 5:
-        out = out + refs[4][...]
-    refs[-1][...] = out.astype(refs[-1].dtype)
+def early_output_kernel(att_a_ref, att_b_ref, up_a_ref, up_b_ref, acc_ref):
+    att = jnp.concatenate([att_a_ref[...], att_b_ref[...]], axis=0)
+    acc_ref[...] = dot(att, jnp.concatenate([up_a_ref[...], up_b_ref[...]], axis=0), TN)
+
+
+def output_weight_kernel(
+    att_a_ref, att_b_ref, up_a_ref, up_b_ref, acc_ref, out_ref, held, sems
+):
+    up = jnp.concatenate([up_a_ref[...], up_b_ref[...]], axis=0)
+    pieces = sems.shape[0]
+    size = HEADS // pieces
+    copies = []
+    for i in range(pieces):
+        rows = pl.ds(i * size, size)
+        att = jnp.concatenate([att_a_ref[:, rows], att_b_ref[:, rows]], axis=0)
+        held[rows] = (acc_ref[rows] + dot(att, up, TN)).astype(BF16)
+        copies.append(pltpu.make_async_copy(held.at[rows], out_ref.at[rows], sems.at[i]))
+        copies[-1].start()
+    for copy in copies:
+        copy.wait()
 
 
 def gained(x, scale_ref, gain_ref):
@@ -418,10 +443,11 @@
 def project_first(x, w_in, gain):
     return call(
         project_first_kernel, [x, gain, w_in], PARTS[:1] * 2, "project_first", params=FIRST,
-        specs={0: IN_HBM, 2: IN_HBM},
+        specs={0: IN_HBM, 2: IN_HBM}, out_specs=[IN_HBM] * 2,
         scratch=[
             pltpu.VMEM((T, HALF), BF16), pltpu.VMEM((HALF, JOINT), BF16),
-            pltpu.VMEM((T, JOINT), F32), pltpu.SemaphoreType.DMA, pltpu.SemaphoreType.DMA((2,)),
+            pltpu.VMEM((T, JOINT + 128), BF16), pltpu.SemaphoreType.DMA,
+            pltpu.SemaphoreType.DMA((3,)), pltpu.SemaphoreType.DMA((2, 4)),
         ],
     )
 
@@ -528,8 +554,8 @@
         1, True, xb, (recv_b, own_b, sums_b), layer, bias2, trig, a2["kv"], cut=2
     )
     begun_out = call(
-        output_weight_kernel, [a2["att"], b2["att"], a2["out"], b2["out"]],
-        [shape_of(F32, HEADS, HALF)], "output_weights",
+        early_output_kernel, [a2["att"], b2["att"], a2["out"], b2["out"]],
+        [shape_of(F32, HEADS, HALF)], "early_output",
     )[0]
     recvs_b = [swap(msg) for msg in b2["msgs"]]
     recvs_b[0] = after(recvs_b[0], recv_a, begun_out)
@@ -560,7 +586,8 @@
     recvs_a = [swap(msg) for msg in msgs_a]
     (total_out,) = call(
         output_weight_kernel, [a1["att"], b1["att"], upa, upb, begun_out],
-        [shape_of(BF16, HEADS, HALF)], "output_weights",
+        [shape_of(BF16, HEADS, HALF)], "output_weights", out_specs=[IN_HBM],
+        scratch=[pltpu.VMEM((HEADS, HALF), BF16), pltpu.SemaphoreType.DMA((8,))],
     )
     pgb1 = back(1, (0, 1), {"recv": recv_b}, own_b, b1, trig, a1["kv"] + b1["kv"])
     pga1 = {}

time: 96.5 us -> 96.7 us (level)
  transfers between devices with their start and end apart: 14 -> 14, of which waited for: 8 -> 8; matrix products, arithmetic and copies ran while one was open for 1% -> 1% of each run, Pallas kernels for 22% -> 21%
where the time goes in v5:
time: 96.7 us; the launch traced here: 96.5 us
  starting transfers between devices  31.9 us (33%)
  Pallas kernels  29.8 us (31%)
  waiting for transfers between devices  29.5 us (31%)
  local copies, waits for them, and re-layouts  3.5 us (4%)
  between operations  1.08 us (1%)
    pallas_call x21, Pallas kernels, call(): pl.pallas_call(kernel, grid=(1,), in_specs=[specs.get(i) or block(*a.shap...  29.8 us
    ppermute x10, starting transfers between devices, swap(): return lax.ppermute(value, 'stretch', [(0, 1), (1, 0)])  19.4 us
    ppermute x4, waiting for transfers between devices, hop(): lax.ppermute(value, 'blk', [(i, (i + step) % count) for i in range(count)])  15.1 us
    ppermute x10, waiting for transfers between devices, swap(): return lax.ppermute(value, 'stretch', [(0, 1), (1, 0)])  14.4 us
    ppermute x4, starting transfers between devices, hop(): lax.ppermute(value, 'blk', [(i, (i + step) % count) for i in range(count)])  12.5 us
    unnamed x16, local copies, waits for them, and re-layouts  3.5 us
  transfers between devices with their start and end apart: 14, of which 8 were waited for; matrix products, arithmetic and copies ran while one was open for 1% of the time, Pallas kernels for 21%

profile of v5, /device:TPU:2, one launch (start us, length us, event | category | flops | bytes accessed | tf_op | source)
XLA Modules:
  0.0 96.5 jit_solution(4142346745992067584)
XLA Ops:
  0.6 0.0 copy-start.6
  0.6 0.0 copy-start.7
  0.7 0.0 copy-start.5
  0.7 0.0 copy-start.4
  0.7 4.9 %project_first.1 = (bf16[128,1664]{1,0:T(8,128)(2,1)}, bf16[128,1664]{1,0:T(8,128)(2,1)}) custom-call(bf16[256,1024]{1,0:T(8,128)(2,1)} %x1_ref, bf16[1,1024]{1,0:T(2,128)(2,1)} %gain_ref.9, bf16[1024,1536]{1,0:T(8,128)(2,1)} %bitcast.6), custom_call_target="tpu_custom_call" | custom-call | flops 1 | bytes 1 | tf_op jit(solution)/shard_map/project_first/pallas_call | solution.py:413
  5.6 2.2 %collective-permute-start = (bf16[128,1664]{1,0:T(8,128)(2,1)}, bf16[128,1664]{1,0:T(8,128)(2,1)S(1)}, u32[]{:S(2)}, u32[]{:S(2)}) collective-permute-start(bf16[128,1664]{1,0:T(8,128)(2,1)} %get-tuple-element.94), channel_id=1, source_target_pairs={{0,1},{1,0},{2,3},{3,2},{4,5},{5,4},{6,7},{7,6},{8,9},{9,8},{10,11... | collective-permute-start | bytes 1277960 | tf_op jit(solution)/shard_map/ppermute | solution.py:427
  7.8 1.4 %collective-permute-start.2 = (bf16[128,1664]{1,0:T(8,128)(2,1)}, bf16[128,1664]{1,0:T(8,128)(2,1)S(1)}, u32[]{:S(2)}, u32[]{:S(2)}) collective-permute-start(bf16[128,1664]{1,0:T(8,128)(2,1)} %get-tuple-element.89), channel_id=1, source_target_pairs={{0,1},{1,0},{2,3},{3,2},{4,5},{5,4},{6,7},{7,6},{8,9},{9,8},{10,11... | collective-permute-start | bytes 1277960 | tf_op jit(solution)/shard_map/ppermute | solution.py:427
  9.2 0.8 dynamic-slice_convert_fusion
  10.1 0.0 copy-done.6
  10.1 0.0 copy-done.7
  10.1 0.1 prepare.1
  10.2 0.0 copy-done.5
  10.2 0.0 copy-done.4
  10.3 0.0 copy-start
  10.3 1.9 %copy-done = bf16[1,1024,1536]{2,1,0:T(8,128)(2,1)S(1)} copy-done((bf16[1,1024,1536]{2,1,0:T(8,128)(2,1)S(1)}, bf16[1,1024,1536]{2,1,0:T(8,128)(2,1)}, u32[]{:S(2)}) %copy-start) | copy-done | bytes 3145752
  12.1 0.0 copy-start.2
  12.1 1.6 %copy-done.2 = bf16[1,1024,1024]{2,1,0:T(8,128)(2,1)S(1)} copy-done((bf16[1,1024,1024]{2,1,0:T(8,128)(2,1)S(1)}, bf16[1,1024,1024]{2,1,0:T(8,128)(2,1)}, u32[]{:S(2)}) %copy-start.2) | copy-done | bytes 2097176
  13.7 1.8 %project_own.1 = (f32[128,1536]{1,0:T(8,128)S(1)}, f32[128,128]{1,0:T(8,128)S(1)}, f32[128,1536]{1,0:T(8,128)S(1)}, f32[128,128]{1,0:T(8,128)S(1)}, bf16[1536,10...) custom-call(bf16[256,1024]{1,0:T(8,128)(2,1)S(1)} %copy-done.4, bf16[1,1024]{1,0:T(2,128)(2,1)S(1)} %copy-done.5, ...), custom_call_target="tpu_custom_call" | custom-call | flops 1 | bytes 1 | tf_op jit(solution)/shard_map/project_own/pallas_call | solution.py:413
  15.5 4.6 %collective-permute-done.msg_ref = bf16[128,1664]{1,0:T(8,128)(2,1)S(1)} collective-permute-done((bf16[128,1664]{1,0:T(8,128)(2,1)}, bf16[128,1664]{1,0:T(8,128)(2,1)S(1)}, u32[]{:S(2)}, u32[]{:S(2)}) %collective-permute-start) | collective-permute-done | bytes 426016 | tf_op jit(solution)/shard_map/ppermute | solution.py:427
  20.1 0.0 copy-done.3
  20.1 1.4 %attend.4 = (bf16[128,1024]{1,0:T(8,128)(2,1)S(1)}, bf16[128,1024]{1,0:T(8,128)(2,1)S(1)}, bf16[128,1024]{1,0:T(8,128)(2,1)S(1)}, bf16[128,256]{1,0:T(8,128)(2,1...) custom-call(bf16[128,1664]{1,0:T(8,128)(2,1)S(1)} %collective-permute-done.msg_ref, ...), custom_call_target="tpu_custom_call" | custom-call | flops 1 | bytes 1 | tf_op jit(solution)/shard_map/attend/pallas_call | solution.py:413
  21.6 5.8 %collective-permute-start.1 = (bf16[128,1024]{1,0:T(8,128)(2,1)S(1)}, bf16[128,1024]{1,0:T(8,128)(2,1)S(1)}, u32[]{:S(2)}, u32[]{:S(2)}) collective-permute-start(bf16[128,1024]{1,0:T(8,128)(2,1)S(1)} %get-tuple-element.102), channel_id=1, source_target_pairs={{0,254},{2,0},{4,2},{6,4},{8,6},{10,8},{12,10},{14,12},{16,14},{18... | collective-permute-start | bytes 786440 | tf_op jit(solution)/shard_map/ppermute | solution.py:432
  27.3 3.9 %collective-permute-done.1.x_ref.refs_13_.x2a_ref = bf16[128,1024]{1,0:T(8,128)(2,1)S(1)} collective-permute-done((bf16[128,1024]{1,0:T(8,128)(2,1)S(1)}, bf16[128,1024]{1,0:T(8,128)(2,1)S(1)}, u32[]{:S(2)}, u32[]{:S(2)}) %collective-permute-start.1) | collective-permute-done | bytes 262176 | tf_op jit(solution)/shard_map/ppermute | solution.py:432
  31.3 0.0 copy-done.1
  31.3 0.6 project.2
  31.9 2.4 %collective-permute-start.4 = (bf16[128,1664]{1,0:T(8,128)(2,1)S(1)}, bf16[128,1664]{1,0:T(8,128)(2,1)S(1)}, u32[]{:S(2)}, u32[]{:S(2)}) collective-permute-start(bf16[128,1664]{1,0:T(8,128)(2,1)S(1)} %get-tuple-element.103), channel_id=1, source_target_pairs={{0,1},{1,0},{2,3},{3,2},{4,5},{5,4},{6,7},{7,6},{8,9},{9,8},{10,11... | collective-permute-start | bytes 1277960 | tf_op jit(solution)/shard_map/ppermute | solution.py:427
  34.3 0.0 collective-permute-done.2.msg_ref
  34.4 1.8 %attend.5 = (bf16[128,1024]{1,0:T(8,128)(2,1)S(1)}, bf16[128,1024]{1,0:T(8,128)(2,1)S(1)}, bf16[128,1024]{1,0:T(8,128)(2,1)S(1)}, bf16[128,256]{1,0:T(8,128)(2,1...) custom-call(bf16[128,1664]{1,0:T(8,128)(2,1)S(1)} %collective-permute-done.2.msg_ref, ...), custom_call_target="tpu_custom_call" | custom-call | flops 1 | bytes 1 | tf_op jit(solution)/shard_map/attend/pallas_call | solution.py:413
  36.1 6.5 %collective-permute-start.3 = (bf16[128,1024]{1,0:T(8,128)(2,1)S(1)}, bf16[128,1024]{1,0:T(8,128)(2,1)S(1)}, u32[]{:S(2)}, u32[]{:S(2)}) collective-permute-start(bf16[128,1024]{1,0:T(8,128)(2,1)S(1)} %get-tuple-element.109), channel_id=1, source_target_pairs={{0,254},{2,0},{4,2},{6,4},{8,6},{10,8},{12,10},{14,12},{16,14},{18... | collective-permute-start | bytes 786440 | tf_op jit(solution)/shard_map/ppermute | solution.py:432
  42.7 3.9 %collective-permute-done.3.x_ref.refs_11_.x2b_ref = bf16[128,1024]{1,0:T(8,128)(2,1)S(1)} collective-permute-done((bf16[128,1024]{1,0:T(8,128)(2,1)S(1)}, bf16[128,1024]{1,0:T(8,128)(2,1)S(1)}, u32[]{:S(2)}, u32[]{:S(2)}) %collective-permute-start.3) | collective-permute-done | bytes 262176 | tf_op jit(solution)/shard_map/ppermute | solution.py:432
  46.6 0.6 project.3
  47.2 0.1 collective-permute-start.5
  47.3 0.0 collective-permute-done.4.msg_ref
  47.4 1.7 %attend.6 = (bf16[128,1024]{1,0:T(8,128)(2,1)S(1)}, bf16[128,1024]{1,0:T(8,128)(2,1)S(1)}, bf16[128,1024]{1,0:T(8,128)(2,1)S(1)}, bf16[128,256]{1,0:T(8,128)(2,1...) custom-call(bf16[128,1664]{1,0:T(8,128)(2,1)S(1)} %collective-permut, ...), custom_call_target="tpu_custom_call" | custom-call | flops 10000000000 | bytes 1 | tf_op jit(solution)/shard_map/attend/pallas_call | solution.py:413
  49.1 3.8 %collective-permute-start.6 = (bf16[128,1024]{1,0:T(8,128)(2,1)S(1)}, bf16[128,1024]{1,0:T(8,128)(2,1)S(1)}, u32[]{:S(2)}, u32[]{:S(2)}) collective-permute-start(bf16[128,1024]{1,0:T(8,128)(2,1)S(1)} %get-tuple-element.123), channel_id=1, source_target_pairs={{0,1},{1,0},{2,3},{3,2},{4,5},{5,4},{6,7},{7,6},{8,9},{9,8},{10,11... | collective-permute-start | bytes 786440 | tf_op jit(solution)/shard_map/ppermute | solution.py:427
  52.9 6.9 %collective-permute-done.5.msg_ref = bf16[128,1664]{1,0:T(8,128)(2,1)S(1)} collective-permute-done((bf16[128,1664]{1,0:T(8,128)(2,1)S(1)}, bf16[128,1664]{1,0:T(8,128)(2,1)S(1)}, u32[]{:S(2)}, u32[]{:S(2)}) %collective-permute-start.5) | collective-permute-done | bytes 426016 | tf_op jit(solution)/shard_map/ppermute | solution.py:427
  59.8 2.1 %attend.7 = (bf16[128,1024]{1,0:T(8,128)(2,1)S(1)}, bf16[128,1024]{1,0:T(8,128)(2,1)S(1)}, bf16[128,1024]{1,0:T(8,128)(2,1)S(1)}, bf16[128,256]{1,0:T(8,128)(2,1...) custom-call(bf16[128,1664]{1,0:T(8,128)(2,1)S(1)} %collective-permut, ...), custom_call_target="tpu_custom_call" | custom-call | flops 1 | bytes 1 | tf_op jit(solution)/shard_map/attend/pallas_call | solution.py:413
  61.9 0.1 collective-permute-start.8
  62.0 3.5 %collective-permute-start.7 = (bf16[128,512]{1,0:T(8,128)(2,1)S(1)}, bf16[128,512]{1,0:T(8,128)(2,1)S(1)}, u32[]{:S(2)}, u32[]{:S(2)}) collective-permute-start(bf16[128,512]{1,0:T(8,128)(2,1)S(1)} %get-tuple-element.127), channel_id=1, source_target_pairs={{0,1},{1,0},{2,3},{3,2},{4,5},{5,4},{6,7},{7,6},{8,9},{9,8},{10,11... | collective-permute-start | bytes 393224 | tf_op jit(solution)/shard_map/ppermute | solution.py:427
  65.5 0.7 early_output.1.acc_ref
  66.2 0.0 collective-permute-done.6.refs_0_
  66.2 2.2 %collective-permute-done.8.refs_0_ = bf16[128,512]{1,0:T(8,128)(2,1)S(1)} collective-permute-done((bf16[128,512]{1,0:T(8,128)(2,1)S(1)}, bf16[128,512]{1,0:T(8,128)(2,1)S(1)}, u32[]{:S(2)}, u32[]{:S(2)}) %collective-permute-start.8) | collective-permute-done | bytes 131104 | tf_op jit(solution)/shard_map/ppermute | solution.py:427
  68.4 1.4 %attend_back.6 = (bf16[128,768]{1,0:T(8,128)(2,1)S(1)}, f32[128,128]{1,0:T(8,128)S(1)}, f32[128,128]{1,0:T(8,128)S(1)}, f32[128,128]{1,0:T(8,128)S(1)}, f32[128,1024]{1,0:T(8,128)S(1)}) custom-call(bf16[128,512]{1,0:T(8,128)(2,1)S(1)} %collective-permute-done.8.refs_0_, f32[128,1024]{1,0:T(8,128)S(1)} %get-tuple-element.128.refs_1_, ...), custom_call_target="tpu_custom_call" | custom-call | flops 1 | bytes 1 | tf_op jit(solution)/shard_map/attend_back/pallas_call | solution.py:413
  69.8 0.0 collective-permute-done.7.refs_0_
  69.8 1.4 %attend_back.7 = (bf16[128,768]{1,0:T(8,128)(2,1)S(1)}, f32[128,128]{1,0:T(8,128)S(1)}, f32[128,128]{1,0:T(8,128)S(1)}, bf16[128,1024]{1,0:T(8,128)(2,1)S(1)}) custom-call(bf16[128,512]{1,0:T(8,128)(2,1)S(1)} %collective-permute-done.7.refs_0_, f32[128,1024]{1,0:T(8,128)S(1)} %get-tuple-element.128.refs_1_, ...), custom_call_target="tpu_custom_call" | custom-call | flops 1 | bytes 1 | tf_op jit(solution)/shard_map/attend_back/pallas_call | solution.py:413
  71.3 0.1 collective-permute-start.10
  71.4 1.9 %attend_back.8 = (bf16[128,768]{1,0:T(8,128)(2,1)S(1)}, bf16[128,768]{1,0:T(8,128)(2,1)S(1)}, bf16[128,1024]{1,0:T(8,128)(2,1)S(1)}) custom-call(bf16[128,1024]{1,0:T(8,128)(2,1)S(1)} %collective-permute-done.6.refs_0_, f32[128,1024]{1,0:T(8,128)S(1)} %get-tuple-element.124.refs_1_, bf16[128,1024]{1,0:T(8,128)(2,1)S(1)} %get-tuple-element.125.refs_2_, ...), custom_call_target="tpu_custom_call" | custom-call | flops 1 | bytes 1 | tf_op jit(solution)/shard_map/attend_back/pallas_call | solution.py:413
  73.3 0.1 collective-permute-start.9
  73.3 1.0 %early_weights.1 = (f32[1024,768]{1,0:T(8,128)S(1)}, f32[1024,768]{1,0:T(8,128)S(1)}, bf16[1024,256]{1,0:T(8,128)(2,1)S(1)}) custom-call(bf16[256,1024]{1,0:T(8,128)(2,1)S(1)} %copy-done.4, bf16[128,1024]{1,0:T(8,128)(2,1)S(1)} %collective-permute-done.1.x_ref.refs_13_.x2a_ref, bf16[128,1024]{1,0:T(8,128)(2,1)S(1)} %collective-permute-done.3.x_ref.refs_11_.x2b_ref, ...), custom_call_target="tpu_custom_call" | custom-call | flops 1 | bytes 1 | tf_op jit(solution)/shard_map/early_weights/pallas_call | solution.py:413
  74.4 7.1 %collective-permute-done.10.up_ref.up_b_ref = bf16[128,1024]{1,0:T(8,128)(2,1)S(1)} collective-permute-done((bf16[128,1024]{1,0:T(8,128)(2,1)S(1)}, bf16[128,1024]{1,0:T(8,128)(2,1)S(1)}, u32[]{:S(2)}, u32[]{:S(2)}) %collective-permute-start.10) | collective-permute-done | bytes 262176 | tf_op jit(solution)/shard_map/ppermute | solution.py:432
  81.5 0.4 output_back.2
  81.9 2.2 %collective-permute-start.12 = (bf16[128,1024]{1,0:T(8,128)(2,1)S(1)}, bf16[128,1024]{1,0:T(8,128)(2,1)S(1)}, u32[]{:S(2)}, u32[]{:S(2)}) collective-permute-start(bf16[128,1024]{1,0:T(8,128)(2,1)S(1)} %get-tuple-element.156), channel_id=1, source_target_pairs={{0,1},{1,0},{2,3},{3,2},{4,5},{5,4},{6,7},{7,6},{8,9},{9,8},{10,11... | collective-permute-start | bytes 786440 | tf_op jit(solution)/shard_map/ppermute | solution.py:427
  84.1 0.1 collective-permute-done.9.up_ref.up_a_ref
  84.3 0.4 output_back.3
  84.7 2.2 %collective-permute-start.11 = (bf16[128,512]{1,0:T(8,128)(2,1)S(1)}, bf16[128,512]{1,0:T(8,128)(2,1)S(1)}, u32[]{:S(2)}, u32[]{:S(2)}) collective-permute-start(bf16[128,512]{1,0:T(8,128)(2,1)S(1)} %get-tuple-element.158), channel_id=1, source_target_pairs={{0,1},{1,0},{2,3},{3,2},{4,5},{5,4},{6,7},{7,6},{8,9},{9,8},{10,11... | collective-permute-start | bytes 393224 | tf_op jit(solution)/shard_map/ppermute | solution.py:427
  87.0 1.4 %collective-permute-start.13 = (bf16[128,512]{1,0:T(8,128)(2,1)S(1)}, bf16[128,512]{1,0:T(8,128)(2,1)S(1)}, u32[]{:S(2)}, u32[]{:S(2)}) collective-permute-start(bf16[128,512]{1,0:T(8,128)(2,1)S(1)} %get-tuple-element.170), channel_id=1, source_target_pairs={{0,1},{1,0},{2,3},{3,2},{4,5},{5,4},{6,7},{7,6},{8,9},{9,8},{10,11... | collective-permute-start | bytes 393224 | tf_op jit(solution)/shard_map/ppermute | solution.py:427
  88.3 1.7 %output_weights.1 = bf16[1024,1024]{1,0:T(8,128)(2,1)} custom-call(bf16[128,1024]{1,0:T(8,128)(2,1)S(1)} %get-tuple-element.174.att_a_ref, bf16[128,1024]{1,0:T(8,128)(2,1)S(1)} %get-tuple-element.175.att_b_ref, bf16[128,1024]{1,0:T(8,128)(2,1)S(1)} %collective-permute-done.9.up_ref.up_a_ref, bf16[128,1024]{1,0:T(8,128)(2,1)S(1)} %collective-permute-done.10.up_ref.up_b_ref, ...), custom_call_target="tpu_custom_call" | custom-call | flops 1 | bytes 1 | tf_op jit(solution)/shard_map/output_weights/pallas_call | solution.py:413
  90.0 0.0 collective-permute-done.12.refs_0_
  90.0 1.8 %attend_back.9 = (bf16[128,768]{1,0:T(8,128)(2,1)S(1)}, bf16[128,768]{1,0:T(8,128)(2,1)S(1)}, f32[128,128]{1,0:T(8,128)S(1)}, f32[128,128]{1,0:T(8,128)S(1)}, f3...) custom-call(bf16[128,1024]{1,0:T(8,128)(2,1)S(1)} %collective-permute-done.12.refs_0_, ...), custom_call_target="tpu_custom_call" | custom-call | flops 1 | bytes 1 | tf_op jit(solution)/shard_map/attend_back/pallas_call | solution.py:413
  91.9 0.0 collective-permute-done.11.refs_0_
  91.9 0.9 attend_back.10.refs_0_
  92.8 0.7 collective-permute-done.13.refs_0_
  93.4 0.9 attend_back.11.refs_2_
  94.3 2.0 %last_weights.1 = bf16[1024,1536]{1,0:T(8,128)(2,1)} custom-call(f32[1024,768]{1,0:T(8,128)S(1)} %get-tuple-element.150.acc0_ref, f32[1024,768]{1,0:T(8,128)S(1)} %get-tuple-element.151.acc1_ref, bf16[1024,256]{1,0:T(8,128)(2,1)S(1)} %get-tuple-element.152.turned_ref, bf16[128,768]{1,0:T(8,128)(2,1)S(1)} %attend_back.10.refs_0_, ...), custom_call_target="tpu_custom_call" | custom-call | flops 1 | bytes 1 | tf_op jit(solution)/shard_map/last_weights/pallas_call | solution.py:413
  (2 shorter events, 0.0 us)
Async XLA Ops:
  0.6 9.5 %copy-start.6 = (f32[256,128]{1,0:T(8,128)S(1)}, f32[256,128]{1,0:T(8,128)}, u32[]{:S(2)}) copy-start(f32[256,128]{1,0:T(8,128)} %constant.23.clone.sin_in) | copy-start | bytes 393220
  0.6 9.4 %copy-start.7 = (f32[256,128]{1,0:T(8,128)S(1)}, f32[256,128]{1,0:T(8,128)}, u32[]{:S(2)}) copy-start(f32[256,128]{1,0:T(8,128)} %constant.22.clone.cos_in) | copy-start | bytes 393220
  0.7 9.6 %copy-start.5 = (bf16[1,1024]{1,0:T(2,128)(2,1)S(1)}, bf16[1,1024]{1,0:T(2,128)(2,1)}, u32[]{:S(2)}) copy-start(bf16[1,1024]{1,0:T(2,128)(2,1)} %gain_ref.9) | copy-start | bytes 6148
  0.7 9.6 %copy-start.4 = (bf16[256,1024]{1,0:T(8,128)(2,1)S(1)}, bf16[256,1024]{1,0:T(8,128)(2,1)}, u32[]{:S(2)}) copy-start(bf16[256,1024]{1,0:T(8,128)(2,1)} %x1_ref) | copy-start | bytes 1572868
  5.6 14.5 %collective-permute-start = (bf16[128,1664]{1,0:T(8,128)(2,1)}, bf16[128,1664]{1,0:T(8,128)(2,1)S(1)}, u32[]{:S(2)}, u32[]{:S(2)}) collective-permute-start(bf16[128,1664]{1,0:T(8,128)(2,1)} %get-tuple-element.94), channel_id=1, source_target_pairs={{0,1},{1,0},{2,3},{3,2},{4,5},{5,4},{6,7},{7,6},{8,9},{9,8},{10,11... | collective-permute-start | bytes 1277960 | tf_op jit(solution)/shard_map/ppermute | solution.py:427
  7.8 26.5 %collective-permute-start.2 = (bf16[128,1664]{1,0:T(8,128)(2,1)}, bf16[128,1664]{1,0:T(8,128)(2,1)S(1)}, u32[]{:S(2)}, u32[]{:S(2)}) collective-permute-start(bf16[128,1664]{1,0:T(8,128)(2,1)} %get-tuple-element.89), channel_id=1, source_target_pairs={{0,1},{1,0},{2,3},{3,2},{4,5},{5,4},{6,7},{7,6},{8,9},{9,8},{10,11... | collective-permute-start | bytes 1277960 | tf_op jit(solution)/shard_map/ppermute | solution.py:427
  10.3 1.9 %copy-start = (bf16[1,1024,1536]{2,1,0:T(8,128)(2,1)S(1)}, bf16[1,1024,1536]{2,1,0:T(8,128)(2,1)}, u32[]{:S(2)}) copy-start(bf16[1,1024,1536]{2,1,0:T(8,128)(2,1)} %param.9) | copy-start | bytes 9437188
  12.1 1.6 %copy-start.2 = (bf16[1,1024,1024]{2,1,0:T(8,128)(2,1)S(1)}, bf16[1,1024,1024]{2,1,0:T(8,128)(2,1)}, u32[]{:S(2)}) copy-start(bf16[1,1024,1024]{2,1,0:T(8,128)(2,1)} %param.10) | copy-start | bytes 6291460
  13.7 6.4 %copy-start.3 = (bf16[1,1024,1024]{2,1,0:T(8,128)(2,1)S(1)}, bf16[1,1024,1024]{2,1,0:T(8,128)(2,1)}, u32[]{:S(2)}) copy-start(bf16[1,1024,1024]{2,1,0:T(8,128)(2,1)} %param.10) | copy-start | bytes 6291460
  20.1 11.1 %copy-start.1 = (bf16[1,1024,1536]{2,1,0:T(8,128)(2,1)S(1)}, bf16[1,1024,1536]{2,1,0:T(8,128)(2,1)}, u32[]{:S(2)}) copy-start(bf16[1,1024,1536]{2,1,0:T(8,128)(2,1)} %param.9) | copy-start | bytes 9437188
  21.6 9.7 %collective-permute-start.1 = (bf16[128,1024]{1,0:T(8,128)(2,1)S(1)}, bf16[128,1024]{1,0:T(8,128)(2,1)S(1)}, u32[]{:S(2)}, u32[]{:S(2)}) collective-permute-start(bf16[128,1024]{1,0:T(8,128)(2,1)S(1)} %get-tuple-element.102), channel_id=1, source_target_pairs={{0,254},{2,0},{4,2},{6,4},{8,6},{10,8},{12,10},{14,12},{16,14},{18... | collective-permute-start | bytes 786440 | tf_op jit(solution)/shard_map/ppermute | solution.py:432
  31.9 15.4 %collective-permute-start.4 = (bf16[128,1664]{1,0:T(8,128)(2,1)S(1)}, bf16[128,1664]{1,0:T(8,128)(2,1)S(1)}, u32[]{:S(2)}, u32[]{:S(2)}) collective-permute-start(bf16[128,1664]{1,0:T(8,128)(2,1)S(1)} %get-tuple-element.103), channel_id=1, source_target_pairs={{0,1},{1,0},{2,3},{3,2},{4,5},{5,4},{6,7},{7,6},{8,9},{9,8},{10,11... | collective-permute-start | bytes 1277960 | tf_op jit(solution)/shard_map/ppermute | solution.py:427
  36.1 10.5 %collective-permute-start.3 = (bf16[128,1024]{1,0:T(8,128)(2,1)S(1)}, bf16[128,1024]{1,0:T(8,128)(2,1)S(1)}, u32[]{:S(2)}, u32[]{:S(2)}) collective-permute-start(bf16[128,1024]{1,0:T(8,128)(2,1)S(1)} %get-tuple-element.109), channel_id=1, source_target_pairs={{0,254},{2,0},{4,2},{6,4},{8,6},{10,8},{12,10},{14,12},{16,14},{18... | collective-permute-start | bytes 786440 | tf_op jit(solution)/shard_map/ppermute | solution.py:432
  47.2 12.5 %collective-permute-start.5 = (bf16[128,1664]{1,0:T(8,128)(2,1)S(1)}, bf16[128,1664]{1,0:T(8,128)(2,1)S(1)}, u32[]{:S(2)}, u32[]{:S(2)}) collective-permute-start(bf16[128,1664]{1,0:T(8,128)(2,1)S(1)} %get-tuple-element.117), channel_id=1, source_target_pairs={{0,1},{1,0},{2,3},{3,2},{4,5},{5,4},{6,7},{7,6},{8,9},{9,8},{10,11... | collective-permute-start | bytes 1277960 | tf_op jit(solution)/shard_map/ppermute | solution.py:427
  49.1 17.1 %collective-permute-start.6 = (bf16[128,1024]{1,0:T(8,128)(2,1)S(1)}, bf16[128,1024]{1,0:T(8,128)(2,1)S(1)}, u32[]{:S(2)}, u32[]{:S(2)}) collective-permute-start(bf16[128,1024]{1,0:T(8,128)(2,1)S(1)} %get-tuple-element.123), channel_id=1, source_target_pairs={{0,1},{1,0},{2,3},{3,2},{4,5},{5,4},{6,7},{7,6},{8,9},{9,8},{10,11... | collective-permute-start | bytes 786440 | tf_op jit(solution)/shard_map/ppermute | solution.py:427
  61.9 6.6 %collective-permute-start.8 = (bf16[128,512]{1,0:T(8,128)(2,1)S(1)}, bf16[128,512]{1,0:T(8,128)(2,1)S(1)}, u32[]{:S(2)}, u32[]{:S(2)}) collective-permute-start(bf16[128,512]{1,0:T(8,128)(2,1)S(1)} %get-tuple-element.135), channel_id=1, source_target_pairs={{0,1},{1,0},{2,3},{3,2},{4,5},{5,4},{6,7},{7,6},{8,9},{9,8},{10,11... | collective-permute-start | bytes 393224 | tf_op jit(solution)/shard_map/ppermute | solution.py:427
  62.0 7.9 %collective-permute-start.7 = (bf16[128,512]{1,0:T(8,128)(2,1)S(1)}, bf16[128,512]{1,0:T(8,128)(2,1)S(1)}, u32[]{:S(2)}, u32[]{:S(2)}) collective-permute-start(bf16[128,512]{1,0:T(8,128)(2,1)S(1)} %get-tuple-element.127), channel_id=1, source_target_pairs={{0,1},{1,0},{2,3},{3,2},{4,5},{5,4},{6,7},{7,6},{8,9},{9,8},{10,11... | collective-permute-start | bytes 393224 | tf_op jit(solution)/shard_map/ppermute | solution.py:427
  71.3 10.2 %collective-permute-start.10 = (bf16[128,1024]{1,0:T(8,128)(2,1)S(1)}, bf16[128,1024]{1,0:T(8,128)(2,1)S(1)}, u32[]{:S(2)}, u32[]{:S(2)}) collective-permute-start(bf16[128,1024]{1,0:T(8,128)(2,1)S(1)} %get-tuple-element.154), channel_id=1, source_target_pairs={{0,2},{2,4},{4,6},{6,8},{8,10},{10,12},{12,14},{14,16},{16,18},{18... | collective-permute-start | bytes 786440 | tf_op jit(solution)/shard_map/ppermute | solution.py:432
  73.3 11.0 %collective-permute-start.9 = (bf16[128,1024]{1,0:T(8,128)(2,1)S(1)}, bf16[128,1024]{1,0:T(8,128)(2,1)S(1)}, u32[]{:S(2)}, u32[]{:S(2)}) collective-permute-start(bf16[128,1024]{1,0:T(8,128)(2,1)S(1)} %get-tuple-element.153), channel_id=1, source_target_pairs={{0,2},{2,4},{4,6},{6,8},{8,10},{10,12},{12,14},{14,16},{16,18},{18... | collective-permute-start | bytes 786440 | tf_op jit(solution)/shard_map/ppermute | solution.py:432
  81.9 8.1 %collective-permute-start.12 = (bf16[128,1024]{1,0:T(8,128)(2,1)S(1)}, bf16[128,1024]{1,0:T(8,128)(2,1)S(1)}, u32[]{:S(2)}, u32[]{:S(2)}) collective-permute-start(bf16[128,1024]{1,0:T(8,128)(2,1)S(1)} %get-tuple-element.156), channel_id=1, source_target_pairs={{0,1},{1,0},{2,3},{3,2},{4,5},{5,4},{6,7},{7,6},{8,9},{9,8},{10,11... | collective-permute-start | bytes 786440 | tf_op jit(solution)/shard_map/ppermute | solution.py:427
  84.7 7.2 %collective-permute-start.11 = (bf16[128,512]{1,0:T(8,128)(2,1)S(1)}, bf16[128,512]{1,0:T(8,128)(2,1)S(1)}, u32[]{:S(2)}, u32[]{:S(2)}) collective-permute-start(bf16[128,512]{1,0:T(8,128)(2,1)S(1)} %get-tuple-element.158), channel_id=1, source_target_pairs={{0,1},{1,0},{2,3},{3,2},{4,5},{5,4},{6,7},{7,6},{8,9},{9,8},{10,11... | collective-permute-start | bytes 393224 | tf_op jit(solution)/shard_map/ppermute | solution.py:427
  87.0 6.5 %collective-permute-start.13 = (bf16[128,512]{1,0:T(8,128)(2,1)S(1)}, bf16[128,512]{1,0:T(8,128)(2,1)S(1)}, u32[]{:S(2)}, u32[]{:S(2)}) collective-permute-start(bf16[128,512]{1,0:T(8,128)(2,1)S(1)} %get-tuple-element.170), channel_id=1, source_target_pairs={{0,1},{1,0},{2,3},{3,2},{4,5},{5,4},{6,7},{7,6},{8,9},{9,8},{10,11... | collective-permute-start | bytes 393224 | tf_op jit(solution)/shard_map/ppermute | solution.py:427

commit v6 on v4

--- a/solution.py
+++ b/solution.py
@@ -322,13 +322,26 @@
     put_message(own, msg_refs)
 
 
-def output_weight_kernel(*refs):
-    att = jnp.concatenate([refs[0][...], refs[1][...]], axis=0)
-    up = jnp.concatenate([refs[2][...], refs[3][...]], axis=0)
-    out = dot(att, up, TN)
-    if len(refs) > 5:
-        out = out + refs[4][...]
-    refs[-1][...] = out.astype(refs[-1].dtype)
+def early_output_kernel(att_a_ref, att_b_ref, up_a_ref, up_b_ref, acc_ref):
+    att = jnp.concatenate([att_a_ref[...], att_b_ref[...]], axis=0)
+    acc_ref[...] = dot(att, jnp.concatenate([up_a_ref[...], up_b_ref[...]], axis=0), TN)
+
+
+def output_weight_kernel(
+    att_a_ref, att_b_ref, up_a_ref, up_b_ref, acc_ref, out_ref, held, sems
+):
+    up = jnp.concatenate([up_a_ref[...], up_b_ref[...]], axis=0)
+    pieces = sems.shape[0]
+    size = HEADS // pieces
+    copies = []
+    for i in range(pieces):
+        rows = pl.ds(i * size, size)
+        att = jnp.concatenate([att_a_ref[:, rows], att_b_ref[:, rows]], axis=0)
+        held[rows] = (acc_ref[rows] + dot(att, up, TN)).astype(BF16)
+        copies.append(pltpu.make_async_copy(held.at[rows], out_ref.at[rows], sems.at[i]))
+        copies[-1].start()
+    for copy in copies:
+        copy.wait()
 
 
 def gained(x, scale_ref, gain_ref):
@@ -528,8 +541,8 @@
         1, True, xb, (recv_b, own_b, sums_b), layer, bias2, trig, a2["kv"], cut=2
     )
     begun_out = call(
-        output_weight_kernel, [a2["att"], b2["att"], a2["out"], b2["out"]],
-        [shape_of(F32, HEADS, HALF)], "output_weights",
+        early_output_kernel, [a2["att"], b2["att"], a2["out"], b2["out"]],
+        [shape_of(F32, HEADS, HALF)], "early_output",
     )[0]
     recvs_b = [swap(msg) for msg in b2["msgs"]]
     recvs_b[0] = after(recvs_b[0], recv_a, begun_out)
@@ -560,7 +573,8 @@
     recvs_a = [swap(msg) for msg in msgs_a]
     (total_out,) = call(
         output_weight_kernel, [a1["att"], b1["att"], upa, upb, begun_out],
-        [shape_of(BF16, HEADS, HALF)], "output_weights",
+        [shape_of(BF16, HEADS, HALF)], "output_weights", out_specs=[IN_HBM],
+        scratch=[pltpu.VMEM((HEADS, HALF), BF16), pltpu.SemaphoreType.DMA((8,))],
     )
     pgb1 = back(1, (0, 1), {"recv": recv_b}, own_b, b1, trig, a1["kv"] + b1["kv"])
     pga1 = {}

time: 96.5 us -> 96.5 us (level)
  transfers between devices with their start and end apart: 14 -> 14, of which waited for: 8 -> 8; matrix products, arithmetic and copies ran while one was open for 1% -> 1% of each run, Pallas kernels for 22% -> 21%
where the time goes in v6:
time: 96.5 us; the launch traced here: 96.3 us
  starting transfers between devices  31.8 us (33%)
  Pallas kernels  29.6 us (31%)
  waiting for transfers between devices  29.5 us (31%)
  local copies, waits for them, and re-layouts  3.5 us (4%)
  between operations  1.08 us (1%)
    pallas_call x21, Pallas kernels, call(): pl.pallas_call(kernel, grid=(1,), in_specs=[specs.get(i) or block(*a.shap...  29.6 us
    ppermute x10, starting transfers between devices, swap(): return lax.ppermute(value, 'stretch', [(0, 1), (1, 0)])  19.4 us
    ppermute x4, waiting for transfers between devices, hop(): lax.ppermute(value, 'blk', [(i, (i + step) % count) for i in range(count)])  15.1 us
    ppermute x10, waiting for transfers between devices, swap(): return lax.ppermute(value, 'stretch', [(0, 1), (1, 0)])  14.4 us
    ppermute x4, starting transfers between devices, hop(): lax.ppermute(value, 'blk', [(i, (i + step) % count) for i in range(count)])  12.5 us
    unnamed x16, local copies, waits for them, and re-layouts  3.5 us
  transfers between devices with their start and end apart: 14, of which 8 were waited for; matrix products, arithmetic and copies ran while one was open for 1% of the time, Pallas kernels for 21%

profile of v6, /device:TPU:2, one launch (start us, length us, event | category | flops | bytes accessed | tf_op | source)
XLA Modules:
  0.0 96.3 jit_solution(7132439882282051129)
XLA Ops:
  0.6 0.0 copy-start.6
  0.6 0.0 copy-start.7
  0.7 0.0 copy-start.5
  0.7 0.0 copy-start.4
  0.7 4.7 %project_first.1 = (bf16[128,1664]{1,0:T(8,128)(2,1)}, bf16[128,1664]{1,0:T(8,128)(2,1)}) custom-call(bf16[256,1024]{1,0:T(8,128)(2,1)} %x1_ref, bf16[1,1024]{1,0:T(2,128)(2,1)} %gain_ref.9, bf16[1024,1536]{1,0:T(8,128)(2,1)} %bitcast.6), custom_call_target="tpu_custom_call" | custom-call | flops 1 | bytes 1 | tf_op jit(solution)/shard_map/project_first/pallas_call | solution.py:401
  5.4 2.2 %collective-permute-start = (bf16[128,1664]{1,0:T(8,128)(2,1)}, bf16[128,1664]{1,0:T(8,128)(2,1)S(1)}, u32[]{:S(2)}, u32[]{:S(2)}) collective-permute-start(bf16[128,1664]{1,0:T(8,128)(2,1)} %get-tuple-element.94), channel_id=1, source_target_pairs={{0,1},{1,0},{2,3},{3,2},{4,5},{5,4},{6,7},{7,6},{8,9},{9,8},{10,11... | collective-permute-start | bytes 1277960 | tf_op jit(solution)/shard_map/ppermute | solution.py:415
  7.6 1.4 %collective-permute-start.2 = (bf16[128,1664]{1,0:T(8,128)(2,1)}, bf16[128,1664]{1,0:T(8,128)(2,1)S(1)}, u32[]{:S(2)}, u32[]{:S(2)}) collective-permute-start(bf16[128,1664]{1,0:T(8,128)(2,1)} %get-tuple-element.89), channel_id=1, source_target_pairs={{0,1},{1,0},{2,3},{3,2},{4,5},{5,4},{6,7},{7,6},{8,9},{9,8},{10,11... | collective-permute-start | bytes 1277960 | tf_op jit(solution)/shard_map/ppermute | solution.py:415
  9.0 0.8 dynamic-slice_convert_fusion
  9.9 0.0 copy-done.6
  9.9 0.0 copy-done.7
  9.9 0.1 prepare.1
  10.0 0.0 copy-done.5
  10.0 0.0 copy-done.4
  10.0 0.0 copy-start
  10.0 1.9 %copy-done = bf16[1,1024,1536]{2,1,0:T(8,128)(2,1)S(1)} copy-done((bf16[1,1024,1536]{2,1,0:T(8,128)(2,1)S(1)}, bf16[1,1024,1536]{2,1,0:T(8,128)(2,1)}, u32[]{:S(2)}) %copy-start) | copy-done | bytes 3145752
  11.9 0.0 copy-start.2
  11.9 1.6 %copy-done.2 = bf16[1,1024,1024]{2,1,0:T(8,128)(2,1)S(1)} copy-done((bf16[1,1024,1024]{2,1,0:T(8,128)(2,1)S(1)}, bf16[1,1024,1024]{2,1,0:T(8,128)(2,1)}, u32[]{:S(2)}) %copy-start.2) | copy-done | bytes 2097176
  13.5 1.8 %project_own.1 = (f32[128,1536]{1,0:T(8,128)S(1)}, f32[128,128]{1,0:T(8,128)S(1)}, f32[128,1536]{1,0:T(8,128)S(1)}, f32[128,128]{1,0:T(8,128)S(1)}, bf16[1536,10...) custom-call(bf16[256,1024]{1,0:T(8,128)(2,1)S(1)} %copy-done.4, bf16[1,1024]{1,0:T(2,128)(2,1)S(1)} %copy-done.5, ...), custom_call_target="tpu_custom_call" | custom-call | flops 1 | bytes 1 | tf_op jit(solution)/shard_map/project_own/pallas_call | solution.py:401
  15.3 4.6 %collective-permute-done.msg_ref = bf16[128,1664]{1,0:T(8,128)(2,1)S(1)} collective-permute-done((bf16[128,1664]{1,0:T(8,128)(2,1)}, bf16[128,1664]{1,0:T(8,128)(2,1)S(1)}, u32[]{:S(2)}, u32[]{:S(2)}) %collective-permute-start) | collective-permute-done | bytes 426016 | tf_op jit(solution)/shard_map/ppermute | solution.py:415
  19.9 0.0 copy-done.3
  19.9 1.4 %attend.4 = (bf16[128,1024]{1,0:T(8,128)(2,1)S(1)}, bf16[128,1024]{1,0:T(8,128)(2,1)S(1)}, bf16[128,1024]{1,0:T(8,128)(2,1)S(1)}, bf16[128,256]{1,0:T(8,128)(2,1...) custom-call(bf16[128,1664]{1,0:T(8,128)(2,1)S(1)} %collective-permute-done.msg_ref, ...), custom_call_target="tpu_custom_call" | custom-call | flops 1 | bytes 1 | tf_op jit(solution)/shard_map/attend/pallas_call | solution.py:401
  21.3 5.8 %collective-permute-start.1 = (bf16[128,1024]{1,0:T(8,128)(2,1)S(1)}, bf16[128,1024]{1,0:T(8,128)(2,1)S(1)}, u32[]{:S(2)}, u32[]{:S(2)}) collective-permute-start(bf16[128,1024]{1,0:T(8,128)(2,1)S(1)} %get-tuple-element.102), channel_id=1, source_target_pairs={{0,254},{2,0},{4,2},{6,4},{8,6},{10,8},{12,10},{14,12},{16,14},{18... | collective-permute-start | bytes 786440 | tf_op jit(solution)/shard_map/ppermute | solution.py:420
  27.1 3.9 %collective-permute-done.1.x_ref.refs_13_.x2a_ref = bf16[128,1024]{1,0:T(8,128)(2,1)S(1)} collective-permute-done((bf16[128,1024]{1,0:T(8,128)(2,1)S(1)}, bf16[128,1024]{1,0:T(8,128)(2,1)S(1)}, u32[]{:S(2)}, u32[]{:S(2)}) %collective-permute-start.1) | collective-permute-done | bytes 262176 | tf_op jit(solution)/shard_map/ppermute | solution.py:420
  31.1 0.0 copy-done.1
  31.1 0.6 project.2
  31.7 2.5 %collective-permute-start.4 = (bf16[128,1664]{1,0:T(8,128)(2,1)S(1)}, bf16[128,1664]{1,0:T(8,128)(2,1)S(1)}, u32[]{:S(2)}, u32[]{:S(2)}) collective-permute-start(bf16[128,1664]{1,0:T(8,128)(2,1)S(1)} %get-tuple-element.103), channel_id=1, source_target_pairs={{0,1},{1,0},{2,3},{3,2},{4,5},{5,4},{6,7},{7,6},{8,9},{9,8},{10,11... | collective-permute-start | bytes 1277960 | tf_op jit(solution)/shard_map/ppermute | solution.py:415
  34.1 0.0 collective-permute-done.2.msg_ref
  34.1 1.8 %attend.5 = (bf16[128,1024]{1,0:T(8,128)(2,1)S(1)}, bf16[128,1024]{1,0:T(8,128)(2,1)S(1)}, bf16[128,1024]{1,0:T(8,128)(2,1)S(1)}, bf16[128,256]{1,0:T(8,128)(2,1...) custom-call(bf16[128,1664]{1,0:T(8,128)(2,1)S(1)} %collective-permute-done.2.msg_ref, ...), custom_call_target="tpu_custom_call" | custom-call | flops 1 | bytes 1 | tf_op jit(solution)/shard_map/attend/pallas_call | solution.py:401
  35.9 6.5 %collective-permute-start.3 = (bf16[128,1024]{1,0:T(8,128)(2,1)S(1)}, bf16[128,1024]{1,0:T(8,128)(2,1)S(1)}, u32[]{:S(2)}, u32[]{:S(2)}) collective-permute-start(bf16[128,1024]{1,0:T(8,128)(2,1)S(1)} %get-tuple-element.109), channel_id=1, source_target_pairs={{0,254},{2,0},{4,2},{6,4},{8,6},{10,8},{12,10},{14,12},{16,14},{18... | collective-permute-start | bytes 786440 | tf_op jit(solution)/shard_map/ppermute | solution.py:420
  42.5 3.9 %collective-permute-done.3.x_ref.refs_11_.x2b_ref = bf16[128,1024]{1,0:T(8,128)(2,1)S(1)} collective-permute-done((bf16[128,1024]{1,0:T(8,128)(2,1)S(1)}, bf16[128,1024]{1,0:T(8,128)(2,1)S(1)}, u32[]{:S(2)}, u32[]{:S(2)}) %collective-permute-start.3) | collective-permute-done | bytes 262176 | tf_op jit(solution)/shard_map/ppermute | solution.py:420
  46.4 0.6 project.3
  47.0 0.1 collective-permute-start.5
  47.1 0.0 collective-permute-done.4.msg_ref
  47.1 1.7 %attend.6 = (bf16[128,1024]{1,0:T(8,128)(2,1)S(1)}, bf16[128,1024]{1,0:T(8,128)(2,1)S(1)}, bf16[128,1024]{1,0:T(8,128)(2,1)S(1)}, bf16[128,256]{1,0:T(8,128)(2,1...) custom-call(bf16[128,1664]{1,0:T(8,128)(2,1)S(1)} %collective-permut, ...), custom_call_target="tpu_custom_call" | custom-call | flops 10000000000 | bytes 1 | tf_op jit(solution)/shard_map/attend/pallas_call | solution.py:401
  48.9 3.8 %collective-permute-start.6 = (bf16[128,1024]{1,0:T(8,128)(2,1)S(1)}, bf16[128,1024]{1,0:T(8,128)(2,1)S(1)}, u32[]{:S(2)}, u32[]{:S(2)}) collective-permute-start(bf16[128,1024]{1,0:T(8,128)(2,1)S(1)} %get-tuple-element.123), channel_id=1, source_target_pairs={{0,1},{1,0},{2,3},{3,2},{4,5},{5,4},{6,7},{7,6},{8,9},{9,8},{10,11... | collective-permute-start | bytes 786440 | tf_op jit(solution)/shard_map/ppermute | solution.py:415
  52.6 6.9 %collective-permute-done.5.msg_ref = bf16[128,1664]{1,0:T(8,128)(2,1)S(1)} collective-permute-done((bf16[128,1664]{1,0:T(8,128)(2,1)S(1)}, bf16[128,1664]{1,0:T(8,128)(2,1)S(1)}, u32[]{:S(2)}, u32[]{:S(2)}) %collective-permute-start.5) | collective-permute-done | bytes 426016 | tf_op jit(solution)/shard_map/ppermute | solution.py:415
  59.5 2.1 %attend.7 = (bf16[128,1024]{1,0:T(8,128)(2,1)S(1)}, bf16[128,1024]{1,0:T(8,128)(2,1)S(1)}, bf16[128,1024]{1,0:T(8,128)(2,1)S(1)}, bf16[128,256]{1,0:T(8,128)(2,1...) custom-call(bf16[128,1664]{1,0:T(8,128)(2,1)S(1)} %collective-permut, ...), custom_call_target="tpu_custom_call" | custom-call | flops 1 | bytes 1 | tf_op jit(solution)/shard_map/attend/pallas_call | solution.py:401
  61.6 0.1 collective-permute-start.8
  61.7 3.5 %collective-permute-start.7 = (bf16[128,512]{1,0:T(8,128)(2,1)S(1)}, bf16[128,512]{1,0:T(8,128)(2,1)S(1)}, u32[]{:S(2)}, u32[]{:S(2)}) collective-permute-start(bf16[128,512]{1,0:T(8,128)(2,1)S(1)} %get-tuple-element.127), channel_id=1, source_target_pairs={{0,1},{1,0},{2,3},{3,2},{4,5},{5,4},{6,7},{7,6},{8,9},{9,8},{10,11... | collective-permute-start | bytes 393224 | tf_op jit(solution)/shard_map/ppermute | solution.py:415
  65.3 0.7 early_output.1.acc_ref
  66.0 0.0 collective-permute-done.6.refs_0_
  66.0 2.2 %collective-permute-done.8.refs_0_ = bf16[128,512]{1,0:T(8,128)(2,1)S(1)} collective-permute-done((bf16[128,512]{1,0:T(8,128)(2,1)S(1)}, bf16[128,512]{1,0:T(8,128)(2,1)S(1)}, u32[]{:S(2)}, u32[]{:S(2)}) %collective-permute-start.8) | collective-permute-done | bytes 131104 | tf_op jit(solution)/shard_map/ppermute | solution.py:415
  68.2 1.4 %attend_back.6 = (bf16[128,768]{1,0:T(8,128)(2,1)S(1)}, f32[128,128]{1,0:T(8,128)S(1)}, f32[128,128]{1,0:T(8,128)S(1)}, f32[128,128]{1,0:T(8,128)S(1)}, f32[128,1024]{1,0:T(8,128)S(1)}) custom-call(bf16[128,512]{1,0:T(8,128)(2,1)S(1)} %collective-permute-done.8.refs_0_, f32[128,1024]{1,0:T(8,128)S(1)} %get-tuple-element.128.refs_1_, ...), custom_call_target="tpu_custom_call" | custom-call | flops 1 | bytes 1 | tf_op jit(solution)/shard_map/attend_back/pallas_call | solution.py:401
  69.6 0.0 collective-permute-done.7.refs_0_
  69.6 1.4 %attend_back.7 = (bf16[128,768]{1,0:T(8,128)(2,1)S(1)}, f32[128,128]{1,0:T(8,128)S(1)}, f32[128,128]{1,0:T(8,128)S(1)}, bf16[128,1024]{1,0:T(8,128)(2,1)S(1)}) custom-call(bf16[128,512]{1,0:T(8,128)(2,1)S(1)} %collective-permute-done.7.refs_0_, f32[128,1024]{1,0:T(8,128)S(1)} %get-tuple-element.128.refs_1_, ...), custom_call_target="tpu_custom_call" | custom-call | flops 1 | bytes 1 | tf_op jit(solution)/shard_map/attend_back/pallas_call | solution.py:401
  71.0 0.1 collective-permute-start.10
  71.1 1.9 %attend_back.8 = (bf16[128,768]{1,0:T(8,128)(2,1)S(1)}, bf16[128,768]{1,0:T(8,128)(2,1)S(1)}, bf16[128,1024]{1,0:T(8,128)(2,1)S(1)}) custom-call(bf16[128,1024]{1,0:T(8,128)(2,1)S(1)} %collective-permute-done.6.refs_0_, f32[128,1024]{1,0:T(8,128)S(1)} %get-tuple-element.124.refs_1_, bf16[128,1024]{1,0:T(8,128)(2,1)S(1)} %get-tuple-element.125.refs_2_, ...), custom_call_target="tpu_custom_call" | custom-call | flops 1 | bytes 1 | tf_op jit(solution)/shard_map/attend_back/pallas_call | solution.py:401
  73.0 0.1 collective-permute-start.9
  73.1 1.0 %early_weights.1 = (f32[1024,768]{1,0:T(8,128)S(1)}, f32[1024,768]{1,0:T(8,128)S(1)}, bf16[1024,256]{1,0:T(8,128)(2,1)S(1)}) custom-call(bf16[256,1024]{1,0:T(8,128)(2,1)S(1)} %copy-done.4, bf16[128,1024]{1,0:T(8,128)(2,1)S(1)} %collective-permute-done.1.x_ref.refs_13_.x2a_ref, bf16[128,1024]{1,0:T(8,128)(2,1)S(1)} %collective-permute-done.3.x_ref.refs_11_.x2b_ref, ...), custom_call_target="tpu_custom_call" | custom-call | flops 1 | bytes 1 | tf_op jit(solution)/shard_map/early_weights/pallas_call | solution.py:401
  74.2 7.1 %collective-permute-done.10.up_ref.up_b_ref = bf16[128,1024]{1,0:T(8,128)(2,1)S(1)} collective-permute-done((bf16[128,1024]{1,0:T(8,128)(2,1)S(1)}, bf16[128,1024]{1,0:T(8,128)(2,1)S(1)}, u32[]{:S(2)}, u32[]{:S(2)}) %collective-permute-start.10) | collective-permute-done | bytes 262176 | tf_op jit(solution)/shard_map/ppermute | solution.py:420
  81.2 0.5 output_back.2
  81.7 2.2 %collective-permute-start.12 = (bf16[128,1024]{1,0:T(8,128)(2,1)S(1)}, bf16[128,1024]{1,0:T(8,128)(2,1)S(1)}, u32[]{:S(2)}, u32[]{:S(2)}) collective-permute-start(bf16[128,1024]{1,0:T(8,128)(2,1)S(1)} %get-tuple-element.156), channel_id=1, source_target_pairs={{0,1},{1,0},{2,3},{3,2},{4,5},{5,4},{6,7},{7,6},{8,9},{9,8},{10,11... | collective-permute-start | bytes 786440 | tf_op jit(solution)/shard_map/ppermute | solution.py:415
  83.9 0.1 collective-permute-done.9.up_ref.up_a_ref
  84.1 0.5 output_back.3
  84.5 2.2 %collective-permute-start.11 = (bf16[128,512]{1,0:T(8,128)(2,1)S(1)}, bf16[128,512]{1,0:T(8,128)(2,1)S(1)}, u32[]{:S(2)}, u32[]{:S(2)}) collective-permute-start(bf16[128,512]{1,0:T(8,128)(2,1)S(1)} %get-tuple-element.158), channel_id=1, source_target_pairs={{0,1},{1,0},{2,3},{3,2},{4,5},{5,4},{6,7},{7,6},{8,9},{9,8},{10,11... | collective-permute-start | bytes 393224 | tf_op jit(solution)/shard_map/ppermute | solution.py:415
  86.7 1.4 %collective-permute-start.13 = (bf16[128,512]{1,0:T(8,128)(2,1)S(1)}, bf16[128,512]{1,0:T(8,128)(2,1)S(1)}, u32[]{:S(2)}, u32[]{:S(2)}) collective-permute-start(bf16[128,512]{1,0:T(8,128)(2,1)S(1)} %get-tuple-element.170), channel_id=1, source_target_pairs={{0,1},{1,0},{2,3},{3,2},{4,5},{5,4},{6,7},{7,6},{8,9},{9,8},{10,11... | collective-permute-start | bytes 393224 | tf_op jit(solution)/shard_map/ppermute | solution.py:415
  88.1 1.7 %output_weights.1 = bf16[1024,1024]{1,0:T(8,128)(2,1)} custom-call(bf16[128,1024]{1,0:T(8,128)(2,1)S(1)} %get-tuple-element.174.att_a_ref, bf16[128,1024]{1,0:T(8,128)(2,1)S(1)} %get-tuple-element.175.att_b_ref, bf16[128,1024]{1,0:T(8,128)(2,1)S(1)} %collective-permute-done.9.up_ref.up_a_ref, bf16[128,1024]{1,0:T(8,128)(2,1)S(1)} %collective-permute-done.10.up_ref.up_b_ref, ...), custom_call_target="tpu_custom_call" | custom-call | flops 1 | bytes 1 | tf_op jit(solution)/shard_map/output_weights/pallas_call | solution.py:401
  89.8 0.0 collective-permute-done.12.refs_0_
  89.8 1.8 %attend_back.9 = (bf16[128,768]{1,0:T(8,128)(2,1)S(1)}, bf16[128,768]{1,0:T(8,128)(2,1)S(1)}, f32[128,128]{1,0:T(8,128)S(1)}, f32[128,128]{1,0:T(8,128)S(1)}, f3...) custom-call(bf16[128,1024]{1,0:T(8,128)(2,1)S(1)} %collective-permute-done.12.refs_0_, ...), custom_call_target="tpu_custom_call" | custom-call | flops 1 | bytes 1 | tf_op jit(solution)/shard_map/attend_back/pallas_call | solution.py:401
  91.7 0.0 collective-permute-done.11.refs_0_
  91.7 0.9 attend_back.10.refs_0_
  92.6 0.6 collective-permute-done.13.refs_0_
  93.2 0.9 attend_back.11.refs_2_
  94.1 2.0 %last_weights.1 = bf16[1024,1536]{1,0:T(8,128)(2,1)} custom-call(f32[1024,768]{1,0:T(8,128)S(1)} %get-tuple-element.150.acc0_ref, f32[1024,768]{1,0:T(8,128)S(1)} %get-tuple-element.151.acc1_ref, bf16[1024,256]{1,0:T(8,128)(2,1)S(1)} %get-tuple-element.152.turned_ref, bf16[128,768]{1,0:T(8,128)(2,1)S(1)} %attend_back.10.refs_0_, ...), custom_call_target="tpu_custom_call" | custom-call | flops 1 | bytes 1 | tf_op jit(solution)/shard_map/last_weights/pallas_call | solution.py:401
  (2 shorter events, 0.0 us)
Async XLA Ops:
  0.6 9.2 %copy-start.6 = (f32[256,128]{1,0:T(8,128)S(1)}, f32[256,128]{1,0:T(8,128)}, u32[]{:S(2)}) copy-start(f32[256,128]{1,0:T(8,128)} %constant.23.clone.sin_in) | copy-start | bytes 393220
  0.6 9.2 %copy-start.7 = (f32[256,128]{1,0:T(8,128)S(1)}, f32[256,128]{1,0:T(8,128)}, u32[]{:S(2)}) copy-start(f32[256,128]{1,0:T(8,128)} %constant.22.clone.cos_in) | copy-start | bytes 393220
  0.7 9.4 %copy-start.5 = (bf16[1,1024]{1,0:T(2,128)(2,1)S(1)}, bf16[1,1024]{1,0:T(2,128)(2,1)}, u32[]{:S(2)}) copy-start(bf16[1,1024]{1,0:T(2,128)(2,1)} %gain_ref.9) | copy-start | bytes 6148
  0.7 9.4 %copy-start.4 = (bf16[256,1024]{1,0:T(8,128)(2,1)S(1)}, bf16[256,1024]{1,0:T(8,128)(2,1)}, u32[]{:S(2)}) copy-start(bf16[256,1024]{1,0:T(8,128)(2,1)} %x1_ref) | copy-start | bytes 1572868
  5.4 14.5 %collective-permute-start = (bf16[128,1664]{1,0:T(8,128)(2,1)}, bf16[128,1664]{1,0:T(8,128)(2,1)S(1)}, u32[]{:S(2)}, u32[]{:S(2)}) collective-permute-start(bf16[128,1664]{1,0:T(8,128)(2,1)} %get-tuple-element.94), channel_id=1, source_target_pairs={{0,1},{1,0},{2,3},{3,2},{4,5},{5,4},{6,7},{7,6},{8,9},{9,8},{10,11... | collective-permute-start | bytes 1277960 | tf_op jit(solution)/shard_map/ppermute | solution.py:415
  7.6 26.5 %collective-permute-start.2 = (bf16[128,1664]{1,0:T(8,128)(2,1)}, bf16[128,1664]{1,0:T(8,128)(2,1)S(1)}, u32[]{:S(2)}, u32[]{:S(2)}) collective-permute-start(bf16[128,1664]{1,0:T(8,128)(2,1)} %get-tuple-element.89), channel_id=1, source_target_pairs={{0,1},{1,0},{2,3},{3,2},{4,5},{5,4},{6,7},{7,6},{8,9},{9,8},{10,11... | collective-permute-start | bytes 1277960 | tf_op jit(solution)/shard_map/ppermute | solution.py:415
  10.0 1.9 %copy-start = (bf16[1,1024,1536]{2,1,0:T(8,128)(2,1)S(1)}, bf16[1,1024,1536]{2,1,0:T(8,128)(2,1)}, u32[]{:S(2)}) copy-start(bf16[1,1024,1536]{2,1,0:T(8,128)(2,1)} %param.9) | copy-start | bytes 9437188
  11.9 1.6 %copy-start.2 = (bf16[1,1024,1024]{2,1,0:T(8,128)(2,1)S(1)}, bf16[1,1024,1024]{2,1,0:T(8,128)(2,1)}, u32[]{:S(2)}) copy-start(bf16[1,1024,1024]{2,1,0:T(8,128)(2,1)} %param.10) | copy-start | bytes 6291460
  13.5 6.4 %copy-start.3 = (bf16[1,1024,1024]{2,1,0:T(8,128)(2,1)S(1)}, bf16[1,1024,1024]{2,1,0:T(8,128)(2,1)}, u32[]{:S(2)}) copy-start(bf16[1,1024,1024]{2,1,0:T(8,128)(2,1)} %param.10) | copy-start | bytes 6291460
  19.9 11.1 %copy-start.1 = (bf16[1,1024,1536]{2,1,0:T(8,128)(2,1)S(1)}, bf16[1,1024,1536]{2,1,0:T(8,128)(2,1)}, u32[]{:S(2)}) copy-start(bf16[1,1024,1536]{2,1,0:T(8,128)(2,1)} %param.9) | copy-start | bytes 9437188
  21.3 9.7 %collective-permute-start.1 = (bf16[128,1024]{1,0:T(8,128)(2,1)S(1)}, bf16[128,1024]{1,0:T(8,128)(2,1)S(1)}, u32[]{:S(2)}, u32[]{:S(2)}) collective-permute-start(bf16[128,1024]{1,0:T(8,128)(2,1)S(1)} %get-tuple-element.102), channel_id=1, source_target_pairs={{0,254},{2,0},{4,2},{6,4},{8,6},{10,8},{12,10},{14,12},{16,14},{18... | collective-permute-start | bytes 786440 | tf_op jit(solution)/shard_map/ppermute | solution.py:420
  31.7 15.4 %collective-permute-start.4 = (bf16[128,1664]{1,0:T(8,128)(2,1)S(1)}, bf16[128,1664]{1,0:T(8,128)(2,1)S(1)}, u32[]{:S(2)}, u32[]{:S(2)}) collective-permute-start(bf16[128,1664]{1,0:T(8,128)(2,1)S(1)} %get-tuple-element.103), channel_id=1, source_target_pairs={{0,1},{1,0},{2,3},{3,2},{4,5},{5,4},{6,7},{7,6},{8,9},{9,8},{10,11... | collective-permute-start | bytes 1277960 | tf_op jit(solution)/shard_map/ppermute | solution.py:415
  35.9 10.5 %collective-permute-start.3 = (bf16[128,1024]{1,0:T(8,128)(2,1)S(1)}, bf16[128,1024]{1,0:T(8,128)(2,1)S(1)}, u32[]{:S(2)}, u32[]{:S(2)}) collective-permute-start(bf16[128,1024]{1,0:T(8,128)(2,1)S(1)} %get-tuple-element.109), channel_id=1, source_target_pairs={{0,254},{2,0},{4,2},{6,4},{8,6},{10,8},{12,10},{14,12},{16,14},{18... | collective-permute-start | bytes 786440 | tf_op jit(solution)/shard_map/ppermute | solution.py:420
  47.0 12.5 %collective-permute-start.5 = (bf16[128,1664]{1,0:T(8,128)(2,1)S(1)}, bf16[128,1664]{1,0:T(8,128)(2,1)S(1)}, u32[]{:S(2)}, u32[]{:S(2)}) collective-permute-start(bf16[128,1664]{1,0:T(8,128)(2,1)S(1)} %get-tuple-element.117), channel_id=1, source_target_pairs={{0,1},{1,0},{2,3},{3,2},{4,5},{5,4},{6,7},{7,6},{8,9},{9,8},{10,11... | collective-permute-start | bytes 1277960 | tf_op jit(solution)/shard_map/ppermute | solution.py:415
  48.9 17.1 %collective-permute-start.6 = (bf16[128,1024]{1,0:T(8,128)(2,1)S(1)}, bf16[128,1024]{1,0:T(8,128)(2,1)S(1)}, u32[]{:S(2)}, u32[]{:S(2)}) collective-permute-start(bf16[128,1024]{1,0:T(8,128)(2,1)S(1)} %get-tuple-element.123), channel_id=1, source_target_pairs={{0,1},{1,0},{2,3},{3,2},{4,5},{5,4},{6,7},{7,6},{8,9},{9,8},{10,11... | collective-permute-start | bytes 786440 | tf_op jit(solution)/shard_map/ppermute | solution.py:415
  61.6 6.6 %collective-permute-start.8 = (bf16[128,512]{1,0:T(8,128)(2,1)S(1)}, bf16[128,512]{1,0:T(8,128)(2,1)S(1)}, u32[]{:S(2)}, u32[]{:S(2)}) collective-permute-start(bf16[128,512]{1,0:T(8,128)(2,1)S(1)} %get-tuple-element.135), channel_id=1, source_target_pairs={{0,1},{1,0},{2,3},{3,2},{4,5},{5,4},{6,7},{7,6},{8,9},{9,8},{10,11... | collective-permute-start | bytes 393224 | tf_op jit(solution)/shard_map/ppermute | solution.py:415
  61.7 7.9 %collective-permute-start.7 = (bf16[128,512]{1,0:T(8,128)(2,1)S(1)}, bf16[128,512]{1,0:T(8,128)(2,1)S(1)}, u32[]{:S(2)}, u32[]{:S(2)}) collective-permute-start(bf16[128,512]{1,0:T(8,128)(2,1)S(1)} %get-tuple-element.127), channel_id=1, source_target_pairs={{0,1},{1,0},{2,3},{3,2},{4,5},{5,4},{6,7},{7,6},{8,9},{9,8},{10,11... | collective-permute-start | bytes 393224 | tf_op jit(solution)/shard_map/ppermute | solution.py:415
  71.0 10.2 %collective-permute-start.10 = (bf16[128,1024]{1,0:T(8,128)(2,1)S(1)}, bf16[128,1024]{1,0:T(8,128)(2,1)S(1)}, u32[]{:S(2)}, u32[]{:S(2)}) collective-permute-start(bf16[128,1024]{1,0:T(8,128)(2,1)S(1)} %get-tuple-element.154), channel_id=1, source_target_pairs={{0,2},{2,4},{4,6},{6,8},{8,10},{10,12},{12,14},{14,16},{16,18},{18... | collective-permute-start | bytes 786440 | tf_op jit(solution)/shard_map/ppermute | solution.py:420
  73.0 11.0 %collective-permute-start.9 = (bf16[128,1024]{1,0:T(8,128)(2,1)S(1)}, bf16[128,1024]{1,0:T(8,128)(2,1)S(1)}, u32[]{:S(2)}, u32[]{:S(2)}) collective-permute-start(bf16[128,1024]{1,0:T(8,128)(2,1)S(1)} %get-tuple-element.153), channel_id=1, source_target_pairs={{0,2},{2,4},{4,6},{6,8},{8,10},{10,12},{12,14},{14,16},{16,18},{18... | collective-permute-start | bytes 786440 | tf_op jit(solution)/shard_map/ppermute | solution.py:420
  81.7 8.1 %collective-permute-start.12 = (bf16[128,1024]{1,0:T(8,128)(2,1)S(1)}, bf16[128,1024]{1,0:T(8,128)(2,1)S(1)}, u32[]{:S(2)}, u32[]{:S(2)}) collective-permute-start(bf16[128,1024]{1,0:T(8,128)(2,1)S(1)} %get-tuple-element.156), channel_id=1, source_target_pairs={{0,1},{1,0},{2,3},{3,2},{4,5},{5,4},{6,7},{7,6},{8,9},{9,8},{10,11... | collective-permute-start | bytes 786440 | tf_op jit(solution)/shard_map/ppermute | solution.py:415
  84.5 7.1 %collective-permute-start.11 = (bf16[128,512]{1,0:T(8,128)(2,1)S(1)}, bf16[128,512]{1,0:T(8,128)(2,1)S(1)}, u32[]{:S(2)}, u32[]{:S(2)}) collective-permute-start(bf16[128,512]{1,0:T(8,128)(2,1)S(1)} %get-tuple-element.158), channel_id=1, source_target_pairs={{0,1},{1,0},{2,3},{3,2},{4,5},{5,4},{6,7},{7,6},{8,9},{9,8},{10,11... | collective-permute-start | bytes 393224 | tf_op jit(solution)/shard_map/ppermute | solution.py:415
  86.7 6.5 %collective-permute-start.13 = (bf16[128,512]{1,0:T(8,128)(2,1)S(1)}, bf16[128,512]{1,0:T(8,128)(2,1)S(1)}, u32[]{:S(2)}, u32[]{:S(2)}) collective-permute-start(bf16[128,512]{1,0:T(8,128)(2,1)S(1)} %get-tuple-element.170), channel_id=1, source_target_pairs={{0,1},{1,0},{2,3},{3,2},{4,5},{5,4},{6,7},{7,6},{8,9},{9,8},{10,11... | collective-permute-start | bytes 393224 | tf_op jit(solution)/shard_map/ppermute | solution.py:415
